TPU v7x, 32 devices: a whole 2x2x4 slice. The times are simulated.
32 devices in a mesh: dp: 8 (over y, x, core), mp: 4 (over z).
Axes of the slice: x: 2, y: 2, z: 4, core: 2. Of those that a mesh axis runs over, the one named last changes fastest.
Arguments:
- latents: bfloat16 [8, 2, 1280, 32], P('dp', None, 'mp'), may hold values from -6 to 6
- noise_target: float32 [8, 2, 1280, 32], P('dp', None, 'mp'), may hold values from -6 to 6
- token_mask: int32 [8, 2, 1280], P('dp', None, 'mp'), may hold values from 0 to 1, as said below
- timesteps: int32 [8, 2, 4], P('dp'), may hold values from 0 to 999
- labels: int32 [8, 2, 4], P('dp'), may hold values from 0 to 599
- state_embed: float32 [3, 32, 1024], P(None, None, 'dp'), as said below
- state_head: float32 [3, 1024, 32], P(None, 'dp'), as said below
- state_time_in: float32 [3, 256, 1024], P(None, None, 'dp'), as said below
- state_time_out: float32 [3, 1024, 1024], P(None, 'dp'), as said below
- state_classes: float32 [3, 600, 1024], P(None, None, 'dp'), as said below
- state_adaptive: float32 [3, 1024, 6, 1024], P(None, 'dp'), as said below
- state_attention_in: float32 [3, 1024, 3, 1024], P(None, 'dp', None, 'mp'), as said below
- state_attention_out: float32 [3, 1024, 1024], P(None, 'mp', 'dp'), as said below
- state_expand: float32 [3, 1024, 4096], P(None, 'dp', 'mp'), as said below
- state_contract: float32 [3, 4096, 1024], P(None, 'mp', 'dp'), as said below
Outputs:
- loss_value: float32 [], replicated
- grad_norm: float32 [], replicated
- new_embed: float32 [32, 1024], P(None, 'dp')
- embed_moments: float32 [2, 32, 1024], P(None, None, 'dp')
- new_head: float32 [1024, 32], P('dp')
- head_moments: float32 [2, 1024, 32], P(None, 'dp')
- new_time_in: float32 [256, 1024], P(None, 'dp')
- time_in_moments: float32 [2, 256, 1024], P(None, None, 'dp')
- new_time_out: float32 [1024, 1024], P('dp')
- time_out_moments: float32 [2, 1024, 1024], P(None, 'dp')
- new_classes: float32 [600, 1024], P(None, 'dp')
- classes_moments: float32 [2, 600, 1024], P(None, None, 'dp')
- new_adaptive: float32 [1024, 6, 1024], P('dp')
- adaptive_moments: float32 [2, 1024, 6, 1024], P(None, 'dp')
- new_attention_in: float32 [1024, 3, 1024], P('dp', None, 'mp')
- attention_in_moments: float32 [2, 1024, 3, 1024], P(None, 'dp', None, 'mp')
- new_attention_out: float32 [1024, 1024], P('mp', 'dp')
- attention_out_moments: float32 [2, 1024, 1024], P(None, 'mp', 'dp')
- new_expand: float32 [1024, 4096], P('dp', 'mp')
- expand_moments: float32 [2, 1024, 4096], P(None, 'dp', 'mp')
- new_contract: float32 [4096, 1024], P('mp', 'dp')
- contract_moments: float32 [2, 4096, 1024], P(None, 'mp', 'dp')
Inputs may be any that keep to these rules, and one draw needn't show every extreme that they name: `token_mask`: in every window a token is valid exactly where its column within the 8-wide patch rows lies below the window's valid width, which is 2 or more. `state_embed`: slice 0 holds the weight, slice 1 the first moment, slice 2 the positive root of the second moment. `state_head`: as for state_embed. `state_time_in`: as for state_embed. `state_time_out`: as for state_embed. `state_classes`: as for state_embed. `state_adaptive`: as for state_embed. `state_attention_in`: as for state_embed. `state_attention_out`: as for state_embed. `state_expand`: as for state_embed. `state_contract`: as for state_embed.
All inputs are finite; a program needn't handle non-finite values.
Results may differ from a plain program's by a relative error of at most 0.004.
The roundings to bfloat16 on the way count: a program that leaves them out, or rounds other values in their place, can miss the bound.
Values may be sent and summed in bfloat16 or wider, within the bound.
A program may use at most 320 MiB of HBM per device.

v0:
```python
import math

import jax
import jax.numpy as jnp
from jax import lax
from jax.sharding import PartitionSpec as P

D = 1024
HD = 64
PATCH = 32
FREQ = 256
CLASSES = 600
WTOK = 320
NMB = 2
WMB = 4


beta_one = 0.9
beta_two = 0.999
adam_eps = 1e-08
learn_rate = 0.15
weight_decay = 0.1
threshold = 0.002
step_count = 10.0
highest = lax.Precision.HIGHEST


def layer_norm(values):
    center = values - jnp.mean(values, axis=-1, keepdims=True)
    return center * lax.rsqrt(jnp.mean(center * center, axis=-1, keepdims=True) + 1e-06)


def modulate(values, shift, scale):
    return layer_norm(values) * (1.0 + scale) + shift


def gelu_exact(values):
    return jax.nn.gelu(values, approximate=False)


def timestep_features(step_ids):
    half_width = FREQ // 2
    frequency = jnp.exp(-math.log(10000.0) * jnp.arange(half_width, dtype=jnp.float32) / half_width)
    angles = step_ids.astype(jnp.float32)[:, None] * frequency[None, :]
    return jnp.concatenate([jnp.cos(angles), jnp.sin(angles)], axis=-1)


def window_positions(places):
    half_width = D // 2
    frequency = jnp.exp(-math.log(10000.0) * jnp.arange(half_width, dtype=jnp.float32) / half_width)
    angles = places.astype(jnp.float32)[:, None] * frequency[None, :]
    return jnp.concatenate([jnp.sin(angles), jnp.cos(angles)], axis=-1)


def dot_rows(former, latter, precision=None):
    return lax.dot_general(
        former,
        latter,
        (((0,), (0,)), ((), ())),
        precision=precision,
        preferred_element_type=jnp.float32,
    )


def dot_last(former, latter):
    return lax.dot_general(
        former, latter, (((1,), (1,)), ((), ())), preferred_element_type=jnp.float32
    )


def gather_rows(normed, key_flags):
    return (
        lax.all_gather(normed.astype(jnp.bfloat16), "mp", axis=0, tiled=True),
        lax.all_gather(key_flags, "mp", axis=0, tiled=True),
    )


def sum_rows(inner_act, last_matrix):
    return lax.psum_scatter(
        jnp.dot(inner_act, last_matrix, preferred_element_type=jnp.float32),
        "mp",
        scatter_dimension=0,
        tiled=True,
    )


def split_heads(qkv_rows):
    shaped = qkv_rows.reshape(WMB, WTOK, 3, -1, HD)
    return (shaped[:, :, 0], shaped[:, :, 1], shaped[:, :, 2])


def attention_scores(query_rows, key_rows, key_flags):
    scores = jnp.einsum(
        "wqhe,wkhe->whqk", query_rows, key_rows, preferred_element_type=jnp.float32
    ) * HD ** (-0.5)
    return jnp.where(key_flags.reshape(WMB, 1, 1, WTOK) > 0, scores, -1e30)


def attend(qkv_rows, key_flags):
    query_rows, key_rows, value_rows = split_heads(qkv_rows)
    scores = attention_scores(query_rows, key_rows, key_flags)
    row_peak = jnp.max(scores, axis=-1, keepdims=True)
    exponents = jnp.exp(scores - row_peak)
    row_totals = jnp.sum(exponents, axis=-1, keepdims=True)
    attn_weights = (exponents / row_totals).astype(jnp.bfloat16)
    mixed_heads = jnp.einsum(
        "whqk,wkhe->wqhe", attn_weights, value_rows, preferred_element_type=jnp.float32
    )
    return (
        mixed_heads.astype(jnp.bfloat16).reshape(WMB * WTOK, -1),
        row_peak + jnp.log(row_totals),
    )


def attend_back(grad_mixed, qkv_rows, key_flags, log_totals):
    query_rows, key_rows, value_rows = split_heads(qkv_rows)
    grad_heads = grad_mixed.astype(jnp.bfloat16).reshape(WMB, WTOK, -1, HD)
    scores = attention_scores(query_rows, key_rows, key_flags)
    attn_full = jnp.exp(scores - log_totals)
    attn_weights = attn_full.astype(jnp.bfloat16)
    grad_values = jnp.einsum(
        "whqk,wqhe->wkhe", attn_weights, grad_heads, preferred_element_type=jnp.float32
    )
    grad_attn = jnp.einsum(
        "wqhe,wkhe->whqk", grad_heads, value_rows, preferred_element_type=jnp.float32
    )
    grad_scores = attn_full * (grad_attn - jnp.sum(attn_full * grad_attn, axis=-1, keepdims=True))
    grad_scores = grad_scores.astype(jnp.bfloat16)
    grad_queries = jnp.einsum(
        "whqk,wkhe->wqhe", grad_scores, key_rows, preferred_element_type=jnp.float32
    ) * HD ** (-0.5)
    grad_keys = jnp.einsum(
        "whqk,wqhe->wkhe", grad_scores, query_rows, preferred_element_type=jnp.float32
    ) * HD ** (-0.5)
    stacked = jnp.stack([grad_queries, grad_keys, grad_values], axis=2)
    return stacked.astype(jnp.bfloat16).reshape(WMB * WTOK, -1)


def branch_back(grad_low, block_input, inner_act, first_matrix, last_matrix, inner_back):
    grad_whole = lax.all_gather(grad_low, "mp", axis=0, tiled=True)
    grad_last = dot_rows(inner_act, grad_whole)
    grad_pre = inner_back(dot_last(grad_whole, last_matrix))
    grad_first = dot_rows(block_input, grad_pre)
    grad_input = lax.psum_scatter(
        dot_last(grad_pre, first_matrix), "mp", scatter_dimension=0, tiled=True
    )
    return (grad_input, grad_first, grad_last)


def adam_update(state_in, gradient, factor):
    clipped = gradient * factor
    first_moment = beta_one * state_in[1] + (1.0 - beta_one) * clipped
    second_moment = beta_two * state_in[2] * state_in[2] + (1.0 - beta_two) * clipped * clipped
    root_moment = jnp.sqrt(second_moment)
    update = (
        first_moment
        / (1.0 - beta_one**step_count)
        / (root_moment / math.sqrt(1.0 - beta_two**step_count) + adam_eps)
    )
    new_weight = state_in[0] - learn_rate * (update + weight_decay * state_in[0])
    return (new_weight, jnp.stack([first_moment, root_moment]))


def add_trees(running, addend):
    if running is None:
        return addend
    return jax.tree.map(lambda summed, extra: summed + extra, running, addend)


def per_device(
    latents,
    noise_target,
    token_mask,
    timesteps,
    labels,
    state_embed,
    state_head,
    state_time_in,
    state_time_out,
    state_classes,
    state_adaptive,
    state_attention_in,
    state_attention_out,
    state_expand,
    state_contract,
):
    rows_local = latents.shape[2]
    mask_values = token_mask.astype(jnp.float32)
    token_total = lax.psum(jnp.sum(mask_values), ("dp", "mp"))
    embed_mat, head_mat, time_in_mat, time_out_mat, classes_mat, adaptive_mat = (
        lax.all_gather(state_embed[0].astype(jnp.bfloat16), "dp", axis=1, tiled=True),
        lax.all_gather(state_head[0].astype(jnp.bfloat16), "dp", axis=0, tiled=True),
        lax.all_gather(state_time_in[0].astype(jnp.bfloat16), "dp", axis=1, tiled=True),
        lax.all_gather(state_time_out[0].astype(jnp.bfloat16), "dp", axis=0, tiled=True),
        lax.all_gather(state_classes[0].astype(jnp.bfloat16), "dp", axis=1, tiled=True),
        lax.all_gather(state_adaptive[0].astype(jnp.bfloat16), "dp", axis=0, tiled=True),
    )
    adaptive_flat = adaptive_mat.reshape(D, 6 * D)
    features = timestep_features(timesteps.reshape(-1)).astype(jnp.bfloat16)
    time_pre = jnp.dot(features, time_in_mat, preferred_element_type=jnp.float32)
    time_hidden, silu_time_back = jax.vjp(jax.nn.silu, time_pre)
    time_hidden = time_hidden.astype(jnp.bfloat16)
    label_pick = (labels.reshape(-1)[:, None] == jnp.arange(CLASSES)[None, :]).astype(jnp.bfloat16)
    condition = jnp.dot(time_hidden, time_out_mat, preferred_element_type=jnp.float32) + jnp.dot(
        label_pick, classes_mat, preferred_element_type=jnp.float32
    )
    cond_act, silu_cond_back = jax.vjp(jax.nn.silu, condition)
    cond_act = cond_act.astype(jnp.bfloat16)
    adaptive = jnp.dot(cond_act, adaptive_flat, preferred_element_type=jnp.float32)
    row_ids = lax.axis_index("mp") * rows_local + jnp.arange(rows_local, dtype=jnp.int32)
    positions = window_positions(row_ids % WTOK)
    window_pick = ((row_ids // WTOK)[:, None] == jnp.arange(WMB)[None, :]).astype(jnp.float32)
    block_parts = (
        state_attention_in[0].astype(jnp.bfloat16),
        state_attention_out[0].astype(jnp.bfloat16),
        state_expand[0].astype(jnp.bfloat16),
        state_contract[0].astype(jnp.bfloat16),
    )
    loss_local = jnp.zeros((), jnp.float32)
    embed_grad = jnp.zeros((PATCH, D), jnp.float32)
    head_grad = jnp.zeros((D, PATCH), jnp.float32)
    adaptive_grads = []
    block_total = None
    for micro_step in range(NMB):
        gathered = (
            lax.all_gather(block_parts[0], "dp", axis=0, tiled=True),
            lax.all_gather(block_parts[1], "dp", axis=1, tiled=True),
            lax.all_gather(block_parts[2], "dp", axis=0, tiled=True),
            lax.all_gather(block_parts[3], "dp", axis=1, tiled=True),
        )
        attend_in_mat = gathered[0].reshape(D, -1)
        attend_out_mat, expand_mat, contract_mat = (gathered[1], gathered[2], gathered[3])
        latent_rows = latents[0, micro_step]
        mask_rows = mask_values[0, micro_step]
        window_mod = adaptive[micro_step * WMB : (micro_step + 1) * WMB]
        mod_rows = jnp.dot(window_pick, window_mod, precision=highest).reshape(rows_local, 6, D)
        residual = jnp.dot(latent_rows, embed_mat, preferred_element_type=jnp.float32) + positions
        normed_one, modulate_one_back = jax.vjp(modulate, residual, mod_rows[:, 0], mod_rows[:, 1])
        attend_input, key_flags = gather_rows(normed_one, mask_rows.astype(jnp.bfloat16))
        qkv_rows = jnp.dot(attend_input, attend_in_mat, preferred_element_type=jnp.float32).astype(
            jnp.bfloat16
        )
        mixed_heads, log_totals = attend(qkv_rows, key_flags)
        branch_one = sum_rows(mixed_heads, attend_out_mat)
        middle = residual + mod_rows[:, 2] * branch_one
        normed_two, modulate_two_back = jax.vjp(modulate, middle, mod_rows[:, 3], mod_rows[:, 4])
        expand_input, unused_flags = gather_rows(normed_two, mask_rows.astype(jnp.bfloat16))
        up_pre = jnp.dot(expand_input, expand_mat, preferred_element_type=jnp.float32)
        hidden_full, gelu_back = jax.vjp(gelu_exact, up_pre)
        hidden_act = hidden_full.astype(jnp.bfloat16)
        branch_two = sum_rows(hidden_act, contract_mat)
        final = middle + mod_rows[:, 5] * branch_two
        final_norm, final_back = jax.vjp(layer_norm, final)
        final_low = final_norm.astype(jnp.bfloat16)
        prediction = jnp.dot(final_low, head_mat, preferred_element_type=jnp.float32)
        pred_error = prediction - noise_target[0, micro_step]
        loss_local = (
            loss_local
            + jnp.sum(jnp.mean(pred_error * pred_error, axis=-1) * mask_rows) / token_total
        )
        grad_pred = (2.0 / PATCH * pred_error * mask_rows[:, None] / token_total).astype(
            jnp.bfloat16
        )
        head_grad = head_grad + dot_rows(final_low, grad_pred)
        grad_final = final_back(dot_last(grad_pred, head_mat))[0]
        grad_gate_two = grad_final * branch_two
        grad_branch_two = (grad_final * mod_rows[:, 5]).astype(jnp.bfloat16)

        def expand_back(grad_hidden):
            return gelu_back(grad_hidden)[0].astype(jnp.bfloat16)

        grad_normed_two, grad_expand, grad_contract = branch_back(
            grad_branch_two, expand_input, hidden_act, expand_mat, contract_mat, expand_back
        )
        grad_mid_part, grad_shift_two, grad_scale_two = modulate_two_back(grad_normed_two)
        grad_middle = grad_final + grad_mid_part
        grad_gate_one = grad_middle * branch_one
        grad_branch_one = (grad_middle * mod_rows[:, 2]).astype(jnp.bfloat16)

        def attention_back(grad_mixed):
            return attend_back(grad_mixed, qkv_rows, key_flags, log_totals)

        grad_normed_one, grad_attend_in, grad_attend_out = branch_back(
            grad_branch_one,
            attend_input,
            mixed_heads,
            attend_in_mat,
            attend_out_mat,
            attention_back,
        )
        grad_res_part, grad_shift_one, grad_scale_one = modulate_one_back(grad_normed_one)
        grad_embedded = (grad_middle + grad_res_part).astype(jnp.bfloat16)
        embed_grad = embed_grad + dot_rows(latent_rows, grad_embedded)
        grad_mod_rows = jnp.stack(
            [
                grad_shift_one,
                grad_scale_one,
                grad_gate_one,
                grad_shift_two,
                grad_scale_two,
                grad_gate_two,
            ],
            axis=1,
        ).reshape(rows_local, 6 * D)
        adaptive_grads.append(dot_rows(window_pick, grad_mod_rows, precision=highest))
        block_terms = (
            grad_attend_in.reshape(D, 3, -1),
            grad_attend_out,
            grad_expand,
            grad_contract,
        )
        reduced = (
            lax.psum_scatter(block_terms[0], "dp", scatter_dimension=0, tiled=True),
            lax.psum_scatter(block_terms[1], "dp", scatter_dimension=1, tiled=True),
            lax.psum_scatter(block_terms[2], "dp", scatter_dimension=0, tiled=True),
            lax.psum_scatter(block_terms[3], "dp", scatter_dimension=1, tiled=True),
        )
        block_total = add_trees(block_total, reduced)
    adaptive_sum, embed_sum, head_sum = lax.psum(
        (jnp.concatenate(adaptive_grads, axis=0), embed_grad, head_grad), "mp"
    )
    grad_adaptive = adaptive_sum.astype(jnp.bfloat16)
    grad_condition = silu_cond_back(dot_last(grad_adaptive, adaptive_flat))[0].astype(jnp.bfloat16)
    grad_time_pre = silu_time_back(dot_last(grad_condition, time_out_mat))[0].astype(jnp.bfloat16)
    adaptive_grad = dot_rows(cond_act, grad_adaptive).reshape(D, 6, D)
    time_out_grad = dot_rows(time_hidden, grad_condition)
    classes_grad = dot_rows(label_pick, grad_condition)
    time_in_grad = dot_rows(features, grad_time_pre)
    small_grads = (
        lax.psum_scatter(embed_sum, "dp", scatter_dimension=1, tiled=True),
        lax.psum_scatter(head_sum, "dp", scatter_dimension=0, tiled=True),
        lax.psum_scatter(time_in_grad, "dp", scatter_dimension=1, tiled=True),
        lax.psum_scatter(time_out_grad, "dp", scatter_dimension=0, tiled=True),
        lax.psum_scatter(classes_grad, "dp", scatter_dimension=1, tiled=True),
        lax.psum_scatter(adaptive_grad, "dp", scatter_dimension=0, tiled=True),
    )
    square_block = jnp.zeros((), jnp.float32)
    for gradient in block_total:
        square_block = square_block + jnp.sum(gradient * gradient)
    square_small = jnp.zeros((), jnp.float32)
    for gradient in small_grads:
        square_small = square_small + jnp.sum(gradient * gradient)
    square_local = square_block + square_small / lax.axis_size("mp")
    loss_value, square_total = lax.psum((loss_local, square_local), ("dp", "mp"))
    grad_norm = jnp.sqrt(square_total)
    factor = jnp.minimum(1.0, threshold / grad_norm)
    all_states = (
        state_embed,
        state_head,
        state_time_in,
        state_time_out,
        state_classes,
        state_adaptive,
        state_attention_in,
        state_attention_out,
        state_expand,
        state_contract,
    )
    all_grads = tuple(small_grads) + tuple(block_total)
    results = [loss_value, grad_norm]
    for state_in, gradient in zip(all_states, all_grads):
        new_weight, moments = adam_update(state_in, gradient, factor)
        results.append(new_weight)
        results.append(moments)
    return tuple(results)


def solution(mesh):
    in_specs = (
        P("dp", None, "mp", None),
        P("dp", None, "mp", None),
        P("dp", None, "mp"),
        P("dp", None, None),
        P("dp", None, None),
        P(None, None, "dp"),
        P(None, "dp", None),
        P(None, None, "dp"),
        P(None, "dp", None),
        P(None, None, "dp"),
        P(None, "dp", None, None),
        P(None, "dp", None, "mp"),
        P(None, "mp", "dp"),
        P(None, "dp", "mp"),
        P(None, "mp", "dp"),
    )
    out_specs = (
        P(),
        P(),
        P(None, "dp"),
        P(None, None, "dp"),
        P("dp", None),
        P(None, "dp", None),
        P(None, "dp"),
        P(None, None, "dp"),
        P("dp", None),
        P(None, "dp", None),
        P(None, "dp"),
        P(None, None, "dp"),
        P("dp", None, None),
        P(None, "dp", None, None),
        P("dp", None, "mp"),
        P(None, "dp", None, "mp"),
        P("mp", "dp"),
        P(None, "mp", "dp"),
        P("dp", "mp"),
        P(None, "dp", "mp"),
        P("mp", "dp"),
        P(None, "mp", "dp"),
    )
    return jax.shard_map(
        per_device, mesh=mesh, in_specs=in_specs, out_specs=out_specs, check_vma=False
    )
```

profile of v0, /device:TPU:0, one launch (start us, length us, event | category | flops | bytes accessed | tf_op | source)
XLA Modules:
  0.0 2129.3 jit_solution(5930244494552501858)
XLA Ops:
  10.8 8.0 fusion.222
  26.2 10.4 all_gather.64
  37.5 10.2 all_gather.65
  53.6 14.6 all-gather.17.cloned.1.call-done
  69.8 75.4 %all-gather.19.cloned.1.call-done = bf16[1024,6,1024]{0,2,1:T(8,128)(2,1)} async-done(((bf16[128,6,1024]{0,2,1:T(8,128)(2,1)}), bf16[1024,6,1024]{0,2,1:T(8,128)(2,1)}) %all-gather.19.cloned.1.call-update) | async-done | bytes 12582928 | tf_op jit(solution)/shard_map/all_gather | solution.py:196
  145.2 7.9 fusion.202
  153.1 4.7 fusion.103
  172.0 11.8 all-reduce.4
  185.9 4.7 fusion.102
  204.1 11.3 all_gather.72
  218.0 12.2 all-gather.21.cloned.1.call-done
  230.2 5.8 convolution_convert_fusion.1
  235.9 6.7 reshape.390
  273.4 12.4 all-gather.31.cloned.1.call-done
  285.8 5.8 convolution_convert_fusion
  291.5 6.7 reshape.391
  338.9 41.7 %reduce-scatter.19.cloned.1.call-done = f32[320,1024]{1,0:T(8,128)} async-done(((f32[1280,1024]{1,0:T(8,128)}), f32[320,1024]{1,0:T(8,128)}) %reduce-scatter.19.cloned.1.call-update) | async-done | bytes 1310736 | tf_op jit(solution)/shard_map/reduce_scatter | solution.py:79
  396.4 81.4 %reduce-scatter.23.cloned.1.call-done = f32[320,1024]{1,0:T(8,128)} async-done(((f32[1280,1024]{1,0:T(8,128)}), f32[320,1024]{1,0:T(8,128)}) %reduce-scatter.23.cloned.1.call-update) | async-done | bytes 1310736 | tf_op jit(solution)/shard_map/reduce_scatter | solution.py:79
  482.3 26.4 %all-gather.27.cloned.1.call-done = bf16[1024,1024]{1,0:T(8,128)(2,1)} async-done(((bf16[128,1024]{1,0:T(8,128)(2,1)}), bf16[1024,1024]{1,0:T(8,128)(2,1)}) %all-gather.27.cloned.1.call-update) | async-done | bytes 2097168 | tf_op jit(solution)/shard_map/all_gather | solution.py:228
  508.7 56.3 %all-gather.25.cloned.1.call-done = bf16[1280,1024]{1,0:T(8,128)(2,1)} async-done(((bf16[320,1024]{1,0:T(8,128)(2,1)}), bf16[1280,1024]{1,0:T(8,128)(2,1)}) %all-gather.25.cloned.1.call-update) | async-done | bytes 2621456 | tf_op jit(solution)/shard_map/all_gather | solution.py:73
  565.0 17.1 multiply_convert_fusion.3
  582.1 12.3 all-gather.29.cloned.1.call-done
  594.4 6.2 fusion.232
  600.7 50.6 %all-gather.33.cloned.1.call-done = bf16[1280,1024]{1,0:T(8,128)(2,1)} async-done(((bf16[320,1024]{1,0:T(8,128)(2,1)}), bf16[1280,1024]{1,0:T(8,128)(2,1)}) %all-gather.33.cloned.1.call-update) | async-done | bytes 2621456 | tf_op jit(solution)/shard_map/all_gather | solution.py:73
  651.3 16.7 multiply_convert_fusion.2
  675.3 44.7 %psum.42 = f32[]{:T(128)} all-reduce(f32[]{:T(128)} %convert_reduce_fusion), channel_id=1, replica_groups=mesh['dp'=8,'mp'=4] {'dp','mp'}, use_global_device_ids=true, to_apply=%region_13.14 | all-reduce | flops 1 | bytes 8 | tf_op jit(solution)/shard_map/psum | solution.py:189
  720.7 9.9 all_gather.76
  734.0 13.2 reduce-scatter.21.cloned.1.call-done
  750.0 93.5 %reduce-scatter.25.cloned.1.call-done = f32[320,1024]{1,0:T(8,128)} async-done(((f32[1280,1024]{1,0:T(8,128)}), f32[320,1024]{1,0:T(8,128)}) %reduce-scatter.25.cloned.1.call-update) | async-done | bytes 1310736 | tf_op jit(solution)/shard_map/reduce_scatter | solution.py:79
  857.0 50.0 %all-gather.39.cloned.1.call-done = bf16[1280,1024]{1,0:T(8,128)(2,1)} async-done(((bf16[320,1024]{1,0:T(8,128)(2,1)}), bf16[1280,1024]{1,0:T(8,128)(2,1)}) %all-gather.39.cloned.1.call-update) | async-done | bytes 2621456 | tf_op jit(solution)/shard_map/all_gather | solution.py:140
  907.0 9.9 add_convert_fusion
  923.1 38.9 %all-gather.35.cloned.1.call-done = bf16[1280,1024]{1,0:T(8,128)(2,1)} async-done(((bf16[320,1024]{1,0:T(8,128)(2,1)}), bf16[1280,1024]{1,0:T(8,128)(2,1)}) %all-gather.35.cloned.1.call-update) | async-done | bytes 2621456 | tf_op jit(solution)/shard_map/all_gather | solution.py:140
  962.0 9.9 add_convert_fusion.1
  973.4 4.7 fusion.235
  978.2 79.1 %reduce-scatter.29.cloned.1.call-done = f32[320,1024]{1,0:T(8,128)} async-done(((f32[1280,1024]{1,0:T(8,128)}), f32[320,1024]{1,0:T(8,128)}) %reduce-scatter.29.cloned.1.call-update) | async-done | bytes 1310736 | tf_op jit(solution)/shard_map/reduce_scatter | solution.py:144
  1063.5 90.2 %reduce-scatter.27.cloned.1.call-done = f32[320,1024]{1,0:T(8,128)} async-done(((f32[1280,1024]{1,0:T(8,128)}), f32[320,1024]{1,0:T(8,128)}) %reduce-scatter.27.cloned.1.call-update) | async-done | bytes 1310736 | tf_op jit(solution)/shard_map/reduce_scatter | solution.py:144
  1158.9 52.3 %all-gather.41.cloned.1.call-done = bf16[1280,1024]{1,0:T(8,128)(2,1)} async-done(((bf16[320,1024]{1,0:T(8,128)(2,1)}), bf16[1280,1024]{1,0:T(8,128)(2,1)}) %all-gather.41.cloned.1.call-update) | async-done | bytes 2621456 | tf_op jit(solution)/shard_map/all_gather | solution.py:140
  1219.3 6.9 multiply_reduce_fusion
  1239.0 6.6 fusion.241
  1246.3 20.5 all-gather.37.cloned.1.call-done
  1274.9 6.6 multiply_reduce_fusion.1
  1294.4 6.6 fusion.240
  1303.7 7.6 fusion.239
  1311.3 50.4 %reduce-scatter.33.cloned.1.call-done = f32[320,1024]{1,0:T(8,128)} async-done(((f32[1280,1024]{1,0:T(8,128)}), f32[320,1024]{1,0:T(8,128)}) %reduce-scatter.33.cloned.1.call-update) | async-done | bytes 1310736 | tf_op jit(solution)/shard_map/reduce_scatter | solution.py:144
  1365.4 93.5 %reduce-scatter.31.cloned.1.call-done = f32[320,1024]{1,0:T(8,128)} async-done(((f32[1280,1024]{1,0:T(8,128)}), f32[320,1024]{1,0:T(8,128)}) %reduce-scatter.31.cloned.1.call-update) | async-done | bytes 1310736 | tf_op jit(solution)/shard_map/reduce_scatter | solution.py:144
  1464.8 8.7 convolution_add_fusion
  1473.9 5.7 fusion.238
  1489.1 4.8 fusion.30
  1509.4 9.2 copy.98
  1528.3 9.1 copy.99
  1537.4 8.3 fusion.114
  1550.3 23.5 %all-reduce.6 = (f32[32,128]{1,0:T(8,128)S(1)}, f32[128,32]{0,1:T(8,128)S(1)}, bf16[8,6144]{1,0:T(8,128)(2,1)S(1)}) all-reduce(f32[32,128]{1,0:T(8,128)} %reduce-scatter.51.cloned.1.call-done, f32[128,32]{0,1:T(8,128)} %reduce-scatter.53.cloned.1.call-done, f32[8,6144]{1,0:T(8,128)S(1)} %pad_maximum_fusion.9), channel_id=1, replica_groups=mesh['dp'=8,'mp'=4] {'mp'}, use_global_device_ids=true, to_apply=%region_57.58 | all-reduce | flops 57344 | bytes 360448 | tf_op jit(solution)/shard_map/psum | solution.py:319
  1573.8 6.5 fusion.133
  1587.3 10.3 fusion.127
  1606.5 37.2 %reduce-scatter.47.cloned.1.call-done = f32[128,1024]{1,0:T(8,128)} async-done(((f32[1024,1024]{1,0:T(8,128)}), f32[128,1024]{1,0:T(8,128)}) %reduce-scatter.47.cloned.1.call-update) | async-done | bytes 524304 | tf_op jit(solution)/shard_map/reduce_scatter | solution.py:315
  1645.5 37.9 %reduce-scatter.45.cloned.1.call-done = f32[256,128]{1,0:T(8,128)} async-done(((f32[256,1024]{1,0:T(8,128)}), f32[256,128]{1,0:T(8,128)}) %reduce-scatter.45.cloned.1.call-update) | async-done | bytes 131088 | tf_op jit(solution)/shard_map/reduce_scatter | solution.py:314
  1684.9 48.0 %reduce-scatter.43.cloned.1.call-done = f32[128,3,256]{2,0,1:T(8,128)} async-done(((f32[1024,3,256]{2,0,1:T(8,128)}), f32[128,3,256]{2,0,1:T(8,128)}) %reduce-scatter.43.cloned.1.call-update) | async-done | bytes 393232 | tf_op jit(solution)/shard_map/reduce_scatter | solution.py:313
  1739.7 33.3 %reduce-scatter.35.cloned.1.call-done = f32[256,128]{1,0:T(8,128)} async-done(((f32[256,1024]{1,0:T(8,128)}), f32[256,128]{1,0:T(8,128)}) %reduce-scatter.35.cloned.1.call-update) | async-done | bytes 131088 | tf_op jit(solution)/shard_map/reduce_scatter | solution.py:332
  1775.3 44.3 %reduce-scatter.39.cloned.1.call-done = f32[600,128]{1,0:T(8,128)} async-done(((f32[600,1024]{1,0:T(8,128)}), f32[600,128]{1,0:T(8,128)}) %reduce-scatter.39.cloned.1.call-update) | async-done | bytes 307216 | tf_op jit(solution)/shard_map/reduce_scatter | solution.py:334
  1821.3 53.4 %reduce-scatter.37.cloned.1.call-done = f32[128,1024]{1,0:T(8,128)} async-done(((f32[1024,1024]{1,0:T(8,128)}), f32[128,1024]{1,0:T(8,128)}) %reduce-scatter.37.cloned.1.call-update) | async-done | bytes 524304 | tf_op jit(solution)/shard_map/reduce_scatter | solution.py:333
  1877.8 157.4 %reduce-scatter.41.cloned.1.call-done = f32[128,6,1024]{0,2,1:T(8,128)} async-done(((f32[1024,6,1024]{0,2,1:T(8,128)}), f32[128,6,1024]{0,2,1:T(8,128)}) %reduce-scatter.41.cloned.1.call-update) | async-done | bytes 3145744 | tf_op jit(solution)/shard_map/reduce_scatter | solution.py:335
  2042.9 39.6 %all-reduce.2 = (f32[]{:T(128)}, f32[]{:T(128)}) all-reduce(f32[]{:T(128)S(6)} %add.455, f32[]{:T(128)S(6)} %add.477), channel_id=1, replica_groups=mesh['dp'=8,'mp'=4] {'dp','mp'}, use_global_device_ids=true, to_apply=%region_26.27 | all-reduce | flops 2 | bytes 16 | tf_op jit(solution)/shard_map/psum | solution.py:344
  2084.5 6.2 fusion.60
  2093.7 6.7 copy.104
  (609 shorter events, 339.2 us)
Async XLA Ops:
  7.2 44.4 %all-gather.15.cloned.1.call-start = ((), (), s32[]{:S(2)}) async-start(), calls=%async_computation.18 | async-start | bytes 2359296 | tf_op jit(solution)/shard_map/all_gather | solution.py:194
  9.0 59.1 %all-gather.17.cloned.1.call-start = ((), (), s32[]{:S(2)}) async-start(), calls=%async_computation.19 | async-start | bytes 1382400 | tf_op jit(solution)/shard_map/all_gather | solution.py:195
  10.8 134.4 %all-gather.19.cloned.1.call-start = ((), (), s32[]{:S(2)}) async-start(), calls=%async_computation.20 | async-start | bytes 14155776 | tf_op jit(solution)/shard_map/all_gather | solution.py:196
  23.4 192.0 %all-gather.23.cloned.1.call-start = ((), (), s32[]{:S(2)}) async-start(), calls=%async_computation.22 | async-start | bytes 1769472 | tf_op jit(solution)/shard_map/all_gather | solution.py:226
  25.1 205.0 %all-gather.21.cloned.1.call-start = ((), (), s32[]{:S(2)}) async-start(), calls=%async_computation.21 | async-start | bytes 3276800 | tf_op jit(solution)/shard_map/all_gather | solution.py:73
  25.2 160.6 %copy-start.96 = (s32[320]{0:T(512)}, s32[320]{0:T(512)S(1)}, u32[]{:S(2)}) copy-start(s32[320]{0:T(512)S(1)} %add_select_fusion) | copy-start | bytes 3844
  25.4 42.8 %copy-start.143 = (s32[8]{0:T(128)}, s32[8]{0:T(128)S(1)}, u32[]{:S(2)}) copy-start(s32[8]{0:T(128)S(1)} %eq.33) | copy-start | bytes 100
  50.6 330.1 %copy-start.2 = (f32[320,1024]{1,0:T(8,128)}, f32[320,1024]{1,0:T(8,128)S(1)}, u32[]{:S(2)}) copy-start(f32[320,1024]{1,0:T(8,128)S(1)} %get-tuple-element.141) | copy-start | bytes 3932164
  50.6 116.3 %copy-start.109 = (f32[320]{0:T(512)}, f32[320]{0:T(512)S(1)}, u32[]{:S(2)}) copy-start(f32[320]{0:T(512)S(1)} %broadcast_multiply_fusion.7) | copy-start | bytes 3844
  51.2 101.9 %copy-start.94 = (f32[8,1024]{1,0:T(8,128)}, f32[8,1024]{1,0:T(8,128)S(1)}, u32[]{:S(2)}) copy-start(f32[8,1024]{1,0:T(8,128)S(1)} %fusion.174) | copy-start | bytes 98308
  51.6 115.3 %copy-start.121 = (f32[320]{0:T(512)}, f32[320]{0:T(512)S(1)}, u32[]{:S(2)}) copy-start(f32[320]{0:T(512)S(1)} %fusion.181) | copy-start | bytes 3844
  69.8 83.3 %copy-start.91 = (f32[8,1024]{1,0:T(8,128)}, f32[8,1024]{1,0:T(8,128)S(1)}, u32[]{:S(2)}) copy-start(f32[8,1024]{1,0:T(8,128)S(1)} %convolution_add_fusion.7) | copy-start | bytes 98308
  169.4 116.3 %all-gather.31.cloned.1.call-start = ((), (), s32[]{:S(2)}) async-start(), calls=%async_computation.28 | async-start | bytes 3276800 | tf_op jit(solution)/shard_map/all_gather | solution.py:73
  183.9 77.1 %copy-start.117 = (pred[4,320]{1,0:T(4,128)(4,1)}, pred[4,320]{1,0:T(4,128)(4,1)S(1)}, u32[]{:S(2)}) copy-start(pred[4,320]{1,0:T(4,128)(4,1)S(1)} %gt.25) | copy-start | bytes 3844
  185.5 292.3 %copy-start.4 = (f32[320,1024]{1,0:T(8,128)}, f32[320,1024]{1,0:T(8,128)S(1)}, u32[]{:S(2)}) copy-start(f32[320,1024]{1,0:T(8,128)S(1)} %get-tuple-element.148) | copy-start | bytes 3932164
  203.1 177.5 %reduce-scatter.19.cloned.1.call-start = ((), (), s32[]{:S(2)}) async-start(), calls=%async_computation.23 | async-start | bytes 6553600 | tf_op jit(solution)/shard_map/reduce_scatter | solution.py:79
  273.1 204.7 %reduce-scatter.23.cloned.1.call-start = ((), (), s32[]{:S(2)}) async-start(), calls=%async_computation.29 | async-start | bytes 6553600 | tf_op jit(solution)/shard_map/reduce_scatter | solution.py:79
  273.4 43.1 %copy-start.119 = (pred[4,320]{1,0:T(4,128)(4,1)}, pred[4,320]{1,0:T(4,128)(4,1)S(1)}, u32[]{:S(2)}) copy-start(pred[4,320]{1,0:T(4,128)(4,1)S(1)} %gt.27) | copy-start | bytes 3844
  328.1 180.6 %all-gather.27.cloned.1.call-start = ((), (), s32[]{:S(2)}) async-start(), calls=%async_computation.25 | async-start | bytes 2359296 | tf_op jit(solution)/shard_map/all_gather | solution.py:228
  330.0 235.0 %all-gather.25.cloned.1.call-start = ((), (), s32[]{:S(2)}) async-start(), calls=%async_computation.24 | async-start | bytes 3276800 | tf_op jit(solution)/shard_map/all_gather | solution.py:73
  385.7 208.7 %all-gather.29.cloned.1.call-start = ((), (), s32[]{:S(2)}) async-start(), calls=%async_computation.26 | async-start | bytes 2359296 | tf_op jit(solution)/shard_map/all_gather | solution.py:229
  387.5 263.7 %all-gather.33.cloned.1.call-start = ((), (), s32[]{:S(2)}) async-start(), calls=%async_computation.30 | async-start | bytes 3276800 | tf_op jit(solution)/shard_map/all_gather | solution.py:73
  389.8 90.4 %copy-start.33 = (f32[320,1,1024]{2,0,1:T(8,128)}, f32[320,1,1024]{2,0,1:T(8,128)S(1)}, u32[]{:S(2)}) copy-start(f32[320,1,1024]{2,0,1:T(8,128)S(1)} %copy.141) | copy-start | bytes 3932164
  482.2 265.0 %reduce-scatter.21.cloned.1.call-start = ((), (), s32[]{:S(2)}) async-start(), calls=%async_computation.27 | async-start | bytes 6553600 | tf_op jit(solution)/shard_map/reduce_scatter | solution.py:79
  600.6 50.7 %copy-start.148 = (bf16[1024,1024]{1,0:T(8,128)(2,1)S(1)}, bf16[1024,1024]{1,0:T(8,128)(2,1)}, u32[]{:S(2)}) copy-start(bf16[1024,1024]{1,0:T(8,128)(2,1)} %all-gather.27.cloned.1.call-done) | copy-start | bytes 6291460
  600.6 242.9 %reduce-scatter.25.cloned.1.call-start = ((), (), s32[]{:S(2)}) async-start(), calls=%async_computation.31 | async-start | bytes 6553600 | tf_op jit(solution)/shard_map/reduce_scatter | solution.py:79
  674.0 56.6 %copy-start.59 = (f32[320,1,1024]{0,2,1:T(8,128)S(1)}, f32[320,1,1024]{0,2,1:T(8,128)}, u32[]{:S(2)}) copy-start(f32[320,1,1024]{0,2,1:T(8,128)} %get-tuple-element.84) | copy-start | bytes 3932164
  674.0 233.0 %all-gather.39.cloned.1.call-start = ((), (), s32[]{:S(2)}) async-start(), calls=%async_computation.35 | async-start | bytes 3276800 | tf_op jit(solution)/shard_map/all_gather | solution.py:140
  748.8 94.8 %copy-start.10 = (f32[320,1024]{1,0:T(8,128)S(1)}, f32[320,1024]{1,0:T(8,128)}, u32[]{:S(2)}) copy-start(f32[320,1024]{1,0:T(8,128)} %copy-done.9) | copy-start | bytes 3932164
  851.5 110.5 %all-gather.35.cloned.1.call-start = ((), (), s32[]{:S(2)}) async-start(), calls=%async_computation.32 | async-start | bytes 3276800 | tf_op jit(solution)/shard_map/all_gather | solution.py:140
  856.7 200.6 %reduce-scatter.29.cloned.1.call-start = ((), (), s32[]{:S(2)}) async-start(), calls=%async_computation.36 | async-start | bytes 6553600 | tf_op jit(solution)/shard_map/reduce_scatter | solution.py:144
  923.0 230.7 %reduce-scatter.27.cloned.1.call-start = ((), (), s32[]{:S(2)}) async-start(), calls=%async_computation.33 | async-start | bytes 6553600 | tf_op jit(solution)/shard_map/reduce_scatter | solution.py:144
  978.1 233.1 %all-gather.41.cloned.1.call-start = ((), (), s32[]{:S(2)}) async-start(), calls=%async_computation.37 | async-start | bytes 3276800 | tf_op jit(solution)/shard_map/all_gather | solution.py:140
  1061.5 92.2 %copy-start.32 = (f32[320,1,1024]{2,0,1:T(8,128)S(1)}, f32[320,1,1024]{2,0,1:T(8,128)}, u32[]{:S(2)}) copy-start(f32[320,1,1024]{2,0,1:T(8,128)} %copy.132) | copy-start | bytes 3932164
  1061.5 92.2 %copy-start.114 = (f32[320]{0:T(512)S(1)}, f32[320]{0:T(512)}, u32[]{:S(2)}) copy-start(f32[320]{0:T(512)} %copy-done.113) | copy-start | bytes 3844
  1063.0 92.5 %copy-start.136 = (f32[320]{0:T(512)S(1)}, f32[320]{0:T(512)}, u32[]{:S(2)}) copy-start(f32[320]{0:T(512)} %copy-done.135) | copy-start | bytes 3844
  1063.0 92.5 %copy-start.126 = (f32[320]{0:T(512)S(1)}, f32[320]{0:T(512)}, u32[]{:S(2)}) copy-start(f32[320]{0:T(512)} %copy-done.125) | copy-start | bytes 3844
  1063.1 203.7 %all-gather.37.cloned.1.call-start = ((), (), s32[]{:S(2)}) async-start(), calls=%async_computation.34 | async-start | bytes 3276800 | tf_op jit(solution)/shard_map/all_gather | solution.py:140
  1157.3 54.0 %copy-start.71 = (bf16[256,1024]{1,0:T(8,128)(2,1)S(1)}, bf16[256,1024]{1,0:T(8,128)(2,1)}, u32[]{:S(2)}) copy-start(bf16[256,1024]{1,0:T(8,128)(2,1)} %all_gather.72) | copy-start | bytes 1572868
  1158.9 202.8 %reduce-scatter.33.cloned.1.call-start = ((), (), s32[]{:S(2)}) async-start(), calls=%async_computation.39 | async-start | bytes 6553600 | tf_op jit(solution)/shard_map/reduce_scatter | solution.py:144
  1245.6 213.3 %reduce-scatter.31.cloned.1.call-start = ((), (), s32[]{:S(2)}) async-start(), calls=%async_computation.38 | async-start | bytes 6553600 | tf_op jit(solution)/shard_map/reduce_scatter | solution.py:144
  1301.0 249.3 %reduce-scatter.53.cloned.1.call-start = ((), (), s32[]{:S(2)}) async-start(), calls=%async_computation.49 | async-start | bytes 147456 | tf_op jit(solution)/shard_map/reduce_scatter | solution.py:331
  1303.6 58.1 %copy-start.5 = (f32[320,1024]{1,0:T(8,128)S(1)}, f32[320,1024]{1,0:T(8,128)}, u32[]{:S(2)}) copy-start(f32[320,1024]{1,0:T(8,128)} %copy-done.4) | copy-start | bytes 3932164
  1303.6 58.1 %copy-start.19 = (f32[320,1,1024]{2,0,1:T(8,128)S(1)}, f32[320,1,1024]{2,0,1:T(8,128)}, u32[]{:S(2)}) copy-start(f32[320,1,1024]{2,0,1:T(8,128)} %copy.135) | copy-start | bytes 3932164
  1303.6 58.1 %copy-start.112 = (f32[320]{0:T(512)S(1)}, f32[320]{0:T(512)}, u32[]{:S(2)}) copy-start(f32[320]{0:T(512)} %copy-done.111) | copy-start | bytes 3844
  1303.6 246.7 %reduce-scatter.51.cloned.1.call-start = ((), (), s32[]{:S(2)}) async-start(), calls=%async_computation.48 | async-start | bytes 147456 | tf_op jit(solution)/shard_map/reduce_scatter | solution.py:330
  1311.3 52.3 %copy-start.134 = (f32[320]{0:T(512)S(1)}, f32[320]{0:T(512)}, u32[]{:S(2)}) copy-start(f32[320]{0:T(512)} %copy-done.133) | copy-start | bytes 3844
  1311.3 52.3 %copy-start.124 = (f32[320]{0:T(512)S(1)}, f32[320]{0:T(512)}, u32[]{:S(2)}) copy-start(f32[320]{0:T(512)} %copy-done.123) | copy-start | bytes 3844
  1363.8 95.1 %copy-start.3 = (f32[320,1024]{1,0:T(8,128)S(1)}, f32[320,1024]{1,0:T(8,128)}, u32[]{:S(2)}) copy-start(f32[320,1024]{1,0:T(8,128)} %copy-done.2) | copy-start | bytes 3932164
  1363.8 95.1 %copy-start.110 = (f32[320]{0:T(512)S(1)}, f32[320]{0:T(512)}, u32[]{:S(2)}) copy-start(f32[320]{0:T(512)} %copy-done.109) | copy-start | bytes 3844
  1365.4 95.7 %copy-start.132 = (f32[320]{0:T(512)S(1)}, f32[320]{0:T(512)}, u32[]{:S(2)}) copy-start(f32[320]{0:T(512)} %copy-done.131) | copy-start | bytes 3844
  1365.4 95.7 %copy-start.122 = (f32[320]{0:T(512)S(1)}, f32[320]{0:T(512)}, u32[]{:S(2)}) copy-start(f32[320]{0:T(512)} %copy-done.121) | copy-start | bytes 3844
  1464.7 139.9 %reduce-scatter.49.cloned.1.call-start = ((), (), s32[]{:S(2)}) async-start(), calls=%async_computation.47 | async-start | bytes 4718592 | tf_op jit(solution)/shard_map/reduce_scatter | solution.py:316
  1473.5 170.2 %reduce-scatter.47.cloned.1.call-start = ((), (), s32[]{:S(2)}) async-start(), calls=%async_computation.46 | async-start | bytes 4718592 | tf_op jit(solution)/shard_map/reduce_scatter | solution.py:315
  1484.2 199.2 %reduce-scatter.45.cloned.1.call-start = ((), (), s32[]{:S(2)}) async-start(), calls=%async_computation.45 | async-start | bytes 1179648 | tf_op jit(solution)/shard_map/reduce_scatter | solution.py:314
  1489.0 243.9 %reduce-scatter.43.cloned.1.call-start = ((), (), s32[]{:S(2)}) async-start(), calls=%async_computation.44 | async-start | bytes 3538944 | tf_op jit(solution)/shard_map/reduce_scatter | solution.py:313
  1497.9 275.2 %reduce-scatter.35.cloned.1.call-start = ((), (), s32[]{:S(2)}) async-start(), calls=%async_computation.40 | async-start | bytes 1179648 | tf_op jit(solution)/shard_map/reduce_scatter | solution.py:332
  1545.7 28.1 %copy-start.92 = (f32[8,1024]{1,0:T(8,128)S(1)}, f32[8,1024]{1,0:T(8,128)}, u32[]{:S(2)}) copy-start(f32[8,1024]{1,0:T(8,128)} %copy-done.91) | copy-start | bytes 98308
  1582.2 237.4 %reduce-scatter.39.cloned.1.call-start = ((), (), s32[]{:S(2)}) async-start(), calls=%async_computation.42 | async-start | bytes 2764800 | tf_op jit(solution)/shard_map/reduce_scatter | solution.py:334
  1584.3 290.4 %reduce-scatter.37.cloned.1.call-start = ((), (), s32[]{:S(2)}) async-start(), calls=%async_computation.41 | async-start | bytes 4718592 | tf_op jit(solution)/shard_map/reduce_scatter | solution.py:333
  1587.2 448.0 %reduce-scatter.41.cloned.1.call-start = ((), (), s32[]{:S(2)}) async-start(), calls=%async_computation.43 | async-start | bytes 28311552 | tf_op jit(solution)/shard_map/reduce_scatter | solution.py:335
  2039.2 44.0 %copy-start.115 = (f32[3,32,128]{2,1,0:T(8,128)S(1)}, f32[3,32,128]{2,1,0:T(8,128)}, u32[]{:S(2)}) copy-start(f32[3,32,128]{2,1,0:T(8,128)} %param.20) | copy-start | bytes 147460
  2039.2 44.7 %copy-start.116 = (f32[3,128,32]{1,2,0:T(8,128)S(1)}, f32[3,128,32]{1,2,0:T(8,128)}, u32[]{:S(2)}) copy-start(f32[3,128,32]{1,2,0:T(8,128)} %param.21) | copy-start | bytes 147460
  2039.2 45.3 %copy-start.16 = (f32[1,128,6,1024]{1,3,2,0:T(8,128)S(1)}, f32[1,128,6,1024]{1,3,2,0:T(8,128)}, u32[]{:S(2)}) copy-start(f32[1,128,6,1024]{1,3,2,0:T(8,128)} %copy-done.15) | copy-start | bytes 9437188
  (130 other events, 558.4 us)
Sparse Core Ops, SparseCore 0:
  10.5 30.7 all-gather.14
  43.7 24.3 all-gather.16
  70.6 74.5 all-gather.18
  147.5 25.7 all-gather.22
  175.3 54.8 all-gather.20
  232.2 53.5 all-gather.30
  288.1 92.5 reduce-scatter.18
  383.5 94.2 reduce-scatter.22
  480.3 28.3 all-gather.26
  510.1 54.7 all-gather.24
  567.4 26.9 all-gather.28
  596.4 54.7 all-gather.32
  653.6 93.5 reduce-scatter.20
  749.3 94.1 reduce-scatter.24
  851.6 55.2 all-gather.38
  908.4 53.5 all-gather.34
  964.7 92.5 reduce-scatter.28
  1059.4 94.2 reduce-scatter.26
  1155.9 55.3 all-gather.40
  1213.2 53.5 all-gather.36
  1269.1 92.5 reduce-scatter.32
  1364.6 94.2 reduce-scatter.30
  1462.4 33.8 reduce-scatter.52
  1500.1 33.3 reduce-scatter.50
  1536.8 51.3 reduce-scatter.48
  1592.4 51.3 reduce-scatter.46
  1647.3 35.9 reduce-scatter.44
  1686.7 46.1 reduce-scatter.42
  1737.0 36.0 reduce-scatter.34
  1776.7 42.8 reduce-scatter.38
  1823.3 51.2 reduce-scatter.36
  1878.3 156.8 reduce-scatter.40
where the time goes:
time: 2140 us; the launch traced here: 2130 us
  waiting for transfers between devices  1380 us (64%)
  matrix products  255 us (12%)
  local copies, waits for them, and re-layouts  199 us (9%)
  blocking collectives  161 us (8%)
  other arithmetic  106 us (5%)
  between operations  27.9 us (1%)
    reduce_scatter x4, waiting for transfers between devices, branch_back(): lax.psum_scatter(dot_last(grad_pre, first_matrix), 'mp', scatter_dimensio...  313 us
    reduce_scatter x4, waiting for transfers between devices, sum_rows(): lax.psum_scatter(jnp.dot(inner_act, last_matrix, preferred_element_type=j...  230 us
    all_gather x4, waiting for transfers between devices, branch_back(): grad_whole = lax.all_gather(grad_low, 'mp', axis=0, tiled=True)  162 us
    reduce_scatter x1, waiting for transfers between devices, per_device(): lax.psum_scatter(adaptive_grad, 'dp', scatter_dimension=0, tiled=True)  157 us
    all_gather x4, waiting for transfers between devices, gather_rows(): lax.all_gather(normed.astype(jnp.bfloat16), 'mp', axis=0, tiled=True)  131 us
    unnamed x356, local copies, waits for them, and re-layouts  102 us
    all_gather x1, waiting for transfers between devices, per_device(): lax.all_gather(state_adaptive[0].astype(jnp.bfloat16), 'dp', axis=0, tile...  75.4 us
    dot_general x18, matrix products, dot_rows(): lax.dot_general(former, latter, (((0,), (0,)), ((), ())), precision=preci...  73.5 us
  transfers between devices with their start and end apart: 32, of which 27 were waited for; matrix products, arithmetic and copies ran while one was open for 23% of the time, Pallas kernels for 0%

commit v1 on v0

v1 whole, which is shorter than its diff:
```python
import functools
import math

import jax
import jax.numpy as jnp
from jax import lax
from jax.experimental import pallas as pl
from jax.experimental.pallas import tpu as pltpu
from jax.sharding import PartitionSpec as P

D = 1024
HEADS = 16
HD = 64
PATCH = 32
FREQ = 256
CLASSES = 600
WTOK = 320
NMB = 2
WMB = 4
TILE = 256
NJ = 12
ROWS = NMB * WTOK
MESH = pl.DeviceIdType.MESH
BF = jnp.bfloat16
F32 = jnp.float32


beta_one = 0.9
beta_two = 0.999
adam_eps = 1e-08
learn_rate = 0.15
weight_decay = 0.1
threshold = 0.002
step_count = 10.0


def timestep_features(step_ids):
    half_width = FREQ // 2
    frequency = jnp.exp(-math.log(10000.0) * jnp.arange(half_width, dtype=F32) / half_width)
    angles = step_ids.astype(F32)[:, None] * frequency[None, :]
    return jnp.concatenate([jnp.cos(angles), jnp.sin(angles)], axis=-1)


def window_positions(places):
    half_width = D // 2
    frequency = jnp.exp(-math.log(10000.0) * jnp.arange(half_width, dtype=F32) / half_width)
    angles = places.astype(F32)[:, None] * frequency[None, :]
    return jnp.concatenate([jnp.sin(angles), jnp.cos(angles)], axis=-1)


def dot_nn(a, b):
    return jnp.dot(a, b, preferred_element_type=F32)


def dot_nt(a, b):
    return lax.dot_general(a, b, (((1,), (1,)), ((), ())), preferred_element_type=F32)


def dot_tn(a, b):
    return lax.dot_general(a, b, (((0,), (0,)), ((), ())), preferred_element_type=F32)


def norm_parts(values):
    center = values - jnp.mean(values, axis=-1, keepdims=True)
    inverse = lax.rsqrt(jnp.mean(center * center, axis=-1, keepdims=True) + 1e-06)
    return center * inverse, inverse


def norm_back(grad, normed, inverse):
    mean_grad = jnp.mean(grad, axis=-1, keepdims=True)
    mean_prod = jnp.mean(grad * normed, axis=-1, keepdims=True)
    return inverse * (grad - mean_grad - normed * mean_prod)


def silu_slope(values):
    gate = jax.nn.sigmoid(values)
    return gate * (1.0 + values * (1.0 - gate))


def gelu_parts(up):
    cdf = 0.5 * (1.0 + lax.erf(up * math.sqrt(0.5)))
    pdf = jnp.exp(-0.5 * up * up) * (1.0 / math.sqrt(2.0 * math.pi))
    return up * cdf, cdf + up * pdf


def per_window(mod):
    return mod[:, None, :]


def tokens3(values):
    return values.reshape(NMB, WTOK, -1)


def spread(values, mod):
    return (tokens3(values) * mod[:, None, :]).reshape(ROWS, -1)


def modulated(normed, shift, scale):
    return (tokens3(normed) * (1.0 + scale[:, None, :]) + shift[:, None, :]).reshape(ROWS, -1)


def window_sum(values):
    return jnp.sum(tokens3(values), axis=1)


def split_heads(qkv):
    shaped = qkv.reshape(NMB, WTOK, 3, HEADS, HD)
    return shaped[:, :, 0], shaped[:, :, 1], shaped[:, :, 2]


def scores_of(query, key, flags):
    scores = jnp.einsum("wqhe,wkhe->whqk", query, key, preferred_element_type=F32) * HD ** (-0.5)
    return jnp.where(flags.reshape(NMB, 1, 1, WTOK) > 0, scores, -1e30)


def attend(qkv, flags):
    query, key, value = split_heads(qkv)
    attn = jax.nn.softmax(scores_of(query, key, flags), axis=-1).astype(BF)
    mixed = jnp.einsum("whqk,wkhe->wqhe", attn, value, preferred_element_type=F32)
    return mixed.astype(BF).reshape(ROWS, D)


def attend_back(grad_mixed, qkv, flags):
    query, key, value = split_heads(qkv)
    grad_heads = grad_mixed.reshape(NMB, WTOK, HEADS, HD)
    attn_full = jax.nn.softmax(scores_of(query, key, flags), axis=-1)
    attn = attn_full.astype(BF)
    grad_value = jnp.einsum("whqk,wqhe->wkhe", attn, grad_heads, preferred_element_type=F32)
    grad_attn = jnp.einsum("wqhe,wkhe->whqk", grad_heads, value, preferred_element_type=F32)
    grad_scores = attn_full * (grad_attn - jnp.sum(attn_full * grad_attn, axis=-1, keepdims=True))
    grad_scores = grad_scores.astype(BF)
    grad_query = jnp.einsum("whqk,wkhe->wqhe", grad_scores, key, preferred_element_type=F32)
    grad_key = jnp.einsum("whqk,wqhe->wkhe", grad_scores, query, preferred_element_type=F32)
    parts = jnp.stack([grad_query * HD ** (-0.5), grad_key * HD ** (-0.5), grad_value], axis=2)
    return parts.astype(BF).reshape(ROWS, 3, D)


def flip(bits, at):
    return [1 - bit if place == at else bit for place, bit in enumerate(bits)]


class Place:
    def __init__(self, nd, nm):
        self.nm = nm
        self.nb = nd.bit_length() - 2
        dp_id = lax.axis_index("dp")
        self.m = lax.axis_index("mp")
        self.core = dp_id % 2
        self.bits = [dp_id // (1 << (self.nb - at)) % 2 for at in range(self.nb)]
        self.sibling = {"dp": self.dp_of(self.bits, 1 - self.core), "mp": self.m}
        self.orders = (list(range(self.nb))[::-1], list(range(self.nb)))
        self.halves = (pl.ds(0, nm // 2), pl.ds(nm // 2, nm - nm // 2))

    def dp_of(self, bits, core):
        total = core
        for at, bit in enumerate(bits):
            total = total + bit * (1 << (self.nb - at))
        return total

    def across(self, at):
        return {"dp": self.dp_of(flip(self.bits, at), self.core), "mp": self.m}

    def along(self, hops):
        return {"dp": self.dp_of(self.bits, self.core), "mp": (self.m + hops) % self.nm}

    def pick(self, half, done, flipped=None):
        where = flip(self.bits, flipped)
        return (self.halves[half],) + tuple(
            pl.ds(0, 2) if at in done else pl.ds(where[at], 1) for at in range(self.nb)
        )

    def mine(self, m=None):
        return (self.m if m is None else m,) + tuple(self.bits)

    def greet(self):
        barrier = pltpu.get_barrier_semaphore()
        others = [self.sibling]
        others += [self.across(at) for at in range(self.nb)]
        others += [self.along(hops) for hops in range(1, self.nm)]
        for other in others:
            pl.semaphore_signal(barrier, inc=1, device_id=other, device_id_type=MESH)
        pl.semaphore_wait(barrier, len(others))


class Copies:
    def __init__(self, send_sems, recv_sems):
        self.send_sems, self.recv_sems = send_sems, recv_sems
        self.started = {}

    def start(self, step, slot, source, target, device):
        copy = pltpu.make_async_remote_copy(
            src_ref=source,
            dst_ref=target,
            send_sem=self.send_sems.at[step, slot],
            recv_sem=self.recv_sems.at[step, slot],
            device_id=device,
            device_id_type=MESH,
        )
        copy.start()
        self.started[step, slot] = copy

    def arrived(self, step, slot):
        self.started[step, slot].wait_recv()

    def drain(self):
        for copy in self.started.values():
            copy.wait_send()


def gather_kernel(nd, nm, shard, whole, send_sems, recv_sems, local_sems):
    place = Place(nd, nm)
    nb, core = place.nb, place.core
    copies = Copies(send_sems, recv_sems)
    z_slots = [hops - 1 for hops in range(1, nm)]
    stage_slot = lambda stage, half: nm - 1 + 2 * stage + half
    twin = nm - 1 + 2 * nb
    locals_ = {}
    place.greet()

    def begin(j):
        here = whole.at[(j,) + place.mine() + (core,)]
        locals_[j] = pltpu.make_async_copy(shard.at[j], here, local_sems.at[j])
        locals_[j].start()
        for hops in range(1, nm):
            copies.start(j, hops - 1, shard.at[j], here, place.along(hops))
        copies.start(j, 2 * twin, shard.at[j], here, place.sibling)

    def stage(j, step):
        if step == 0:
            locals_[j].wait()
            for hops in range(1, nm):
                copies.arrived(j, hops - 1)
        else:
            for half in range(2):
                copies.arrived(j, stage_slot(step - 1, half))
        if step < nb:
            for half in range(2):
                order = place.orders[half]
                block = whole.at[(j,) + place.pick(half, order[:step]) + (core,)]
                copies.start(j, stage_slot(step, half), block, block, place.across(order[step]))
        if step == 0:
            for hops in range(1, nm):
                block = whole.at[(j,) + place.mine((place.m + nm - hops) % nm) + (core,)]
                copies.start(j, twin + hops - 1, block, block, place.sibling)
        else:
            for half in range(2):
                order = place.orders[half]
                block = whole.at[
                    (j,) + place.pick(half, order[: step - 1], order[step - 1]) + (core,)
                ]
                copies.start(j, twin + stage_slot(step - 1, half), block, block, place.sibling)

    def finish(j):
        for slot in range(twin, 2 * twin + 1):
            copies.arrived(j, slot)

    for turn in range(NJ + nb + 2):
        if turn < NJ:
            begin(turn)
        for step in range(nb + 1):
            if 0 <= turn - 1 - step < NJ:
                stage(turn - 1 - step, step)
        if 0 <= turn - 2 - nb < NJ:
            finish(turn - 2 - nb)
    copies.drain()


def gather_blocks(shard):
    nd, nm = lax.axis_size("dp"), lax.axis_size("mp")
    nb = nd.bit_length() - 2
    rows = shard.shape[1]
    slots = 2 * (nm - 1 + 2 * nb) + 1
    whole = pl.pallas_call(
        functools.partial(gather_kernel, nd, nm),
        out_shape=jax.ShapeDtypeStruct((NJ, nm) + (2,) * nb + (2, rows, TILE), BF),
        in_specs=[pl.BlockSpec(memory_space=pl.ANY)],
        out_specs=pl.BlockSpec(memory_space=pl.ANY),
        scratch_shapes=[
            pltpu.SemaphoreType.DMA((NJ, slots)),
            pltpu.SemaphoreType.DMA((NJ, slots)),
            pltpu.SemaphoreType.DMA((NJ,)),
        ],
        compiler_params=pltpu.CompilerParams(collective_id=0, has_side_effects=True),
    )(shard)
    return whole.reshape(NJ, nm, nd * rows, TILE)


def reduce_kernel(nd, nm, partial, total, mine_ref, twin_ref, stage_refs, z_ref, send_sems, recv_sems, local_sems):
    place = Place(nd, nm)
    nb, core = place.nb, place.core
    copies = Copies(send_sems, recv_sems)
    orders = [order[::-1] for order in place.orders]
    locals_ = {}
    place.greet()
    slot_of = lambda step, half: 1 + 2 * step + half
    z_slot = 1 + 2 * nb

    def add_to(target, index, source):
        shape = source.shape[:-2]
        count = math.prod(shape)

        def body(at, carry):
            inner, places = at, []
            for size in shape[::-1]:
                places.append(inner % size)
                inner = inner // size
            places = places[::-1]
            spot = tuple(
                base.start + offset if isinstance(base, pl.Slice) else base
                for base, offset in zip(index, places)
            )
            target[spot] = (target[spot].astype(F32) + source[tuple(places)].astype(F32)).astype(BF)
            return carry

        lax.fori_loop(0, count, body, 0)

    def begin(j):
        every = (slice(None),) * (nb + 1)
        locals_[j] = pltpu.make_async_copy(
            partial.at[(j,) + every + (core,)], mine_ref.at[j], local_sems.at[j]
        )
        locals_[j].start()
        copies.start(
            j, 0, partial.at[(j,) + every + (1 - core,)], twin_ref.at[j], place.sibling
        )

    def stage(j, step):
        if step == 0:
            locals_[j].wait()
            copies.arrived(j, 0)
            add_to(mine_ref.at[j], (pl.ds(0, nm),) + (pl.ds(0, 2),) * nb, twin_ref.at[j])
        else:
            for half in range(2):
                copies.arrived(j, slot_of(step - 1, half))
                index = place.pick(half, orders[half][step:])
                add_to(mine_ref.at[j], index, stage_refs[step - 1].at[j, half])
        if step < nb:
            for half in range(2):
                order = orders[half]
                block = mine_ref.at[(j,) + place.pick(half, order[step + 1 :], order[step])]
                target = stage_refs[step].at[j, half]
                copies.start(j, slot_of(step, half), block, target, place.across(order[step]))
        else:
            for hops in range(1, nm):
                block = mine_ref.at[(j,) + place.mine((place.m + hops) % nm)]
                copies.start(j, z_slot + hops - 1, block, z_ref.at[j, hops - 1], place.along(hops))

    def finish(j):
        summed = mine_ref[(j,) + place.mine()].astype(F32)
        for hops in range(1, nm):
            copies.arrived(j, z_slot + hops - 1)
            summed = summed + z_ref[j, hops - 1].astype(F32)
        total[j] = summed

    for turn in range(NJ + nb + 2):
        if turn < NJ:
            begin(turn)
        for step in range(nb + 1):
            if 0 <= turn - 1 - step < NJ:
                stage(turn - 1 - step, step)
        if 0 <= turn - 2 - nb < NJ:
            finish(turn - 2 - nb)
    copies.drain()


def reduce_blocks(partial):
    nd, nm = lax.axis_size("dp"), lax.axis_size("mp")
    nb = nd.bit_length() - 2
    rows = partial.shape[2] // nd
    bits = (2,) * nb
    slots = 2 * nb + nm

    def kernel(partial, total, mine_ref, twin_ref, *rest):
        stage_refs = [HalfRefs(rest[2 * step], rest[2 * step + 1]) for step in range(nb)]
        reduce_kernel(nd, nm, partial, total, mine_ref, twin_ref, stage_refs, *rest[2 * nb :])

    stage_shapes = []
    for step in range(nb):
        low_first = tuple(1 if at <= step else 2 for at in range(nb))
        high_first = tuple(1 if nb - 1 - at <= step else 2 for at in range(nb))
        stage_shapes.append(pltpu.VMEM((NJ, nm // 2) + low_first + (rows, TILE), BF))
        stage_shapes.append(pltpu.VMEM((NJ, nm - nm // 2) + high_first + (rows, TILE), BF))
    total = pl.pallas_call(
        kernel,
        out_shape=jax.ShapeDtypeStruct((NJ, rows, TILE), F32),
        in_specs=[pl.BlockSpec(memory_space=pl.ANY)],
        out_specs=pl.BlockSpec(memory_space=pltpu.VMEM),
        scratch_shapes=[
            pltpu.VMEM((NJ, nm) + bits + (rows, TILE), BF),
            pltpu.VMEM((NJ, nm) + bits + (rows, TILE), BF),
            *stage_shapes,
            pltpu.VMEM((NJ, nm - 1, rows, TILE), BF),
            pltpu.SemaphoreType.DMA((NJ, slots)),
            pltpu.SemaphoreType.DMA((NJ, slots)),
            pltpu.SemaphoreType.DMA((NJ,)),
        ],
        compiler_params=pltpu.CompilerParams(
            collective_id=1, has_side_effects=True, vmem_limit_bytes=60 << 20
        ),
    )(partial.reshape((NJ, nm) + bits + (2, rows, TILE)))
    return total


class HalfRefs:
    def __init__(self, first, second):
        self.refs = (first, second)

    @property
    def at(self):
        return self

    def __getitem__(self, index):
        j, half = index
        return self.refs[half].at[j]


def adam_update(state_in, gradient, factor):
    clipped = gradient * factor
    first_moment = beta_one * state_in[1] + (1.0 - beta_one) * clipped
    second_moment = beta_two * state_in[2] * state_in[2] + (1.0 - beta_two) * clipped * clipped
    root_moment = jnp.sqrt(second_moment)
    update = (
        first_moment
        / (1.0 - beta_one**step_count)
        / (root_moment / math.sqrt(1.0 - beta_two**step_count) + adam_eps)
    )
    new_weight = state_in[0] - learn_rate * (update + weight_decay * state_in[0])
    return (new_weight, jnp.stack([first_moment, root_moment]))


def per_device(
    latents,
    noise_target,
    token_mask,
    timesteps,
    labels,
    state_embed,
    state_head,
    state_time_in,
    state_time_out,
    state_classes,
    state_adaptive,
    state_attention_in,
    state_attention_out,
    state_expand,
    state_contract,
):
    nd, nm = lax.axis_size("dp"), lax.axis_size("mp")
    dp_id, mp_id = lax.axis_index("dp"), lax.axis_index("mp")
    rows = state_attention_in.shape[1]
    attn_in_tiles = state_attention_in[0].transpose(1, 0, 2)
    expand_tiles = state_expand[0].reshape(rows, 4, TILE).transpose(1, 0, 2)
    contract_tiles = state_contract[0].reshape(4, TILE, rows).transpose(0, 2, 1)
    ff_tiles = jnp.stack([expand_tiles, contract_tiles], axis=1).reshape(8, rows, TILE)
    shard = jnp.concatenate(
        [attn_in_tiles, state_attention_out[0].T[None], ff_tiles], axis=0
    ).astype(BF)
    weights = gather_blocks(shard)

    mask = token_mask.astype(F32).reshape(ROWS)
    token_total = lax.psum(jnp.sum(mask), ("dp", "mp"))
    ends = jnp.stack([state_embed[0], state_head[0].T]).astype(BF)
    ends = lax.all_gather(ends, "dp", axis=2, tiled=True)
    embed_mat, head_t = ends[0], ends[1]

    both_ids = lax.all_gather(jnp.stack([timesteps, labels])[:, 0], "dp", axis=1, tiled=False)
    both_ids = both_ids.reshape(2, nd * NMB * WMB)
    features = timestep_features(both_ids[0]).astype(BF)
    pick = (both_ids[1][:, None] == jnp.arange(CLASSES)[None, :]).astype(BF)
    time_pre = dot_nn(features, state_time_in[0].astype(BF))
    time_hidden = jax.nn.silu(time_pre).astype(BF)
    time_out_part = state_time_out[0].astype(BF)
    condition = lax.psum_scatter(
        dot_nn(time_hidden, time_out_part), "dp", scatter_dimension=1, tiled=True
    ) + dot_nn(pick, state_classes[0].astype(BF))
    cond_act = jax.nn.silu(condition).astype(BF)
    adaptive_part = state_adaptive[0].astype(BF).reshape(rows, 6 * D)
    mine = lax.dynamic_index_in_dim(
        cond_act.reshape(nd * NMB, WMB, rows), mp_id, 1, keepdims=False
    )
    mod = lax.psum_scatter(dot_nn(mine, adaptive_part), "dp", scatter_dimension=0, tiled=True)
    mod = mod.reshape(NMB, 6, D)

    latent_rows = latents.reshape(ROWS, PATCH)
    noise_rows = noise_target.reshape(ROWS, PATCH)
    positions = window_positions(jnp.arange(WTOK, dtype=jnp.int32))
    residual = (tokens3(dot_nn(latent_rows, embed_mat)) + positions[None]).reshape(ROWS, D)
    ln_one, inv_one = norm_parts(residual)
    n_one = modulated(ln_one, mod[:, 0], mod[:, 1]).astype(BF)
    qkv = jnp.einsum("tk,jmkc->tjmc", n_one, weights[:3], preferred_element_type=F32).astype(BF)
    qkv = qkv.reshape(ROWS, 3, D)
    mixed = attend(qkv, mask)
    mixed_tiles = mixed.reshape(ROWS, nm, TILE)
    branch_one = jnp.einsum("tmc,mnc->tn", mixed_tiles, weights[3], preferred_element_type=F32)
    middle = residual + spread(branch_one, mod[:, 2])
    ln_two, inv_two = norm_parts(middle)
    n_two = modulated(ln_two, mod[:, 3], mod[:, 4]).astype(BF)
    up = jnp.einsum("tk,fmkc->tfmc", n_two, weights[4::2], preferred_element_type=F32)
    hidden, slope = gelu_parts(up)
    hidden = hidden.astype(BF)
    branch_two = jnp.einsum("tfmc,fmnc->tn", hidden, weights[5::2], preferred_element_type=F32)
    final = middle + spread(branch_two, mod[:, 5])
    ln_out, inv_out = norm_parts(final)
    ln_low = ln_out.astype(BF)
    prediction = dot_nt(ln_low, head_t)
    error = prediction - noise_rows
    loss_local = jnp.sum(jnp.mean(error * error, axis=-1) * mask) / token_total

    grad_pred = (2.0 / PATCH * error * mask[:, None] / token_total).astype(BF)
    head_grad = dot_tn(grad_pred, ln_low)
    grad_final = norm_back(dot_nn(grad_pred, head_t), ln_out, inv_out)
    gate_two = window_sum(grad_final * branch_two)
    g_two = spread(grad_final, mod[:, 5]).astype(BF)
    contract_grad = jnp.einsum("tn,tfmc->fmnc", g_two, hidden, preferred_element_type=F32)
    grad_hidden = jnp.einsum("tn,fmnc->tfmc", g_two, weights[5::2], preferred_element_type=F32)
    grad_up = (grad_hidden * slope).astype(BF)
    expand_grad = jnp.einsum("tk,tfmc->fmkc", n_two, grad_up, preferred_element_type=F32)
    grad_n_two = jnp.einsum("tfmc,fmkc->tk", grad_up, weights[4::2], preferred_element_type=F32)
    shift_two, scale_two = window_sum(grad_n_two), window_sum(grad_n_two * ln_two)
    grad_middle = grad_final + norm_back(spread(grad_n_two, 1.0 + mod[:, 4]), ln_two, inv_two)
    gate_one = window_sum(grad_middle * branch_one)
    g_one = spread(grad_middle, mod[:, 2]).astype(BF)
    out_grad = jnp.einsum("tn,tmc->mnc", g_one, mixed_tiles, preferred_element_type=F32)
    grad_mixed = jnp.einsum("tn,mnc->tmc", g_one, weights[3], preferred_element_type=F32)
    grad_qkv = attend_back(grad_mixed.astype(BF).reshape(ROWS, D), qkv, mask)
    grad_qkv = grad_qkv.reshape(ROWS, 3, nm, TILE)
    in_grad = jnp.einsum("tk,tjmc->jmkc", n_one, grad_qkv, preferred_element_type=F32)
    grad_n_one = jnp.einsum("tjmc,jmkc->tk", grad_qkv, weights[:3], preferred_element_type=F32)
    shift_one, scale_one = window_sum(grad_n_one), window_sum(grad_n_one * ln_one)
    grad_embedded = grad_middle + norm_back(spread(grad_n_one, 1.0 + mod[:, 1]), ln_one, inv_one)
    embed_grad = dot_tn(latent_rows, grad_embedded.astype(BF))
    ff_grad = jnp.stack([expand_grad, contract_grad], axis=1).reshape(8, nm, D, TILE)
    partial = jnp.concatenate([in_grad, out_grad[None], ff_grad], axis=0).astype(BF)
    reduced = reduce_blocks(partial)

    ends_grad = lax.psum(jnp.stack([embed_grad, head_grad]), ("dp", "mp"))
    ends_grad = lax.dynamic_slice_in_dim(ends_grad, dp_id * rows, rows, 2)
    grad_mod = jnp.stack([shift_one, scale_one, gate_one, shift_two, scale_two, gate_two], axis=1)
    grad_mod = grad_mod.astype(BF).reshape(NMB, 6 * D)
    grad_mod = lax.all_gather(grad_mod, ("dp", "mp"), axis=0, tiled=False)
    grad_mod = grad_mod.reshape(nd, nm, NMB, 6 * D).transpose(0, 2, 1, 3)
    grad_mod = grad_mod.reshape(nd * NMB * WMB, 6 * D)
    adaptive_grad = dot_tn(cond_act, grad_mod).reshape(rows, 6, D)
    grad_cond = (dot_nt(grad_mod, adaptive_part) * silu_slope(condition)).astype(BF)
    classes_grad = dot_tn(pick, grad_cond)
    grad_cond_all = lax.all_gather(grad_cond, "dp", axis=1, tiled=True)
    time_out_grad = dot_tn(time_hidden, grad_cond_all)
    grad_time = (dot_nt(grad_cond_all, time_out_part) * silu_slope(time_pre)).astype(BF)
    time_in_grad = dot_tn(features, grad_time)

    small_grads = (
        ends_grad[0],
        ends_grad[1].T,
        time_in_grad,
        time_out_grad,
        classes_grad,
        adaptive_grad,
    )
    square_small = sum(jnp.sum(gradient * gradient) for gradient in small_grads)
    square_local = jnp.sum(reduced * reduced) + square_small / nm
    loss_value, square_total = lax.psum((loss_local, square_local), ("dp", "mp"))
    grad_norm = jnp.sqrt(square_total)
    factor = jnp.minimum(1.0, threshold / grad_norm)
    ff_reduced = reduced[4:].reshape(4, 2, rows, TILE)
    block_grads = (
        reduced[:3].transpose(1, 0, 2),
        reduced[3].T,
        ff_reduced[:, 0].transpose(1, 0, 2).reshape(rows, 4 * TILE),
        ff_reduced[:, 1].transpose(0, 2, 1).reshape(4 * TILE, rows),
    )
    all_states = (
        state_embed,
        state_head,
        state_time_in,
        state_time_out,
        state_classes,
        state_adaptive,
        state_attention_in,
        state_attention_out,
        state_expand,
        state_contract,
    )
    results = [loss_value, grad_norm]
    for state_in, gradient in zip(all_states, small_grads + block_grads):
        new_weight, moments = adam_update(state_in, gradient, factor)
        results.append(new_weight)
        results.append(moments)
    return tuple(results)


def solution(mesh):
    in_specs = (
        P("dp", None, "mp", None),
        P("dp", None, "mp", None),
        P("dp", None, "mp"),
        P("dp", None, None),
        P("dp", None, None),
        P(None, None, "dp"),
        P(None, "dp", None),
        P(None, None, "dp"),
        P(None, "dp", None),
        P(None, None, "dp"),
        P(None, "dp", None, None),
        P(None, "dp", None, "mp"),
        P(None, "mp", "dp"),
        P(None, "dp", "mp"),
        P(None, "mp", "dp"),
    )
    out_specs = (
        P(),
        P(),
        P(None, "dp"),
        P(None, None, "dp"),
        P("dp", None),
        P(None, "dp", None),
        P(None, "dp"),
        P(None, None, "dp"),
        P("dp", None),
        P(None, "dp", None),
        P(None, "dp"),
        P(None, None, "dp"),
        P("dp", None, None),
        P(None, "dp", None, None),
        P("dp", None, "mp"),
        P(None, "dp", None, "mp"),
        P("mp", "dp"),
        P(None, "mp", "dp"),
        P("dp", "mp"),
        P(None, "dp", "mp"),
        P("mp", "dp"),
        P(None, "mp", "dp"),
    )
    return jax.shard_map(
        per_device, mesh=mesh, in_specs=in_specs, out_specs=out_specs, check_vma=False
    )
```

time: 2140 us -> 939 us (0.44)
  waiting for transfers between devices: 1380 us -> 52.9 us
  Pallas kernels: 0 us -> 247 us
  matrix products: 255 us -> 172 us
  local copies, waits for them, and re-layouts: 199 us -> 146 us
    reduce_scatter x18 -> x1, waiting for transfers between devices: 955 us -> 0.02 us  [per_device(): lax.psum_scatter(dot_nn(time_hidden, time_out_part), 'dp', scatter_dimens...]
    all_gather x14 -> x0, waiting for transfers between devices: 422 us -> none  [the longest x4 162 us: branch_back(): grad_whole = lax.all_gather(grad_low, 'mp', axis=0, tiled=True)]
    pallas_call x0 -> x2, Pallas kernels: none -> 247 us  [the longest x1 125 us: gather_blocks(): pl.pallas_call(functools.partial(gather_kernel, nd, nm), out_shape=jax.Sh...]
    dot_general x59 -> x31, matrix products: 255 us -> 161 us  [the longest x1 13.7 us: per_device(): jnp.einsum('tn,fmnc->tfmc', g_two, weights[5::2], preferred_element_type=...]
    unnamed x356 -> x185, local copies, waits for them, and re-layouts: 102 us -> 19 us
    all_gather x4, blocking collectives: 41.8 us -> 100 us  [the longest x1 73.4 us: per_device(): grad_mod = lax.all_gather(grad_mod, ('dp', 'mp'), axis=0, tiled=False)]
    unnamed x32 -> x4, waiting for transfers between devices: 0.52 us -> 52.9 us
    another operation x2 -> x13, local copies, waits for them, and re-layouts: 18.3 us -> 56.5 us  [the longest x1 21.6 us: per_device(): jnp.stack([expand_grad, contract_grad], axis=1).reshape(8, nm, D, TILE)]
  transfers between devices with their start and end apart: 32 -> 3, of which waited for: 27 -> 1; matrix products, arithmetic and copies ran while one was open for 23% -> 6% of each run, Pallas kernels for 0% -> 27%
where the time goes in v1:
time: 939 us; the launch traced here: 928 us
  Pallas kernels  247 us (26%)
  blocking collectives  179 us (19%)
  matrix products  172 us (18%)
  local copies, waits for them, and re-layouts  146 us (16%)
  other arithmetic  107 us (11%)
  waiting for transfers between devices  52.9 us (6%)
  between operations  23.7 us (3%)
    pallas_call x1, Pallas kernels, gather_blocks(): pl.pallas_call(functools.partial(gather_kernel, nd, nm), out_shape=jax.Sh...  125 us
    pallas_call x1, Pallas kernels, reduce_blocks(): pl.pallas_call(kernel, out_shape=jax.ShapeDtypeStruct((NJ, rows, TILE), F...  122 us
    all_gather x1, blocking collectives, per_device(): grad_mod = lax.all_gather(grad_mod, ('dp', 'mp'), axis=0, tiled=False)  73.4 us
    unnamed x4, waiting for transfers between devices  52.9 us
    psum x1, blocking collectives, per_device(): token_total = lax.psum(jnp.sum(mask), ('dp', 'mp'))  39.6 us
    psum x1, blocking collectives, per_device(): lax.psum((loss_local, square_local), ('dp', 'mp'))  39.2 us
    another operation x17, other arithmetic, adam_update(): return (new_weight, jnp.stack([first_moment, root_moment]))  24 us
    another operation x1, local copies, waits for them, and re-layouts, per_device(): jnp.stack([expand_grad, contract_grad], axis=1).reshape(8, nm, D, TILE)  21.6 us
  transfers between devices with their start and end apart: 3, of which 1 were waited for; matrix products, arithmetic and copies ran while one was open for 6% of the time, Pallas kernels for 27%

profile of v1, /device:TPU:0, one launch (start us, length us, event | category | flops | bytes accessed | tf_op | source)
XLA Modules:
  0.0 928.4 jit_solution(9237287548249184067)
XLA Ops:
  8.0 10.3 %all_gather.13 = s32[2,8,2,4]{3,2,1,0:T(2,128)S(1)} all-gather(s32[2,1,2,4]{3,2,1,0:T(2,128)S(1)} %pad_add_fusion), channel_id=1, replica_groups=mesh['dp'=8,'mp'=4] {'dp'}, dimensions={1}, use_global_device_ids=true | all-gather | bytes 576 | tf_op jit(solution)/shard_map/all_gather | solution.py:466
  27.4 124.6 %shard_map.318 = bf16[12,4,2,2,2,128,256]{6,5,4,3,2,1,0:T(8,128)(2,1)} custom-call(bf16[12,128,256]{2,1,0:T(8,128)(2,1)} %pad_maximum_fusion.7.shard), custom_call_target="tpu_custom_call" | custom-call | tf_op jit(solution)/shard_map/pallas_call | solution.py:273
  152.0 3.2 slice.229
  155.2 6.3 slice.224
  163.5 8.2 all_gather.12
  174.7 2.1 slice.426
  179.7 2.3 multiply_sine_fusion
  185.3 2.7 fusion.165
  188.3 52.8 %all-reduce.7.cloned.1.call-done = f32[16,6144]{1,0:T(8,128)} async-done(((f32[16,6144]{1,0:T(8,128)}), f32[16,6144]{1,0:T(8,128)}) %all-reduce.7.cloned.1.call-update) | async-done | bytes 393232
  242.2 2.3 fusion.30
  245.6 8.5 convolution_convert_fusion
  254.1 6.3 copy.207
  260.4 10.5 %reshape_reshape.6 = bf16[2,320,3,16,64]{1,0,4,3,2:T(2,128)(2,1)} reshape(bf16[640,3,4,256]{0,3,2,1:T(8,128)(2,1)} %copy.207) | data formatting | bytes 7864320 | tf_op jit(solution)/shard_map/reshape;reshape | solution.py:107
  271.0 7.6 fusion.182
  278.6 10.9 %fusion.186 = (f32[2,16,320]{2,1,0:T(8,128)S(1)}, f32[2,16,320,320]{2,3,1,0:T(8,128)}) fusion(pred[2,320]{1,0:T(4,128)(4,1)S(1)} %compare_bitcast_fusion, bf16[2,320,1,16,64]{1,0,4,3,2:T(2,128)(2,1)} %get-tuple-element.159, bf16[2,320,1,16,64]{1,0,4,3,2:T(2,128)(2,1)} %get-tuple-element.158), kind=kOutput, calls=%fused_computation.379 | convolution fusion | flops 432537920 | bytes 15770240 | tf_op jit(solution)/shard_map/sub | solution.py:118
  289.5 7.5 fusion.54
  297.0 2.8 copy.212
  299.8 4.8 reshape_reshape.14
  304.7 5.5 fusion.180
  311.4 11.2 %multiply_convert_fusion.1 = (bf16[640,4,4,256]{3,0,2,1:T(8,128)(2,1)S(1)}, f32[640,4,4,256]{3,0,2,1:T(8,128)}) fusion(bf16[12,4,1024,256]{3,2,1,0:T(8,128)(2,1)} %bitcast.673, bf16[640,1024]{1,0:T(8,128)(2,1)S(1)} %fusion.34), kind=kOutput, calls=%fused_computation.15 | convolution fusion | flops 5381816320 | bytes 25427968 | tf_op jit(solution)/shard_map/tk,fmkc->tfmc/dot_general | solution.py:498
  322.6 11.1 %fusion.178 = (f32[640]{0:T(1024)S(1)}, f32[640,1024]{1,0:T(8,128)S(1)}, f32[640,1024,1,1]{1,0,3,2:T(8,128)}) fusion(f32[640,1024]{1,0:T(8,128)S(1)} %get-tuple-element.151, f32[2,1024]{1,0:T(2,128)S(1)} %get-tuple-element.232, bf16[640,4,4,256]{3,0,2,1:T(8,128)(2,1)S(1)} %get-tuple-element.214, bf16[12,4,1024,256]{3,2,1,0:T(8,128)(2,1)} %bitcast.674), kind=kOutput, calls=%fused_computation.373 | convolution fusion | flops 5370674688 | bytes 21506560 | tf_op jit(solution)/shard_map/tfmc,fmnc->tn/dot_general | solution.py:501
  336.9 39.6 %psum.28 = f32[]{:T(128)} all-reduce(f32[]{:T(128)} %get-tuple-element.140), channel_id=1, replica_groups=mesh['dp'=8,'mp'=4] {'dp','mp'}, use_global_device_ids=true, to_apply=%region_13.14 | all-reduce | flops 1 | bytes 8 | tf_op jit(solution)/shard_map/psum | solution.py:461
  376.6 3.0 convolution_bitcast_fusion.1
  379.6 3.7 fusion.176
  383.3 2.2 bitcast_multiply_fusion.9
  386.0 13.7 %fusion.7 = bf16[640,4,4,256]{3,0,2,1:T(8,128)(2,1)} fusion(f32[640,4,4,256]{3,0,2,1:T(8,128)} %get-tuple-element.215, bf16[12,4,1024,256]{3,2,1,0:T(8,128)(2,1)} %bitcast.675, bf16[640,1024]{1,0:T(8,128)(2,1)S(1)} %fusion.36), kind=kOutput, calls=%fused_computation.14 | convolution fusion | flops 5394923520 | bytes 25427968 | tf_op jit(solution)/shard_map/tn,fmnc->tfmc/dot_general | solution.py:515
  399.7 10.0 %fusion.38 = (f32[640]{0:T(1024)S(1)}, f32[640]{0:T(1024)S(1)}, f32[640,1024,1,1]{1,0,3,2:T(8,128)S(1)}) fusion(f32[2,1024]{1,0:T(2,128)S(1)} %bitcast.708, f32[640]{0:T(1024)S(1)} %add_rsqrt_fusion.1, f32[640,1024]{1,0:T(8,128)S(1)} %copy-done.1, f32[640]{0:T(1024)S(1)} %broadcast_multiply_fusion.8, bf16[640,4,4,256]{3,0,2,1:T(8,128)(2,1)} %fusion.7, ...), kind=kOutput, calls=%fused_computation.85 | convolution fusion | flops 5372640256 | bytes 18892800 | tf_op jit(solution)/shard_map/tfmc,fmkc->tk/dot_general | solution.py:518
  409.8 3.4 bitcast_multiply_fusion.12
  413.6 2.2 copy-done.17
  415.7 2.6 convolution_convert_fusion.1
  418.3 3.2 convert_bitcast_fusion.3
  421.6 9.3 convert_bitcast_fusion.1
  430.8 9.0 convert_bitcast_fusion
  439.9 2.4 copy.215
  442.3 4.7 reshape_reshape.15
  447.0 9.8 %fusion.51 = bf16[2,320,16,64]{1,3,2,0:T(8,128)(2,1)} fusion(bf16[2,320,16,64]{1,0,3,2:T(2,128)(2,1)} %reshape_reshape.15, f32[2,16,320,320]{2,3,1,0:T(8,128)} %get-tuple-element.212, f32[2,16,320]{2,1,0:T(8,128)S(1)} %get-tuple-element.211), kind=kOutput, calls=%fused_computation.99 | convolution fusion | flops 426639360 | bytes 15769600 | tf_op jit(solution)/shard_map/whqk,wqhe->wkhe/dot_general | solution.py:128
  456.8 10.1 %multiply_reduce_fusion = (f32[2,16,320]{2,1,0:T(8,128)S(1)}, f32[2,16,320,320]{2,3,1,0:T(8,128)}) fusion(f32[2,16,320,320]{2,3,1,0:T(8,128)} %get-tuple-element.212, f32[2,16,320]{2,1,0:T(8,128)S(1)} %get-tuple-element.211, bf16[2,320,1,16,64]{1,0,4,3,2:T(2,128)(2,1)S(1)} %copy-done.34, bf16[2,320,16,64]{1,0,3,2:T(2,128)(2,1)S(1)} %copy-done.35), kind=kOutput, calls=%fused_computation.4 | convolution fusion | flops 429250560 | bytes 28917760 | tf_op jit(solution)/shard_map/wqhe,wkhe->whqk/dot_general | solution.py:129
  466.9 11.3 %multiply_convert_fusion = bf16[2,16,320,320]{2,3,1,0:T(8,128)(2,1)S(1)} fusion(f32[2,16,320,320]{2,3,1,0:T(8,128)} %get-tuple-element.222, f32[2,16,320]{2,1,0:T(8,128)S(1)} %get-tuple-element.221, f32[2,16,320,320]{2,3,1,0:T(8,128)} %get-tuple-element.212, f32[2,16,320]{2,1,0:T(8,128)S(1)} %get-tuple-element.211), kind=kLoop, calls=%fused_computation.3 | loop fusion | flops 13107200 | bytes 32849920 | tf_op jit(solution)/shard_map/convert_element_type | solution.py:131
  478.3 3.7 fusion.50
  482.0 2.8 fusion.49
  492.3 4.2 copy.223
  496.5 4.5 stack.178
  500.9 4.2 copy.218
  505.1 4.6 stack.176
  509.7 4.2 copy.220
  513.9 4.5 stack.177
  521.5 9.1 fusion.37
  530.7 3.0 bitcast_multiply_fusion.11
  536.5 73.4 %all_gather.14 = bf16[32,2,6144]{2,1,0:T(2,128)(2,1)S(1)} all-gather(bf16[1,2,6144]{2,1,0:T(2,128)(2,1)S(1)} %bitcast.710), channel_id=1, replica_groups=mesh['dp'=8,'mp'=4] {'dp','mp'}, dimensions={0}, use_global_device_ids=true | all-gather | bytes 811008 | tf_op jit(solution)/shard_map/all_gather | solution.py:540
  613.2 8.6 all_gather.15
  623.5 2.0 multiply_reduce_fusion.11
  627.2 9.4 %convert_bitcast_fusion.2 = bf16[3,4,1024,256]{2,3,1,0:T(8,128)(2,1)} fusion(bf16[640,3,4,256]{0,3,2,1:T(8,128)(2,1)} %copy-done.18, bf16[640,1024]{1,0:T(8,128)(2,1)} %copy-done.37), kind=kOutput, calls=%fused_computation.32 | convolution fusion | flops 4029677568 | bytes 11534336 | tf_op jit(solution)/shard_map/tk,tjmc->jmkc/dot_general | solution.py:527
  638.0 2.9 copy.225
  640.9 13.8 %pad_maximum_fusion.1 = bf16[4,2,4,1024,256]{3,4,2,0,1:T(8,128)(2,1)} fusion(bf16[4,1,4,1024,256]{3,4,2,0,1:T(8,128)(2,1)} %convert_bitcast_fusion, bf16[4,1,4,1024,256]{3,4,2,0,1:T(8,128)(2,1)} %convert_bitcast_fusion.1), kind=kLoop, calls=%fused_computation.2 | loop fusion | flops 8388608 | bytes 33554432 | tf_op jit(solution)/shard_map/stack | solution.py:532
  654.7 21.6 %copy.228 = bf16[4,2,4,1024,256]{4,3,2,1,0:T(8,128)(2,1)} copy(bf16[4,2,4,1024,256]{3,4,2,0,1:T(8,128)(2,1)} %pad_maximum_fusion.1) | data formatting | bytes 33554432 | tf_op jit(solution)/shard_map/stack | solution.py:532
  678.7 8.8 copy.224
  687.5 17.1 %pad_maximum_fusion.partial = bf16[12,4,2,2,2,128,256]{6,5,4,3,2,1,0:T(8,128)(2,1)} fusion(bf16[8,4,2,2,2,128,256]{6,5,4,3,2,1,0:T(8,128)(2,1)} %bitcast.677, bf16[1,4,2,2,2,128,256]{6,5,4,3,2,1,0:T(8,128)(2,1)S(1)} %bitcast.692, bf16[3,4,2,2,2,128,256]{6,5,4,3,2,1,0:T(8,128)(2,1)} %bitcast.680), kind=kLoop, calls=%fused_computation.1 | loop fusion | flops 25165824 | bytes 50331648 | tf_op jit(solution)/shard_map/concatenate | solution.py:533
  704.6 122.3 %shard_map.319 = f32[12,128,256]{2,1,0:T(8,128)} custom-call(bf16[12,4,2,2,2,128,256]{6,5,4,3,2,1,0:T(8,128)(2,1)} %pad_maximum_fusion.partial), custom_call_target="tpu_custom_call" | custom-call | tf_op jit(solution)/shard_map/pallas_call | solution.py:383
  826.9 2.9 multiply_reduce_fusion.1
  837.5 39.2 %all-reduce.1 = (f32[]{:T(128)}, f32[]{:T(128)}) all-reduce(f32[]{:T(128)S(6)} %div.237, f32[]{:T(128)S(6)} %add.338), channel_id=1, replica_groups=mesh['dp'=8,'mp'=4] {'dp','mp'}, use_global_device_ids=true, to_apply=%region_14.15 | all-reduce | flops 2 | bytes 16 | tf_op jit(solution)/shard_map/psum | solution.py:561
  889.7 2.8 bitcast_subtract_fusion.1
  894.9 2.1 mul.1134
  901.2 6.2 fusion.75
  915.7 3.3 pad_maximum_fusion.2
  (296 shorter events, 81.7 us)
Async XLA Ops:
  7.2 176.3 %reduce-scatter.2.cloned.1.call-start = ((), (), s32[]{:S(2)}) async-start(), calls=%async_computation.1 | async-start | bytes 294912 | tf_op jit(solution)/shard_map/reduce_scatter | solution.py:473
  18.4 7.9 copy-start.52
  19.6 6.8 copy-start.43
  19.8 6.2 copy-start.56
  19.8 6.2 copy-start.58
  22.6 218.5 %all-reduce.7.cloned.1.call-start = ((), (), s32[]{:S(2)}) async-start(), calls=%async_computation.3 | async-start | bytes 786432
  26.4 125.6 %copy-start.45 = (f32[1,256,128]{1,2,0:T(8,128)}, f32[1,256,128]{1,2,0:T(8,128)S(1)}, u32[]{:S(2)}) copy-start(f32[1,256,128]{1,2,0:T(8,128)S(1)} %copy.267) | copy-start | bytes 393220
  155.2 7.9 copy-start.71
  155.2 8.0 copy-start.67
  163.1 20.4 %copy-start.73 = (s32[64]{0:T(128)}, s32[64]{0:T(128)S(1)}, u32[]{:S(2)}) copy-start(s32[64]{0:T(128)S(1)} %eq.15) | copy-start | bytes 772
  163.3 18.9 %copy-start.53 = (bf16[640,32]{0,1:T(8,128)(2,1)}, bf16[640,32]{0,1:T(8,128)(2,1)S(1)}, u32[]{:S(2)}) copy-start(bf16[640,32]{0,1:T(8,128)(2,1)S(1)} %reshape.365) | copy-start | bytes 122884
  174.7 3.8 copy-start.75
  182.8 59.4 %copy-start.65 = (f32[640]{0:T(1024)}, f32[640]{0:T(1024)S(1)}, u32[]{:S(2)}) copy-start(f32[640]{0:T(1024)S(1)} %broadcast_multiply_fusion.9) | copy-start | bytes 7684
  182.8 5.4 copy-start.72
  183.4 61.1 %copy-start.69 = (f32[640]{0:T(1024)}, f32[640]{0:T(1024)S(1)}, u32[]{:S(2)}) copy-start(f32[640]{0:T(1024)S(1)} %add_rsqrt_fusion.2) | copy-start | bytes 7684
  185.3 55.8 %copy-start.63 = (bf16[64,128]{1,0:T(8,128)(2,1)}, bf16[64,128]{1,0:T(8,128)(2,1)S(1)}, u32[]{:S(2)}) copy-start(bf16[64,128]{1,0:T(8,128)(2,1)S(1)} %get-tuple-element.207) | copy-start | bytes 49156
  188.0 642.8 %all-reduce.5.cloned.1.call-start = ((), (), s32[]{:S(2)}) async-start(), calls=%async_computation.2 | async-start | bytes 524288 | tf_op jit(solution)/shard_map/psum | solution.py:536
  310.2 12.4 %copy-start = (f32[640,1024]{1,0:T(8,128)}, f32[640,1024]{1,0:T(8,128)S(1)}, u32[]{:S(2)}) copy-start(f32[640,1024]{1,0:T(8,128)S(1)} %get-tuple-element.151) | copy-start | bytes 7864324
  311.4 11.2 %copy-start.38 = (bf16[640,1024]{1,0:T(8,128)(2,1)}, bf16[640,1024]{1,0:T(8,128)(2,1)S(1)}, u32[]{:S(2)}) copy-start(bf16[640,1024]{1,0:T(8,128)(2,1)S(1)} %fusion.34) | copy-start | bytes 3932164
  322.6 11.1 %copy-start.26 = (bf16[640,4,4,256]{3,0,2,1:T(8,128)(2,1)}, bf16[640,4,4,256]{3,0,2,1:T(8,128)(2,1)S(1)}, u32[]{:S(2)}) copy-start(bf16[640,4,4,256]{3,0,2,1:T(8,128)(2,1)S(1)} %get-tuple-element.214) | copy-start | bytes 15728644
  379.6 3.8 copy-start.3
  379.6 3.8 copy-start.16
  385.9 13.8 %copy-start.40 = (bf16[640,1024]{1,0:T(8,128)(2,1)}, bf16[640,1024]{1,0:T(8,128)(2,1)S(1)}, u32[]{:S(2)}) copy-start(bf16[640,1024]{1,0:T(8,128)(2,1)S(1)} %fusion.36) | copy-start | bytes 3932164
  385.9 13.7 %copy-start.1 = (f32[640,1024]{1,0:T(8,128)S(1)}, f32[640,1024]{1,0:T(8,128)}, u32[]{:S(2)}) copy-start(f32[640,1024]{1,0:T(8,128)} %copy-done) | copy-start | bytes 7864324
  399.7 10.1 %copy-start.14 = (f32[640,1024,1]{1,0,2:T(8,128)S(1)}, f32[640,1024,1]{1,0,2:T(8,128)}, u32[]{:S(2)}) copy-start(f32[640,1024,1]{1,0,2:T(8,128)} %get-tuple-element.213) | copy-start | bytes 7864324
  409.7 3.5 copy-start.15
  413.2 5.1 copy-start.8
  413.2 2.5 copy-start.17
  413.2 8.3 slice-start.3
  415.7 2.6 copy-start.23
  415.7 5.8 slice-start.4
  418.3 3.2 copy-start.39
  418.3 12.5 %slice-start.1 = ((s8[5242880]{0:T(1024)(128)(4,1)}), s8[4194304]{0:T(1024)(128)(4,1)S(1)}, s32[]{:S(2)}) async-start(s8[5242880]{0:T(1024)(128)(4,1)} %bitcast.694), calls=%async_computation.5 | async-start | bytes 8388608
  421.5 9.3 %slice-start.2 = ((s8[5242880]{0:T(1024)(128)(4,1)}), s8[1048576]{0:T(1024)(128)(4,1)S(1)}, s32[]{:S(2)}) async-start(s8[5242880]{0:T(1024)(128)(4,1)} %bitcast.694), calls=%async_computation.6 | async-start | bytes 2097152
  421.5 9.3 copy-start.41
  447.0 9.8 %copy-start.34 = (bf16[2,320,1,16,64]{1,0,4,3,2:T(2,128)(2,1)S(1)}, bf16[2,320,1,16,64]{1,0,4,3,2:T(2,128)(2,1)}, u32[]{:S(2)}) copy-start(bf16[2,320,1,16,64]{1,0,4,3,2:T(2,128)(2,1)} %get-tuple-element.160) | copy-start | bytes 3932164
  447.0 9.8 %copy-start.35 = (bf16[2,320,16,64]{1,0,3,2:T(2,128)(2,1)S(1)}, bf16[2,320,16,64]{1,0,3,2:T(2,128)(2,1)}, u32[]{:S(2)}) copy-start(bf16[2,320,16,64]{1,0,3,2:T(2,128)(2,1)} %reshape_reshape.15) | copy-start | bytes 3932164
  466.9 11.3 %copy-start.20 = (bf16[2,320,1,16,64]{1,0,4,3,2:T(2,128)(2,1)S(1)}, bf16[2,320,1,16,64]{1,0,4,3,2:T(2,128)(2,1)}, u32[]{:S(2)}) copy-start(bf16[2,320,1,16,64]{1,0,4,3,2:T(2,128)(2,1)} %get-tuple-element.159) | copy-start | bytes 3932164
  478.3 3.7 copy-start.19
  521.5 9.2 copy-start.18
  521.5 9.2 copy-start.9
  530.6 3.1 copy-start.6
  536.4 76.4 %copy-start.10 = (bf16[1,128,6,1024]{1,3,2,0:T(8,128)(2,1)S(1)}, bf16[1,128,6,1024]{1,3,2,0:T(8,128)(2,1)}, u32[]{:S(2)}) copy-start(bf16[1,128,6,1024]{1,3,2,0:T(8,128)(2,1)} %copy.203) | copy-start | bytes 4718596
  536.4 76.4 %copy-start.60 = (f32[64,128]{1,0:T(8,128)S(1)}, f32[64,128]{1,0:T(8,128)}, u32[]{:S(2)}) copy-start(f32[64,128]{1,0:T(8,128)} %get-tuple-element.208) | copy-start | bytes 98308
  609.9 11.9 %copy-start.74 = (s32[64]{0:T(128)S(1)}, s32[64]{0:T(128)}, u32[]{:S(2)}) copy-start(s32[64]{0:T(128)} %copy-done.73) | copy-start | bytes 772
  609.9 13.6 %copy-start.50 = (f32[64,128]{1,0:T(8,128)S(1)}, f32[64,128]{1,0:T(8,128)}, u32[]{:S(2)}) copy-start(f32[64,128]{1,0:T(8,128)} %copy-done.49) | copy-start | bytes 98308
  609.9 13.6 %copy-start.57 = (bf16[64,128]{1,0:T(8,128)(2,1)S(1)}, bf16[64,128]{1,0:T(8,128)(2,1)}, u32[]{:S(2)}) copy-start(bf16[64,128]{1,0:T(8,128)(2,1)} %copy-done.56) | copy-start | bytes 49156
  609.9 13.6 %copy-start.59 = (bf16[64,128]{1,0:T(8,128)(2,1)S(1)}, bf16[64,128]{1,0:T(8,128)(2,1)}, u32[]{:S(2)}) copy-start(bf16[64,128]{1,0:T(8,128)(2,1)} %copy-done.58) | copy-start | bytes 49156
  654.7 21.6 %copy-start.54 = (bf16[640,32]{0,1:T(8,128)(2,1)S(1)}, bf16[640,32]{0,1:T(8,128)(2,1)}, u32[]{:S(2)}) copy-start(bf16[640,32]{0,1:T(8,128)(2,1)} %copy-done.53) | copy-start | bytes 122884
  654.7 23.3 %copy-start.51 = (f32[1,32,1024]{2,1,0:T(8,128)S(1)}, f32[1,32,1024]{2,1,0:T(8,128)}, u32[]{:S(2)}) copy-start(f32[1,32,1024]{2,1,0:T(8,128)} %convolution_bitcast_fusion.1) | copy-start | bytes 393220
  704.6 122.3 %copy-start.64 = (bf16[64,128]{1,0:T(8,128)(2,1)S(1)}, bf16[64,128]{1,0:T(8,128)(2,1)}, u32[]{:S(2)}) copy-start(bf16[64,128]{1,0:T(8,128)(2,1)} %copy-done.63) | copy-start | bytes 49156
  826.9 2.9 copy-start.11
  829.8 47.6 %copy-start.33 = (f32[3,128,3,256]{3,1,2,0:T(8,128)S(1)}, f32[3,128,3,256]{3,1,2,0:T(8,128)}, u32[]{:S(2)}) copy-start(f32[3,128,3,256]{3,1,2,0:T(8,128)} %param.26) | copy-start | bytes 3538948
  829.8 48.8 %copy-start.44 = (f32[1,256,128]{1,2,0:T(8,128)S(1)}, f32[1,256,128]{1,2,0:T(8,128)}, u32[]{:S(2)}) copy-start(f32[1,256,128]{1,2,0:T(8,128)} %copy-done.43) | copy-start | bytes 393220
  830.8 50.5 %copy-start.46 = (f32[1,256,128]{1,2,0:T(8,128)S(1)}, f32[1,256,128]{1,2,0:T(8,128)}, u32[]{:S(2)}) copy-start(f32[1,256,128]{1,2,0:T(8,128)} %copy-done.45) | copy-start | bytes 393220
  830.8 50.5 %copy-start.47 = (f32[1,256,128]{1,2,0:T(8,128)S(1)}, f32[1,256,128]{1,2,0:T(8,128)}, u32[]{:S(2)}) copy-start(f32[1,256,128]{1,2,0:T(8,128)} %copy.274) | copy-start | bytes 393220
  878.6 8.6 slice-start
  888.3 4.2 copy-start.21
  889.6 2.9 copy-start.27
  889.7 4.1 copy-start.31
  893.7 4.7 copy-start.22
  901.2 6.2 copy-start.36
  901.2 7.2 copy-start.68
  901.2 9.1 copy-start.55
  (20 other events, 31.5 us)
Sparse Core Ops, SparseCore 0:
  22.7 33.8 reduce-scatter.1
  188.1 52.9 all-reduce.6
  678.8 125.2 all-reduce.4

commit v2 on v1

--- a/solution.py
+++ b/solution.py
@@ -60,12 +60,6 @@
     return lax.dot_general(a, b, (((0,), (0,)), ((), ())), preferred_element_type=F32)
 
 
-def norm_parts(values):
-    center = values - jnp.mean(values, axis=-1, keepdims=True)
-    inverse = lax.rsqrt(jnp.mean(center * center, axis=-1, keepdims=True) + 1e-06)
-    return center * inverse, inverse
-
-
 def norm_back(grad, normed, inverse):
     mean_grad = jnp.mean(grad, axis=-1, keepdims=True)
     mean_prod = jnp.mean(grad * normed, axis=-1, keepdims=True)
@@ -83,56 +77,8 @@
     return up * cdf, cdf + up * pdf
 
 
-def per_window(mod):
-    return mod[:, None, :]
-
-
 def tokens3(values):
     return values.reshape(NMB, WTOK, -1)
-
-
-def spread(values, mod):
-    return (tokens3(values) * mod[:, None, :]).reshape(ROWS, -1)
-
-
-def modulated(normed, shift, scale):
-    return (tokens3(normed) * (1.0 + scale[:, None, :]) + shift[:, None, :]).reshape(ROWS, -1)
-
-
-def window_sum(values):
-    return jnp.sum(tokens3(values), axis=1)
-
-
-def split_heads(qkv):
-    shaped = qkv.reshape(NMB, WTOK, 3, HEADS, HD)
-    return shaped[:, :, 0], shaped[:, :, 1], shaped[:, :, 2]
-
-
-def scores_of(query, key, flags):
-    scores = jnp.einsum("wqhe,wkhe->whqk", query, key, preferred_element_type=F32) * HD ** (-0.5)
-    return jnp.where(flags.reshape(NMB, 1, 1, WTOK) > 0, scores, -1e30)
-
-
-def attend(qkv, flags):
-    query, key, value = split_heads(qkv)
-    attn = jax.nn.softmax(scores_of(query, key, flags), axis=-1).astype(BF)
-    mixed = jnp.einsum("whqk,wkhe->wqhe", attn, value, preferred_element_type=F32)
-    return mixed.astype(BF).reshape(ROWS, D)
-
-
-def attend_back(grad_mixed, qkv, flags):
-    query, key, value = split_heads(qkv)
-    grad_heads = grad_mixed.reshape(NMB, WTOK, HEADS, HD)
-    attn_full = jax.nn.softmax(scores_of(query, key, flags), axis=-1)
-    attn = attn_full.astype(BF)
-    grad_value = jnp.einsum("whqk,wqhe->wkhe", attn, grad_heads, preferred_element_type=F32)
-    grad_attn = jnp.einsum("wqhe,wkhe->whqk", grad_heads, value, preferred_element_type=F32)
-    grad_scores = attn_full * (grad_attn - jnp.sum(attn_full * grad_attn, axis=-1, keepdims=True))
-    grad_scores = grad_scores.astype(BF)
-    grad_query = jnp.einsum("whqk,wkhe->wqhe", grad_scores, key, preferred_element_type=F32)
-    grad_key = jnp.einsum("whqk,wqhe->wkhe", grad_scores, query, preferred_element_type=F32)
-    parts = jnp.stack([grad_query * HD ** (-0.5), grad_key * HD ** (-0.5), grad_value], axis=2)
-    return parts.astype(BF).reshape(ROWS, 3, D)
 
 
 def flip(bits, at):
@@ -202,12 +148,13 @@
     def arrived(self, step, slot):
         self.started[step, slot].wait_recv()
 
-    def drain(self):
-        for copy in self.started.values():
-            copy.wait_send()
-
-
-def gather_kernel(nd, nm, shard, whole, send_sems, recv_sems, local_sems):
+    def drain(self, step=None):
+        for key in list(self.started):
+            if step is None or key[0] == step:
+                self.started.pop(key).wait_send()
+
+
+def gather_steps(nd, nm, shard, whole, send_sems, recv_sems, local_sems, load, compute, last):
     place = Place(nd, nm)
     nb, core = place.nb, place.core
     copies = Copies(send_sems, recv_sems)
@@ -253,8 +200,9 @@
     def finish(j):
         for slot in range(twin, 2 * twin + 1):
             copies.arrived(j, slot)
-
-    for turn in range(NJ + nb + 2):
+        load(j)
+
+    for turn in range(max(NJ + nb + 2, last + nb)):
         if turn < NJ:
             begin(turn)
         for step in range(nb + 1):
@@ -262,44 +210,301 @@
                 stage(turn - 1 - step, step)
         if 0 <= turn - 2 - nb < NJ:
             finish(turn - 2 - nb)
+        compute(turn + 2 - nb)
     copies.drain()
 
 
-def gather_blocks(shard):
+def row_norm(values):
+    center = values - jnp.mean(values, axis=-1, keepdims=True)
+    inverse = lax.rsqrt(jnp.mean(center * center, axis=-1, keepdims=True) + 1e-06)
+    return center * inverse, inverse
+
+
+def each(count, body):
+    lax.fori_loop(0, count, lambda at, carry: (body(at), carry)[1], 0)
+
+
+def span(at, size):
+    return pl.ds(pl.multiple_of(at * size, size), size)
+
+
+def head_lanes(head, dtype=F32):
+    lanes = lax.broadcasted_iota(jnp.int32, (1, TILE), 1) // HD
+    return (lanes == head).astype(dtype)
+
+
+def soft_rows(query, key, key_bias):
+    scores = dot_nt(query, key) * HD ** (-0.5)
+    scores = jnp.where(key_bias > 0, scores, -1e30)
+    exponents = jnp.exp(scores - jnp.max(scores, axis=-1, keepdims=True))
+    return exponents / jnp.sum(exponents, axis=-1, keepdims=True)
+
+
+BLOCK = 64
+PER_WINDOW = WTOK // BLOCK
+NBLOCK = ROWS // BLOCK
+LANE_BLOCK = 128
+
+
+def transpose_rows(source, target):
+    def body(at):
+        target[:, span(at, LANE_BLOCK)] = source[span(at, LANE_BLOCK), :].T
+
+    each(ROWS // LANE_BLOCK, body)
+
+
+FORWARD_TURNS = (
+    (5, ("qkv", 0)),
+    (6, ("qkv", 1)),
+    (7, ("qkv", 2)),
+    (7, ("attend", 0)),
+    (8, ("attend", 1)),
+    (9, ("attend", 2)),
+    (10, ("attend", 3)),
+    (10, ("out",)),
+    (11, ("up", 0)),
+    (12, ("down", 0)),
+    (12, ("up", 1)),
+    (13, ("down", 1)),
+    (13, ("up", 2)),
+    (14, ("down", 2)),
+    (15, ("up", 3)),
+    (16, ("down", 3)),
+)
+
+
+def forward_kernel(nd, nm, shard, residual, mod, flags, *refs):
+    (whole, n_one_t, qkv_out, mixed_out, branch_one_out, middle_out, n_two_t, hidden_out, slope_out, branch_two_out) = refs[:10]
+    (n_one, qkv, mixed, branch_one, middle, n_two, flipped, hidden, slope, branch_two, loaded) = refs[10:21]
+    send_sems, recv_sems, local_sems, load_sems, spill_sems = refs[21:]
+    spilled = {}
+
+    def spill(name, source, target):
+        copy = pltpu.make_async_copy(source, target, spill_sems.at[len(spilled)])
+        copy.start()
+        spilled[name] = copy
+
+    loads = {}
+    slots = loaded.shape[0]
+
+    def load(j):
+        loads[j] = pltpu.make_async_copy(whole.at[j], loaded.at[j % slots], load_sems.at[j])
+        loads[j].start()
+
+    def tile(j, m):
+        return loaded.at[j % slots, m].reshape(D, TILE)
+
+    def first_norm():
+        def body(at):
+            window, here = at // PER_WINDOW, span(at, BLOCK)
+            normed, _ = row_norm(residual[here, :])
+            normed = normed * (1.0 + mod[window, 1:2, :]) + mod[window, 0:1, :]
+            n_one[here, :] = normed.astype(BF)
+
+        each(NBLOCK, body)
+        transpose_rows(n_one, flipped.at[0])
+        spill("n_one", flipped.at[0], n_one_t)
+
+    def qkv_unit(j):
+        def body(m):
+            qkv[j, m] = dot_nn(n_one[...], tile(j, m)[...]).astype(BF)
+
+        each(nm, body)
+        spill(("qkv", j), qkv.at[j], qkv_out.at[j])
+
+    def attend_unit(m):
+        def body(window):
+            here = span(window, WTOK)
+            query, key, value = qkv[0, m, here, :], qkv[1, m, here, :], qkv[2, m, here, :]
+            total = jnp.zeros((WTOK, TILE), F32)
+            for head in range(TILE // HD):
+                lanes = head_lanes(head, BF)
+                attn = soft_rows(query * lanes, key, flags[window]).astype(BF)
+                total = total + dot_nn(attn, value * lanes)
+            mixed[m, here, :] = total.astype(BF)
+
+        each(NMB, body)
+        if m == nm - 1:
+            spill("mixed", mixed, mixed_out)
+
+    def add_nt(source, j, target, fresh):
+        def body(at):
+            columns = span(at, TILE)
+            total = dot_nt(source[0], tile(j, 0)[columns, :])
+            for m in range(1, nm):
+                total = total + dot_nt(source[m], tile(j, m)[columns, :])
+            target[:, columns] = total if fresh else target[:, columns] + total
+
+        each(D // TILE, body)
+
+    def out_unit():
+        add_nt(mixed, 3, branch_one, True)
+        spill("branch_one", branch_one, branch_one_out)
+
+        def body(at):
+            window, here = at // PER_WINDOW, span(at, BLOCK)
+            rows = residual[here, :] + mod[window, 2:3, :] * branch_one[here, :]
+            middle[here, :] = rows
+            normed, _ = row_norm(rows)
+            normed = normed * (1.0 + mod[window, 4:5, :]) + mod[window, 3:4, :]
+            n_two[here, :] = normed.astype(BF)
+
+        each(NBLOCK, body)
+        spill("middle", middle, middle_out)
+        transpose_rows(n_two, flipped.at[1])
+        spill("n_two", flipped.at[1], n_two_t)
+
+    def up_unit(f):
+        slot = f % 2
+        if f >= 2:
+            spilled["hidden", f - 2].wait()
+            spilled["slope", f - 2].wait()
+
+        def body(m):
+            up = dot_nn(n_two[...], tile(4 + 2 * f, m)[...])
+            value, grad = gelu_parts(up)
+            hidden[slot, m] = value.astype(BF)
+            slope[slot, :, span(m, TILE)] = grad
+
+        each(nm, body)
+        spill(("hidden", f), hidden.at[slot], hidden_out.at[f])
+        spill(("slope", f), slope.at[slot], slope_out.at[f])
+
+    def down_unit(f):
+        add_nt(hidden.at[f % 2], 5 + 2 * f, branch_two, f == 0)
+        if f == 3:
+            spill("branch_two", branch_two, branch_two_out)
+
+    units = {"qkv": qkv_unit, "attend": attend_unit, "out": out_unit, "up": up_unit, "down": down_unit}
+    need = {"qkv": lambda j: j, "out": lambda: 3, "up": lambda f: 4 + 2 * f, "down": lambda f: 5 + 2 * f}
+
+    def compute(turn):
+        if turn == 1:
+            first_norm()
+        for when, (name, *args) in FORWARD_TURNS:
+            if when == turn:
+                if name in need:
+                    loads[need[name](*args)].wait()
+                units[name](*args)
+
+    last = max(when for when, _ in FORWARD_TURNS)
+    gather_steps(nd, nm, shard, whole, send_sems, recv_sems, local_sems, load, compute, last)
+    for name, copy in spilled.items():
+        if name not in [(kind, f) for kind in ("hidden", "slope") for f in (0, 1)]:
+            copy.wait()
+
+
+def forward_blocks(shard, residual, mod, flags):
     nd, nm = lax.axis_size("dp"), lax.axis_size("mp")
     nb = nd.bit_length() - 2
     rows = shard.shape[1]
     slots = 2 * (nm - 1 + 2 * nb) + 1
-    whole = pl.pallas_call(
-        functools.partial(gather_kernel, nd, nm),
-        out_shape=jax.ShapeDtypeStruct((NJ, nm) + (2,) * nb + (2, rows, TILE), BF),
-        in_specs=[pl.BlockSpec(memory_space=pl.ANY)],
-        out_specs=pl.BlockSpec(memory_space=pl.ANY),
+    shapes = [
+        ((NJ, nm) + (2,) * nb + (2, rows, TILE), BF),
+        ((D, ROWS), BF),
+        ((3, nm, ROWS, TILE), BF),
+        ((nm, ROWS, TILE), BF),
+        ((ROWS, D), F32),
+        ((ROWS, D), F32),
+        ((D, ROWS), BF),
+        ((4, nm, ROWS, TILE), BF),
+        ((4, ROWS, D), F32),
+        ((ROWS, D), F32),
+    ]
+    return pl.pallas_call(
+        functools.partial(forward_kernel, nd, nm),
+        out_shape=[jax.ShapeDtypeStruct(shape, dtype) for shape, dtype in shapes],
+        in_specs=[pl.BlockSpec(memory_space=pl.ANY)] + [pl.BlockSpec(memory_space=pltpu.VMEM)] * 3,
+        out_specs=[pl.BlockSpec(memory_space=pl.ANY)] * len(shapes),
         scratch_shapes=[
+            pltpu.VMEM((ROWS, D), BF),
+            pltpu.VMEM((3, nm, ROWS, TILE), BF),
+            pltpu.VMEM((nm, ROWS, TILE), BF),
+            pltpu.VMEM((ROWS, D), F32),
+            pltpu.VMEM((ROWS, D), F32),
+            pltpu.VMEM((ROWS, D), BF),
+            pltpu.VMEM((2, D, ROWS), BF),
+            pltpu.VMEM((2, nm, ROWS, TILE), BF),
+            pltpu.VMEM((2, ROWS, D), F32),
+            pltpu.VMEM((ROWS, D), F32),
+            pltpu.VMEM((4, nm) + (2,) * nb + (2, rows, TILE), BF),
             pltpu.SemaphoreType.DMA((NJ, slots)),
             pltpu.SemaphoreType.DMA((NJ, slots)),
             pltpu.SemaphoreType.DMA((NJ,)),
+            pltpu.SemaphoreType.DMA((NJ,)),
+            pltpu.SemaphoreType.DMA((24,)),
         ],
-        compiler_params=pltpu.CompilerParams(collective_id=0, has_side_effects=True),
-    )(shard)
-    return whole.reshape(NJ, nm, nd * rows, TILE)
-
-
-def reduce_kernel(nd, nm, partial, total, mine_ref, twin_ref, stage_refs, z_ref, send_sems, recv_sems, local_sems):
+        compiler_params=pltpu.CompilerParams(
+            collective_id=0, has_side_effects=True, vmem_limit_bytes=60 << 20
+        ),
+    )(shard, residual, mod, flags)
+
+
+PIECES = (5, 4, 7, 6, 9, 8, 11, 10, 3, 2, 1, 0)
+BACKWARD_TURNS = (
+    (0, ("head",)),
+    (1, ("slope", 0)),
+    (1, ("spread", 0)),
+    (2, ("slope", 1)),
+    (2, ("spread", 1)),
+    (3, ("slope", 2)),
+    (3, ("spread", 2)),
+    (4, ("slope", 3)),
+    (4, ("spread", 3)),
+    (5, ("mid",)),
+    (6, ("attend", 0)),
+    (7, ("attend", 1)),
+    (8, ("attend", 2)),
+    (9, ("attend", 3)),
+    (10, ("inward", 2)),
+    (11, ("inward", 1)),
+    (12, ("inward", 0)),
+    (12, ("last",)),
+)
+HELD = 5
+TWINS = 4
+
+
+def backward_kernel(nd, nm, whole, n_one_t, qkv, mixed, branch_one, middle, n_two_t, hidden, slope, branch_two, residual, *refs):
+    (mod, flags, row_mask, token_total, noise, latents, head_t) = refs[:7]
+    (total, loss, ends, grad_mod) = refs[7:11]
+    (partial, twin_ref, xa, xb, grad_rows, grad_in, grad_low, grad_low_t, normed_t, pool, loaded, z_ref) = refs[11:23]
+    rest = refs[23:]
     place = Place(nd, nm)
     nb, core = place.nb, place.core
+    stage_refs = [rest[2 * step : 2 * step + 2] for step in range(nb)]
+    send_sems, recv_sems, free_sem, load_sems = rest[2 * nb :]
     copies = Copies(send_sems, recv_sems)
     orders = [order[::-1] for order in place.orders]
-    locals_ = {}
     place.greet()
     slot_of = lambda step, half: 1 + 2 * step + half
     z_slot = 1 + 2 * nb
+    loads = {}
+
+    def load(name, source, target):
+        copy = pltpu.make_async_copy(source, target, load_sems.at[len(loads)])
+        copy.start()
+        loads[name] = copy
+
+    def load_tiles(j, slot):
+        load(("w", j), whole.at[j], loaded.at[slot])
+
+    def tile(slot, m):
+        return loaded.at[slot, m].reshape(D, TILE)
+
+    HIDDEN, QUERY, MIXED_GRAD = 4, 5, 8
+
+    load("branch_two", branch_two, xb)
+    load("middle", middle, xa)
+    load(("hidden", 0), hidden.at[0], pool.at[HIDDEN])
+    load("n_two", n_two_t, normed_t)
+    load_tiles(5, 0)
+    load_tiles(4, 1)
 
     def add_to(target, index, source):
         shape = source.shape[:-2]
-        count = math.prod(shape)
-
-        def body(at, carry):
+
+        def body(at):
             inner, places = at, []
             for size in shape[::-1]:
                 places.append(inner % size)
@@ -308,110 +513,305 @@
             spot = tuple(
                 base.start + offset if isinstance(base, pl.Slice) else base
                 for base, offset in zip(index, places)
-            )
+            ) + (core,)
             target[spot] = (target[spot].astype(F32) + source[tuple(places)].astype(F32)).astype(BF)
-            return carry
-
-        lax.fori_loop(0, count, body, 0)
-
-    def begin(j):
-        every = (slice(None),) * (nb + 1)
-        locals_[j] = pltpu.make_async_copy(
-            partial.at[(j,) + every + (core,)], mine_ref.at[j], local_sems.at[j]
-        )
-        locals_[j].start()
-        copies.start(
-            j, 0, partial.at[(j,) + every + (1 - core,)], twin_ref.at[j], place.sibling
-        )
-
-    def stage(j, step):
+
+        each(math.prod(shape), body)
+
+    every = (slice(None),) * (nb + 1)
+
+    def begin(s):
+        if s >= TWINS:
+            pl.semaphore_wait(free_sem, 1)
+        source = partial.at[(s % HELD,) + every + (1 - core,)]
+        copies.start(s, 0, source, twin_ref.at[s % TWINS], place.sibling)
+
+    def stage(s, step):
+        mine = partial.at[s % HELD]
         if step == 0:
-            locals_[j].wait()
-            copies.arrived(j, 0)
-            add_to(mine_ref.at[j], (pl.ds(0, nm),) + (pl.ds(0, 2),) * nb, twin_ref.at[j])
+            copies.arrived(s, 0)
+            add_to(mine, (pl.ds(0, nm),) + (pl.ds(0, 2),) * nb, twin_ref.at[s % TWINS])
+            if s + TWINS < NJ:
+                pl.semaphore_signal(free_sem, inc=1, device_id=place.sibling, device_id_type=MESH)
         else:
             for half in range(2):
-                copies.arrived(j, slot_of(step - 1, half))
+                copies.arrived(s, slot_of(step - 1, half))
                 index = place.pick(half, orders[half][step:])
-                add_to(mine_ref.at[j], index, stage_refs[step - 1].at[j, half])
+                add_to(mine, index, stage_refs[step - 1][half].at[s])
         if step < nb:
             for half in range(2):
                 order = orders[half]
-                block = mine_ref.at[(j,) + place.pick(half, order[step + 1 :], order[step])]
-                target = stage_refs[step].at[j, half]
-                copies.start(j, slot_of(step, half), block, target, place.across(order[step]))
+                block = mine.at[place.pick(half, order[step + 1 :], order[step]) + (core,)]
+                target = stage_refs[step][half].at[s]
+                copies.start(s, slot_of(step, half), block, target, place.across(order[step]))
         else:
             for hops in range(1, nm):
-                block = mine_ref.at[(j,) + place.mine((place.m + hops) % nm)]
-                copies.start(j, z_slot + hops - 1, block, z_ref.at[j, hops - 1], place.along(hops))
-
-    def finish(j):
-        summed = mine_ref[(j,) + place.mine()].astype(F32)
+                block = mine.at[place.mine((place.m + hops) % nm) + (core,)]
+                copies.start(s, z_slot + hops - 1, block, z_ref.at[s, hops - 1], place.along(hops))
+
+    def finish(s):
+        summed = partial[(s % HELD,) + place.mine() + (core,)].astype(F32)
         for hops in range(1, nm):
-            copies.arrived(j, z_slot + hops - 1)
-            summed = summed + z_ref[j, hops - 1].astype(F32)
-        total[j] = summed
-
-    for turn in range(NJ + nb + 2):
+            copies.arrived(s, z_slot + hops - 1)
+            summed = summed + z_ref[s, hops - 1].astype(F32)
+        total[PIECES[s]] = summed
+        copies.drain(s)
+
+    def weight_grad(s):
+        j = PIECES[s]
+        if j >= 4 and j % 2 == 1:
+            f = (j - 5) // 2
+            loads["hidden", f].wait()
+            left, right = grad_low_t, HIDDEN
+        elif j >= 4:
+            left, right = normed_t, (j - 4) // 2
+        elif j == 3:
+            loads["mixed"].wait()
+            left, right = grad_low_t, HIDDEN
+        else:
+            if j == 2:
+                loads["n_one"].wait()
+            left, right = normed_t, j
+
+        def body(m):
+            grads = dot_nn(left[...], pool[right, m]).astype(BF)
+            partial.at[s % HELD, m].reshape(D, TILE)[...] = grads
+
+        each(nm, body)
+        if j in (5, 7, 9):
+            load(("hidden", f + 1), hidden.at[f + 1], pool.at[HIDDEN])
+        if j == 11:
+            load("mixed", mixed, pool.at[HIDDEN])
+        if j == 10:
+            load("n_one", n_one_t, normed_t)
+
+    def rows_of(at):
+        return at // PER_WINDOW, span(at, BLOCK)
+
+    def add_mod(window, which, values):
+        grad_mod[window, which : which + 1, :] += jnp.sum(values, axis=0, keepdims=True)
+
+    def head_unit():
+        loads["branch_two"].wait()
+        loads["middle"].wait()
+        loss[...] = jnp.zeros_like(loss)
+        ends[...] = jnp.zeros_like(ends)
+        grad_mod[...] = jnp.zeros_like(grad_mod)
+
+        def body(at):
+            window, here = rows_of(at)
+            gate = mod[window, 5:6, :]
+            branch = xb[here, :]
+            normed, inverse = row_norm(xa[here, :] + gate * branch)
+            low = normed.astype(BF)
+            error = dot_nt(low, head_t[...]) - noise[here, :]
+            mask = row_mask[here, :]
+            share = jnp.sum(error * error, axis=-1, keepdims=True) * (1.0 / PATCH) * mask
+            loss[...] += jnp.sum(share, axis=0, keepdims=True) / token_total[...]
+            grad_pred = (2.0 / PATCH * error * mask / token_total[...]).astype(BF)
+            ends[1] += dot_tn(grad_pred, low)
+            grad = norm_back(dot_nn(grad_pred, head_t[...]), normed, inverse)
+            add_mod(window, 5, grad * branch)
+            grad_rows[here, :] = grad
+            grad_low[here, :] = (grad * gate).astype(BF)
+
+        each(NBLOCK, body)
+        transpose_rows(grad_low, grad_low_t)
+        load(("slope", 0), slope.at[0], xa)
+        load(("slope", 1), slope.at[1], xb)
+
+    def slope_unit(f):
+        loads["slope", f].wait()
+        loads["w", 5 + 2 * f].wait()
+        slopes = xa if f % 2 == 0 else xb
+
+        def body(m):
+            grad = dot_nn(grad_low[...], tile(0, m)[...])
+            pool[f, m] = (grad * slopes[:, span(m, TILE)]).astype(BF)
+
+        each(nm, body)
+        if f + 2 < 4:
+            load(("slope", f + 2), slope.at[f + 2], slopes)
+        elif f == 2:
+            load("middle_again", middle, xa)
+        else:
+            load("branch_one", branch_one, xb)
+        load_tiles(7 + 2 * f if f < 3 else 3, 0)
+
+    def add_rows(right, slot, fresh):
+        def body(at):
+            columns = span(at, TILE)
+            summed = dot_nt(pool[right, 0], tile(slot, 0)[columns, :])
+            for m in range(1, nm):
+                summed = summed + dot_nt(pool[right, m], tile(slot, m)[columns, :])
+            grad_in[:, columns] = summed if fresh else grad_in[:, columns] + summed
+
+        each(D // TILE, body)
+
+    def spread_unit(f):
+        loads["w", 4 + 2 * f].wait()
+        add_rows(f, 1, f == 0)
+        load_tiles(6 + 2 * f if f < 3 else 2, 1)
+        if f == 3:
+            for part in range(3):
+                load(("qkv", part), qkv.at[part], pool.at[QUERY + part])
+
+    def norm_unit(which, after):
+        def body(at):
+            window, here = rows_of(at)
+            normed, inverse = row_norm(xa[here, :])
+            grad = grad_in[here, :]
+            add_mod(window, which, grad)
+            add_mod(window, which + 1, grad * normed)
+            grad = grad * (1.0 + mod[window, which + 1 : which + 2, :])
+            after(window, here, grad_rows[here, :] + norm_back(grad, normed, inverse))
+
+        each(NBLOCK, body)
+
+    def mid_unit():
+        loads["middle_again"].wait()
+        loads["branch_one"].wait()
+
+        def after(window, here, grad):
+            add_mod(window, 2, grad * xb[here, :])
+            grad_rows[here, :] = grad
+            grad_low[here, :] = (grad * mod[window, 2:3, :]).astype(BF)
+
+        norm_unit(3, after)
+        load("residual", residual, xa)
+        loads["w", 3].wait()
+
+        def body(m):
+            pool[MIXED_GRAD, m] = dot_nn(grad_low[...], tile(0, m)[...]).astype(BF)
+
+        each(nm, body)
+        load_tiles(1, 0)
+
+    def attend_unit(m):
+        if m == 0:
+            for part in range(3):
+                loads["qkv", part].wait()
+
+        def body(window):
+            here = span(window, WTOK)
+            query, key, value = (pool[QUERY + part, m, here, :] for part in range(3))
+            grad_mixed = pool[MIXED_GRAD, m, here, :]
+            grads = [jnp.zeros((WTOK, TILE), F32) for _ in range(3)]
+            for head in range(TILE // HD):
+                lanes = head_lanes(head, BF)
+                own_query, own_grad = query * lanes, grad_mixed * lanes
+                attn = soft_rows(own_query, key, flags[window])
+                grads[2] = grads[2] + dot_tn(attn.astype(BF), own_grad)
+                grad_attn = dot_nt(own_grad, value)
+                inner = jnp.sum(attn * grad_attn, axis=-1, keepdims=True)
+                grad_scores = (attn * (grad_attn - inner)).astype(BF)
+                grads[0] = grads[0] + dot_nn(grad_scores, key * lanes)
+                grads[1] = grads[1] + dot_tn(grad_scores, own_query)
+            pool[0, m, here, :] = (grads[0] * HD ** (-0.5)).astype(BF)
+            pool[1, m, here, :] = (grads[1] * HD ** (-0.5)).astype(BF)
+            pool[2, m, here, :] = grads[2].astype(BF)
+
+        each(NMB, body)
+
+    def inward_unit(j):
+        slot = 1 if j != 1 else 0
+        loads["w", j].wait()
+        add_rows(j, slot, j == 2)
+        if j == 2:
+            load_tiles(0, 1)
+
+    def last_unit():
+        loads["residual"].wait()
+
+        def after(window, here, grad):
+            ends[0] += dot_tn(latents[here, :], grad.astype(BF))
+
+        norm_unit(0, after)
+
+    units = {
+        "head": head_unit,
+        "slope": slope_unit,
+        "spread": spread_unit,
+        "mid": mid_unit,
+        "attend": attend_unit,
+        "inward": inward_unit,
+        "last": last_unit,
+    }
+
+    def compute(turn):
+        for when, (name, *args) in BACKWARD_TURNS:
+            if when == turn:
+                units[name](*args)
+
+    last = max(when for when, _ in BACKWARD_TURNS)
+    for turn in range(max(NJ + nb + 2, last + 1)):
+        if turn == 0:
+            compute(turn)
+        if 0 < turn <= last and turn in (1, 5, 9):
+            compute(turn)
+        if turn == 8:
+            transpose_rows(grad_low, grad_low_t)
         if turn < NJ:
+            if turn == 1:
+                loads["n_two"].wait()
+            weight_grad(turn)
             begin(turn)
         for step in range(nb + 1):
             if 0 <= turn - 1 - step < NJ:
                 stage(turn - 1 - step, step)
         if 0 <= turn - 2 - nb < NJ:
             finish(turn - 2 - nb)
-    copies.drain()
-
-
-def reduce_blocks(partial):
+        if turn not in (0, 1, 5, 9):
+            compute(turn)
+
+
+def backward_blocks(saved, residual, mod, flags, row_mask, token_total, noise, latents, head_t):
     nd, nm = lax.axis_size("dp"), lax.axis_size("mp")
     nb = nd.bit_length() - 2
-    rows = partial.shape[2] // nd
+    rows = D // nd
     bits = (2,) * nb
     slots = 2 * nb + nm
-
-    def kernel(partial, total, mine_ref, twin_ref, *rest):
-        stage_refs = [HalfRefs(rest[2 * step], rest[2 * step + 1]) for step in range(nb)]
-        reduce_kernel(nd, nm, partial, total, mine_ref, twin_ref, stage_refs, *rest[2 * nb :])
-
     stage_shapes = []
     for step in range(nb):
-        low_first = tuple(1 if at <= step else 2 for at in range(nb))
-        high_first = tuple(1 if nb - 1 - at <= step else 2 for at in range(nb))
-        stage_shapes.append(pltpu.VMEM((NJ, nm // 2) + low_first + (rows, TILE), BF))
-        stage_shapes.append(pltpu.VMEM((NJ, nm - nm // 2) + high_first + (rows, TILE), BF))
-    total = pl.pallas_call(
-        kernel,
-        out_shape=jax.ShapeDtypeStruct((NJ, rows, TILE), F32),
-        in_specs=[pl.BlockSpec(memory_space=pl.ANY)],
-        out_specs=pl.BlockSpec(memory_space=pltpu.VMEM),
+        high_first = tuple(1 if at <= step else 2 for at in range(nb))
+        stage_shapes.append(pltpu.VMEM((NJ, nm // 2) + high_first + (rows, TILE), BF))
+        stage_shapes.append(pltpu.VMEM((NJ, nm - nm // 2) + high_first[::-1] + (rows, TILE), BF))
+    in_hbm = (*saved, residual)
+    in_vmem = (mod, flags, row_mask, token_total, noise, latents, head_t)
+    return pl.pallas_call(
+        functools.partial(backward_kernel, nd, nm),
+        out_shape=[
+            jax.ShapeDtypeStruct((NJ, rows, TILE), F32),
+            jax.ShapeDtypeStruct((1, 1), F32),
+            jax.ShapeDtypeStruct((2, PATCH, D), F32),
+            jax.ShapeDtypeStruct((NMB, 6, D), F32),
+        ],
+        in_specs=[pl.BlockSpec(memory_space=pl.ANY)] * len(in_hbm)
+        + [pl.BlockSpec(memory_space=pltpu.VMEM)] * len(in_vmem),
+        out_specs=[pl.BlockSpec(memory_space=pltpu.VMEM)] * 4,
         scratch_shapes=[
-            pltpu.VMEM((NJ, nm) + bits + (rows, TILE), BF),
-            pltpu.VMEM((NJ, nm) + bits + (rows, TILE), BF),
+            pltpu.VMEM((HELD, nm) + bits + (2, rows, TILE), BF),
+            pltpu.VMEM((TWINS, nm) + bits + (rows, TILE), BF),
+            pltpu.VMEM((ROWS, D), F32),
+            pltpu.VMEM((ROWS, D), F32),
+            pltpu.VMEM((ROWS, D), F32),
+            pltpu.VMEM((ROWS, D), F32),
+            pltpu.VMEM((ROWS, D), BF),
+            pltpu.VMEM((D, ROWS), BF),
+            pltpu.VMEM((D, ROWS), BF),
+            pltpu.VMEM((9, nm, ROWS, TILE), BF),
+            pltpu.VMEM((2, nm) + bits + (2, rows, TILE), BF),
+            pltpu.VMEM((NJ, nm - 1, rows, TILE), BF),
             *stage_shapes,
-            pltpu.VMEM((NJ, nm - 1, rows, TILE), BF),
             pltpu.SemaphoreType.DMA((NJ, slots)),
             pltpu.SemaphoreType.DMA((NJ, slots)),
-            pltpu.SemaphoreType.DMA((NJ,)),
+            pltpu.SemaphoreType.REGULAR,
+            pltpu.SemaphoreType.DMA((36,)),
         ],
         compiler_params=pltpu.CompilerParams(
-            collective_id=1, has_side_effects=True, vmem_limit_bytes=60 << 20
+            collective_id=1, has_side_effects=True, vmem_limit_bytes=61 << 20
         ),
-    )(partial.reshape((NJ, nm) + bits + (2, rows, TILE)))
-    return total
-
-
-class HalfRefs:
-    def __init__(self, first, second):
-        self.refs = (first, second)
-
-    @property
-    def at(self):
-        return self
-
-    def __getitem__(self, index):
-        j, half = index
-        return self.refs[half].at[j]
+    )(*in_hbm, *in_vmem)
 
 
 def adam_update(state_in, gradient, factor):
@@ -455,7 +855,6 @@
     shard = jnp.concatenate(
         [attn_in_tiles, state_attention_out[0].T[None], ff_tiles], axis=0
     ).astype(BF)
-    weights = gather_blocks(shard)
 
     mask = token_mask.astype(F32).reshape(ROWS)
     token_total = lax.psum(jnp.sum(mask), ("dp", "mp"))
@@ -485,57 +884,22 @@
     noise_rows = noise_target.reshape(ROWS, PATCH)
     positions = window_positions(jnp.arange(WTOK, dtype=jnp.int32))
     residual = (tokens3(dot_nn(latent_rows, embed_mat)) + positions[None]).reshape(ROWS, D)
-    ln_one, inv_one = norm_parts(residual)
-    n_one = modulated(ln_one, mod[:, 0], mod[:, 1]).astype(BF)
-    qkv = jnp.einsum("tk,jmkc->tjmc", n_one, weights[:3], preferred_element_type=F32).astype(BF)
-    qkv = qkv.reshape(ROWS, 3, D)
-    mixed = attend(qkv, mask)
-    mixed_tiles = mixed.reshape(ROWS, nm, TILE)
-    branch_one = jnp.einsum("tmc,mnc->tn", mixed_tiles, weights[3], preferred_element_type=F32)
-    middle = residual + spread(branch_one, mod[:, 2])
-    ln_two, inv_two = norm_parts(middle)
-    n_two = modulated(ln_two, mod[:, 3], mod[:, 4]).astype(BF)
-    up = jnp.einsum("tk,fmkc->tfmc", n_two, weights[4::2], preferred_element_type=F32)
-    hidden, slope = gelu_parts(up)
-    hidden = hidden.astype(BF)
-    branch_two = jnp.einsum("tfmc,fmnc->tn", hidden, weights[5::2], preferred_element_type=F32)
-    final = middle + spread(branch_two, mod[:, 5])
-    ln_out, inv_out = norm_parts(final)
-    ln_low = ln_out.astype(BF)
-    prediction = dot_nt(ln_low, head_t)
-    error = prediction - noise_rows
-    loss_local = jnp.sum(jnp.mean(error * error, axis=-1) * mask) / token_total
-
-    grad_pred = (2.0 / PATCH * error * mask[:, None] / token_total).astype(BF)
-    head_grad = dot_tn(grad_pred, ln_low)
-    grad_final = norm_back(dot_nn(grad_pred, head_t), ln_out, inv_out)
-    gate_two = window_sum(grad_final * branch_two)
-    g_two = spread(grad_final, mod[:, 5]).astype(BF)
-    contract_grad = jnp.einsum("tn,tfmc->fmnc", g_two, hidden, preferred_element_type=F32)
-    grad_hidden = jnp.einsum("tn,fmnc->tfmc", g_two, weights[5::2], preferred_element_type=F32)
-    grad_up = (grad_hidden * slope).astype(BF)
-    expand_grad = jnp.einsum("tk,tfmc->fmkc", n_two, grad_up, preferred_element_type=F32)
-    grad_n_two = jnp.einsum("tfmc,fmkc->tk", grad_up, weights[4::2], preferred_element_type=F32)
-    shift_two, scale_two = window_sum(grad_n_two), window_sum(grad_n_two * ln_two)
-    grad_middle = grad_final + norm_back(spread(grad_n_two, 1.0 + mod[:, 4]), ln_two, inv_two)
-    gate_one = window_sum(grad_middle * branch_one)
-    g_one = spread(grad_middle, mod[:, 2]).astype(BF)
-    out_grad = jnp.einsum("tn,tmc->mnc", g_one, mixed_tiles, preferred_element_type=F32)
-    grad_mixed = jnp.einsum("tn,mnc->tmc", g_one, weights[3], preferred_element_type=F32)
-    grad_qkv = attend_back(grad_mixed.astype(BF).reshape(ROWS, D), qkv, mask)
-    grad_qkv = grad_qkv.reshape(ROWS, 3, nm, TILE)
-    in_grad = jnp.einsum("tk,tjmc->jmkc", n_one, grad_qkv, preferred_element_type=F32)
-    grad_n_one = jnp.einsum("tjmc,jmkc->tk", grad_qkv, weights[:3], preferred_element_type=F32)
-    shift_one, scale_one = window_sum(grad_n_one), window_sum(grad_n_one * ln_one)
-    grad_embedded = grad_middle + norm_back(spread(grad_n_one, 1.0 + mod[:, 1]), ln_one, inv_one)
-    embed_grad = dot_tn(latent_rows, grad_embedded.astype(BF))
-    ff_grad = jnp.stack([expand_grad, contract_grad], axis=1).reshape(8, nm, D, TILE)
-    partial = jnp.concatenate([in_grad, out_grad[None], ff_grad], axis=0).astype(BF)
-    reduced = reduce_blocks(partial)
-
-    ends_grad = lax.psum(jnp.stack([embed_grad, head_grad]), ("dp", "mp"))
+    flags = token_mask.reshape(NMB, 1, WTOK)
+    saved = forward_blocks(shard, residual, mod, flags)
+    reduced, loss_local, ends_grad, grad_mod = backward_blocks(
+        saved,
+        residual,
+        mod,
+        flags,
+        mask[:, None],
+        token_total.reshape(1, 1),
+        noise_rows,
+        latent_rows,
+        head_t,
+    )
+    loss_local = loss_local[0, 0]
+    ends_grad = lax.psum(ends_grad, ("dp", "mp"))
     ends_grad = lax.dynamic_slice_in_dim(ends_grad, dp_id * rows, rows, 2)
-    grad_mod = jnp.stack([shift_one, scale_one, gate_one, shift_two, scale_two, gate_two], axis=1)
     grad_mod = grad_mod.astype(BF).reshape(NMB, 6 * D)
     grad_mod = lax.all_gather(grad_mod, ("dp", "mp"), axis=0, tiled=False)
     grad_mod = grad_mod.reshape(nd, nm, NMB, 6 * D).transpose(0, 2, 1, 3)

time: 939 us -> 779 us (0.83)
  matrix products: 172 us -> 15.1 us
  waiting for transfers between devices: 52.9 us -> 170 us
  local copies, waits for them, and re-layouts: 146 us -> 42.6 us
  other arithmetic: 107 us -> 55.8 us
  Pallas kernels: 247 us -> 286 us
    dot_general x17 -> x0, matrix products: 137 us -> none  [the longest x1 13.7 us: per_device(): jnp.einsum('tn,fmnc->tfmc', g_two, weights[5::2], preferred_element_type=...]
    psum x1, waiting for transfers between devices: 0.01 us -> 117 us  [per_device(): ends_grad = lax.psum(ends_grad, ('dp', 'mp'))]
    another operation x9 -> x2, local copies, waits for them, and re-layouts: 55.4 us -> 1 us  [the longest x1 0.97 us: per_device(): mask[:, None]]
    pallas_call x2, Pallas kernels: 247 us -> 286 us  [the longest x1 154 us: backward_blocks(): pl.pallas_call(functools.partial(backward_kernel, nd, nm), out_shape=[jax...]
    transpose x4 -> x0, local copies, waits for them, and re-layouts: 17.1 us -> none  [the longest x1 8.81 us: per_device(): jnp.einsum('tk,tjmc->jmkc', n_one, grad_qkv, preferred_element_type=F32)]
    slice x3 -> x0, local copies, waits for them, and re-layouts: 17.1 us -> none  [the longest x1 7.58 us: split_heads(): return (shaped[:, :, 0], shaped[:, :, 1], shaped[:, :, 2])]
    concatenate x1 -> x0, other arithmetic: 17.1 us -> none  [per_device(): jnp.concatenate([in_grad, out_grad[None], ff_grad], axis=0).astype(BF)]
    another operation x3 -> x1, other arithmetic: 14.7 us -> 0.2 us  [the longest x1 13.8 us: per_device(): jnp.stack([expand_grad, contract_grad], axis=1).reshape(8, nm, D, TILE)]
  transfers between devices with their start and end apart: 3 -> 3, of which waited for: 1 -> 2; matrix products, arithmetic and copies ran while one was open for 6% -> 5% of each run, Pallas kernels for 27% -> 0%
where the time goes in v2:
time: 779 us; the launch traced here: 771 us
  Pallas kernels  286 us (37%)
  blocking collectives  180 us (23%)
  waiting for transfers between devices  170 us (22%)
  other arithmetic  55.8 us (7%)
  local copies, waits for them, and re-layouts  42.6 us (5%)
  between operations  21.5 us (3%)
  matrix products  15.1 us (2%)
    pallas_call x1, Pallas kernels, backward_blocks(): pl.pallas_call(functools.partial(backward_kernel, nd, nm), out_shape=[jax...  154 us
    pallas_call x1, Pallas kernels, forward_blocks(): pl.pallas_call(functools.partial(forward_kernel, nd, nm), out_shape=[jax....  133 us
    psum x1, waiting for transfers between devices, per_device(): ends_grad = lax.psum(ends_grad, ('dp', 'mp'))  117 us
    all_gather x1, blocking collectives, per_device(): grad_mod = lax.all_gather(grad_mod, ('dp', 'mp'), axis=0, tiled=False)  71.7 us
    unnamed x4, waiting for transfers between devices  52.7 us
    psum x1, blocking collectives, per_device(): token_total = lax.psum(jnp.sum(mask), ('dp', 'mp'))  39.8 us
    psum x1, blocking collectives, per_device(): lax.psum((loss_local, square_local), ('dp', 'mp'))  39.7 us
    another operation x15, other arithmetic, adam_update(): return (new_weight, jnp.stack([first_moment, root_moment]))  31.2 us
  transfers between devices with their start and end apart: 3, of which 2 were waited for; matrix products, arithmetic and copies ran while one was open for 5% of the time, Pallas kernels for 0%

profile of v2, /device:TPU:0, one launch (start us, length us, event | category | flops | bytes accessed | tf_op | source)
XLA Modules:
  0.0 771.3 jit_solution(11108202431919247730)
XLA Ops:
  7.2 1.1 fusion.109
  9.2 10.3 %all_gather.13 = s32[2,8,2,4]{3,2,1,0:T(2,128)S(1)} all-gather(s32[2,1,2,4]{3,2,1,0:T(2,128)S(1)} %pad_add_fusion), channel_id=1, replica_groups=mesh['dp'=8,'mp'=4] {'dp'}, dimensions={1}, use_global_device_ids=true | all-gather | bytes 576 | tf_op jit(solution)/shard_map/all_gather | solution.py:865
  20.0 2.0 fusion.59
  22.0 1.3 reshape.208.flags.refs_1_
  24.0 1.3 convert_reduce_fusion
  25.9 3.3 slice.335
  29.2 1.9 copy.89
  31.2 1.3 fusion.96
  32.5 1.3 slice.338
  34.2 1.1 slice.337
  36.2 1.1 slice.336
  37.3 0.9 copy.84
  38.2 1.0 broadcast_in_dim_reshape.4.refs_2_
  39.1 0.9 copy.90
  40.0 39.8 %psum.28.refs_3_ = f32[1,1]{1,0:T(1,128)} all-reduce(f32[1,1]{1,0:T(1,128)} %bitcast.26), channel_id=1, replica_groups=mesh['dp'=8,'mp'=4] {'dp','mp'}, use_global_device_ids=true, to_apply=%region_3.4 | all-reduce | flops 1 | bytes 8 | tf_op jit(solution)/shard_map/psum | solution.py:860
  84.1 2.3 multiply_sine_fusion
  88.1 10.2 %all_gather.12 = bf16[2,32,1024]{2,1,0:T(8,128)(2,1)S(1)} all-gather(bf16[2,32,128]{2,1,0:T(8,128)(2,1)S(1)} %pad_maximum_fusion.16), channel_id=1, replica_groups=mesh['dp'=8,'mp'=4] {'dp'}, dimensions={2}, use_global_device_ids=true | all-gather | bytes 147456 | tf_op jit(solution)/shard_map/all_gather | solution.py:862
  98.3 2.0 bitcast_add_fusion.1.residual
  100.3 1.0 fusion.47
  101.3 0.9 pad_maximum_fusion.5.shard
  102.2 1.2 multiply_convert_fusion
  103.5 1.3 fusion.98
  105.5 52.7 %all-reduce.7.cloned.1.call-done = f32[16,6144]{1,0:T(8,128)} async-done(((f32[16,6144]{1,0:T(8,128)}), f32[16,6144]{1,0:T(8,128)}) %all-reduce.7.cloned.1.call-update) | async-done | bytes 393232
  158.1 0.9 constant_dynamic-slice_fusion.1
  159.7 132.6 %shard_map.318 = (bf16[12,4,2,2,2,128,256]{6,5,4,3,2,1,0:T(8,128)(2,1)}, bf16[1024,640]{1,0:T(8,128)(2,1)}, bf16[3,4,640,256]{3,2,1,0:T(8,128)(2,1)}, bf16[4,640...) custom-call(bf16[12,128,256]{2,1,0:T(8,128)(2,1)} %pad_maximum_fusio, ...), custom_call_target="tpu_custom_call" | custom-call | tf_op jit(solution)/shard_map/pallas_call | solution.py:414
  292.4 153.8 %shard_map.319 = (f32[12,128,256]{2,1,0:T(8,128)}, f32[1,1]{1,0:T(1,128)}, f32[2,32,1024]{2,1,0:T(8,128)}, f32[2,6,1024]{2,1,0:T(8,128)}) custom-call(bf16[12,4,2,2,2,128,256]{6,5,4,3,2,1,0:T(8,128)(2,1)} %get-tuple-element.36.whole, bf16[1024,640]{1,0:T(8,128)(2,1)} %get-tuple-element.37.n_one_t, bf16[3,4,640,256]{3,2,1,0:T(8,128)(2,1)} %get-tuple-element.38.qkv, ...), custom_call_target="tpu_custom_call" | custom-call | tf_op jit(solution)/shard_map/pallas_call | solution.py:781
  446.2 0.8 convert_element_type.69
  447.1 71.7 %all_gather.14 = bf16[32,2,6144]{2,1,0:T(2,128)(2,1)S(1)} all-gather(bf16[1,2,6144]{2,1,0:T(2,128)(2,1)S(1)} %all_gather_reshape.3), channel_id=1, replica_groups=mesh['dp'=8,'mp'=4] {'dp','mp'}, dimensions={0}, use_global_device_ids=true | all-gather | bytes 811008 | tf_op jit(solution)/shard_map/all_gather | solution.py:904
  518.8 1.3 copy.127
  520.1 1.6 reshape.212
  522.1 8.3 %all_gather.15 = bf16[64,1024]{1,0:T(8,128)(2,1)S(1)} all-gather(bf16[64,128]{1,0:T(8,128)(2,1)S(1)} %fusion.4), channel_id=1, replica_groups=mesh['dp'=8,'mp'=4] {'dp'}, dimensions={1}, use_global_device_ids=true | all-gather | bytes 147456 | tf_op jit(solution)/shard_map/all_gather | solution.py:910
  530.4 1.7 multiply_reduce_fusion.2
  532.1 2.0 multiply_reduce_fusion.4
  534.1 1.7 multiply_reduce_fusion.3
  535.8 2.7 multiply_reduce_fusion
  538.6 2.3 slice.190
  541.6 2.4 multiply_reduce_fusion.1
  544.0 117.0 %all-reduce.5.cloned.1.call-done = f32[2,32,1024]{2,1,0:T(8,128)} async-done(((f32[2,32,1024]{2,1,0:T(8,128)}), f32[2,32,1024]{2,1,0:T(8,128)}) %all-reduce.5.cloned.1.call-update) | async-done | bytes 262160 | tf_op jit(solution)/shard_map/psum | solution.py:901
  661.0 1.3 multiply_reduce_fusion.5
  666.9 39.7 %all-reduce.1 = (f32[]{:T(128)}, f32[]{:T(128)}) all-reduce(f32[]{:T(128)} %bitcast.29, f32[]{:T(128)S(6)} %add.237), channel_id=1, replica_groups=mesh['dp'=8,'mp'=4] {'dp','mp'}, use_global_device_ids=true, to_apply=%region_4.5 | all-reduce | flops 2 | bytes 16 | tf_op jit(solution)/shard_map/psum | solution.py:925
  707.3 2.6 fusion.66
  710.0 1.2 fusion.29
  711.2 2.0 copy.101
  713.3 2.9 bitcast_subtract_fusion.1
  716.2 2.3 fusion.30
  718.5 1.8 fusion.67
  721.0 1.8 copy.106
  722.8 7.1 fusion.10
  729.9 1.1 fusion.65
  731.0 1.1 copy.99
  732.1 2.1 mul.806
  734.2 2.4 multiply_add_fusion
  736.6 2.5 fusion.58
  739.2 1.2 bitcast_subtract_fusion.2
  741.1 2.1 copy.104
  743.2 1.7 copy.103
  744.9 1.7 copy.105
  746.5 2.2 pad_maximum_fusion.4
  748.8 1.9 pad_maximum_fusion.6
  750.8 5.6 pad_maximum_fusion
  756.4 0.9 pad_maximum_fusion.7
  757.2 1.4 fusion.100
  760.6 1.5 pad_maximum_fusion.2
  762.0 1.3 fusion.82
  (130 shorter events, 15.4 us)
Async XLA Ops:
  7.2 95.1 %reduce-scatter.2.cloned.1.call-start = ((), (), s32[]{:S(2)}) async-start(), calls=%async_computation.1 | async-start | bytes 294912 | tf_op jit(solution)/shard_map/reduce_scatter | solution.py:872
  8.4 22.7 %copy-start.18 = (f32[1,256,128]{1,2,0:T(8,128)}, f32[1,256,128]{1,2,0:T(8,128)S(1)}, u32[]{:S(2)}) copy-start(f32[1,256,128]{1,2,0:T(8,128)S(1)} %copy.109) | copy-start | bytes 393220
  19.8 11.4 %copy-start.33 = (bf16[64,128]{1,0:T(8,128)(2,1)}, bf16[64,128]{1,0:T(8,128)(2,1)S(1)}, u32[]{:S(2)}) copy-start(bf16[64,128]{1,0:T(8,128)(2,1)S(1)} %get-tuple-element.160) | copy-start | bytes 49156
  19.8 11.4 %copy-start.35 = (bf16[64,128]{1,0:T(8,128)(2,1)}, bf16[64,128]{1,0:T(8,128)(2,1)S(1)}, u32[]{:S(2)}) copy-start(bf16[64,128]{1,0:T(8,128)(2,1)S(1)} %get-tuple-element.161) | copy-start | bytes 49156
  21.9 136.2 %all-reduce.7.cloned.1.call-start = ((), (), s32[]{:S(2)}) async-start(), calls=%async_computation.3 | async-start | bytes 786432
  25.9 8.0 %copy-start.39 = (bf16[1,2,320,32]{2,3,1,0:T(8,128)(2,1)S(1)}, bf16[1,2,320,32]{2,3,1,0:T(8,128)(2,1)}, u32[]{:S(2)}) copy-start(bf16[1,2,320,32]{2,3,1,0:T(8,128)(2,1)} %param.15) | copy-start | bytes 122884
  25.9 8.1 %copy-start.31 = (f32[3,256,128]{2,1,0:T(8,128)S(1)}, f32[3,256,128]{2,1,0:T(8,128)}, u32[]{:S(2)}) copy-start(f32[3,256,128]{2,1,0:T(8,128)} %param.27) | copy-start | bytes 1179652
  29.2 9.9 %copy-start.37 = (f32[1,2,320,32]{2,3,1,0:T(8,128)S(1)}, f32[1,2,320,32]{2,3,1,0:T(8,128)}, u32[]{:S(2)}) copy-start(f32[1,2,320,32]{2,3,1,0:T(8,128)} %param.16) | copy-start | bytes 245764
  31.2 51.6 %copy-start.42 = (u32[32]{0:T(128)S(1)}, u32[32]{0:T(128)}, u32[]{:S(2)}) copy-start(u32[32]{0:T(128)} %constant.60) | copy-start | bytes 388
  34.0 64.3 %copy-start.14 = (bf16[1,2,320,32]{3,2,1,0:T(8,128)(2,1)}, bf16[1,2,320,32]{3,2,1,0:T(8,128)(2,1)S(1)}, u32[]{:S(2)}) copy-start(bf16[1,2,320,32]{3,2,1,0:T(8,128)(2,1)S(1)} %copy.85) | copy-start | bytes 122884
  34.2 52.4 %copy-start.20 = (f32[1,256,128]{1,2,0:T(8,128)}, f32[1,256,128]{1,2,0:T(8,128)S(1)}, u32[]{:S(2)}) copy-start(f32[1,256,128]{1,2,0:T(8,128)S(1)} %copy.108) | copy-start | bytes 393220
  38.2 49.1 %copy-start.22 = (bf16[128,4,256]{2,0,1:T(8,128)(2,1)S(1)}, bf16[128,4,256]{2,0,1:T(8,128)(2,1)}, u32[]{:S(2)}) copy-start(bf16[128,4,256]{2,0,1:T(8,128)(2,1)} %copy.128) | copy-start | bytes 786436
  84.1 3.2 copy-start.23
  88.1 14.1 %copy-start.40 = (s32[64]{0:T(128)S(1)}, s32[64]{0:T(128)}, u32[]{:S(2)}) copy-start(s32[64]{0:T(128)} %eq.15) | copy-start | bytes 772
  88.1 13.2 %copy-start.6 = (bf16[4,2,128,256]{3,2,1,0:T(8,128)(2,1)S(1)}, bf16[4,2,128,256]{3,2,1,0:T(8,128)(2,1)}, u32[]{:S(2)}) copy-start(bf16[4,2,128,256]{3,2,1,0:T(8,128)(2,1)} %pad_maximum_fusion.8) | copy-start | bytes 1572868
  104.8 556.2 %all-reduce.5.cloned.1.call-start = ((), (), s32[]{:S(2)}) async-start(), calls=%async_computation.2 | async-start | bytes 524288 | tf_op jit(solution)/shard_map/psum | solution.py:901
  518.8 13.3 %copy-start.34 = (bf16[64,128]{1,0:T(8,128)(2,1)S(1)}, bf16[64,128]{1,0:T(8,128)(2,1)}, u32[]{:S(2)}) copy-start(bf16[64,128]{1,0:T(8,128)(2,1)} %copy-done.33) | copy-start | bytes 49156
  518.8 13.3 %copy-start.36 = (bf16[64,128]{1,0:T(8,128)(2,1)S(1)}, bf16[64,128]{1,0:T(8,128)(2,1)}, u32[]{:S(2)}) copy-start(bf16[64,128]{1,0:T(8,128)(2,1)} %copy-done.35) | copy-start | bytes 49156
  520.1 14.0 %copy-start.41 = (s32[64]{0:T(128)S(1)}, s32[64]{0:T(128)}, u32[]{:S(2)}) copy-start(s32[64]{0:T(128)} %eq.15) | copy-start | bytes 772
  521.7 14.1 %copy-start.1 = (bf16[64,6144]{1,0:T(8,128)(2,1)}, bf16[64,6144]{1,0:T(8,128)(2,1)S(1)}, u32[]{:S(2)}) copy-start(bf16[64,6144]{1,0:T(8,128)(2,1)S(1)} %reshape.212) | copy-start | bytes 2359300
  707.3 2.7 copy-start.5
  713.2 2.9 copy-start.2
  713.2 5.2 copy-start.19
  713.2 5.2 copy-start.21
  713.2 5.2 copy-start.24
  713.2 5.2 copy-start.25
  713.2 5.2 copy-start.26
  713.3 5.2 copy-start.27
  713.3 5.2 copy-start.28
  722.8 7.1 copy-start.13
  722.8 7.1 copy-start.15
  722.8 8.2 %copy-start.8 = (f32[128,4,256]{2,0,1:T(8,128)S(1)}, f32[128,4,256]{2,0,1:T(8,128)}, u32[]{:S(2)}) copy-start(f32[128,4,256]{2,0,1:T(8,128)} %get-tuple-element.141) | copy-start | bytes 1572868
  729.9 4.4 copy-start.3
  729.9 6.7 copy-start.4
  734.2 4.9 copy-start.7
  736.6 3.8 copy-start.29
  736.6 3.8 copy-start.30
  740.4 10.3 %copy-start = (f32[1,128,6,1024]{3,1,2,0:T(8,128)S(1)}, f32[1,128,6,1024]{3,1,2,0:T(8,128)}, u32[]{:S(2)}) copy-start(f32[1,128,6,1024]{3,1,2,0:T(8,128)} %get-tuple-element.120) | copy-start | bytes 9437188
  750.7 5.7 copy-start.16
  750.7 5.7 copy-start.17
  750.7 6.5 copy-start.38
  750.7 8.5 %copy-start.32 = (f32[3,32,128]{2,1,0:T(8,128)S(1)}, f32[3,32,128]{2,1,0:T(8,128)}, u32[]{:S(2)}) copy-start(f32[3,32,128]{2,1,0:T(8,128)} %param.20) | copy-start | bytes 147460
  750.7 9.8 %copy-start.9 = (f32[1,128,1024]{2,1,0:T(8,128)S(1)}, f32[1,128,1024]{2,1,0:T(8,128)}, u32[]{:S(2)}) copy-start(f32[1,128,1024]{2,1,0:T(8,128)} %get-tuple-element.128) | copy-start | bytes 1572868
  750.7 9.8 %copy-start.10 = (f32[1,128,1024]{2,1,0:T(8,128)S(1)}, f32[1,128,1024]{2,1,0:T(8,128)}, u32[]{:S(2)}) copy-start(f32[1,128,1024]{2,1,0:T(8,128)} %get-tuple-element.129) | copy-start | bytes 1572868
  750.7 9.8 %copy-start.11 = (f32[1,128,1024]{2,1,0:T(8,128)S(1)}, f32[1,128,1024]{2,1,0:T(8,128)}, u32[]{:S(2)}) copy-start(f32[1,128,1024]{2,1,0:T(8,128)} %get-tuple-element.130) | copy-start | bytes 1572868
  750.8 9.8 %copy-start.12 = (f32[1,128,1024]{2,1,0:T(8,128)S(1)}, f32[1,128,1024]{2,1,0:T(8,128)}, u32[]{:S(2)}) copy-start(f32[1,128,1024]{2,1,0:T(8,128)} %get-tuple-element.131) | copy-start | bytes 1572868
Sparse Core Ops, SparseCore 0:
  22.1 33.9 reduce-scatter.1
  104.9 53.1 all-reduce.6
  538.7 122.2 all-reduce.4

commit v3 on v2

--- a/solution.py
+++ b/solution.py
@@ -48,22 +48,30 @@
     return jnp.concatenate([jnp.sin(angles), jnp.cos(angles)], axis=-1)
 
 
+def dot_general(a, b, a_dim, b_dim):
+    return lax.dot_general(a, b, (((a_dim,), (b_dim,)), ((), ())), preferred_element_type=F32)
+
+
 def dot_nn(a, b):
     return jnp.dot(a, b, preferred_element_type=F32)
 
 
 def dot_nt(a, b):
-    return lax.dot_general(a, b, (((1,), (1,)), ((), ())), preferred_element_type=F32)
+    return dot_general(a, b, 1, 1)
 
 
 def dot_tn(a, b):
-    return lax.dot_general(a, b, (((0,), (0,)), ((), ())), preferred_element_type=F32)
+    return dot_general(a, b, 0, 0)
 
 
 def norm_back(grad, normed, inverse):
     mean_grad = jnp.mean(grad, axis=-1, keepdims=True)
     mean_prod = jnp.mean(grad * normed, axis=-1, keepdims=True)
     return inverse * (grad - mean_grad - normed * mean_prod)
+
+
+def silu(values):
+    return values * jax.nn.sigmoid(values)
 
 
 def silu_slope(values):
@@ -90,6 +98,8 @@
         self.nm = nm
         self.nb = nd.bit_length() - 2
         dp_id = lax.axis_index("dp")
+        self.nd = nd
+        self.dp_id = dp_id
         self.m = lax.axis_index("mp")
         self.core = dp_id % 2
         self.bits = [dp_id // (1 << (self.nb - at)) % 2 for at in range(self.nb)]
@@ -109,6 +119,9 @@
     def along(self, hops):
         return {"dp": self.dp_of(self.bits, self.core), "mp": (self.m + hops) % self.nm}
 
+    def beside(self, hops):
+        return {"dp": (self.dp_id + hops) % self.nd, "mp": self.m}
+
     def pick(self, half, done, flipped=None):
         where = flip(self.bits, flipped)
         return (self.halves[half],) + tuple(
@@ -118,10 +131,12 @@
     def mine(self, m=None):
         return (self.m if m is None else m,) + tuple(self.bits)
 
-    def greet(self):
+    def greet(self, everyone=False):
         barrier = pltpu.get_barrier_semaphore()
-        others = [self.sibling]
-        others += [self.across(at) for at in range(self.nb)]
+        if everyone:
+            others = [self.beside(hops) for hops in range(1, self.nd)]
+        else:
+            others = [self.sibling] + [self.across(at) for at in range(self.nb)]
         others += [self.along(hops) for hops in range(1, self.nm)]
         for other in others:
             pl.semaphore_signal(barrier, inc=1, device_id=other, device_id_type=MESH)
@@ -154,15 +169,41 @@
                 self.started.pop(key).wait_send()
 
 
-def gather_steps(nd, nm, shard, whole, send_sems, recv_sems, local_sems, load, compute, last):
-    place = Place(nd, nm)
-    nb, core = place.nb, place.core
+class Exchange:
+    def __init__(self, place, send_sems, recv_sems):
+        self.place = place
+        self.copies = Copies(send_sems, recv_sems)
+
+    def dp_gather(self, group, source, target):
+        for hops in range(1, self.place.nd):
+            here = target.at[self.place.dp_id]
+            self.copies.start(group, hops - 1, source, here, self.place.beside(hops))
+
+    def dp_scatter(self, group, source, target):
+        for hops in range(1, self.place.nd):
+            block = source.at[(self.place.dp_id + hops) % self.place.nd]
+            self.copies.start(group, hops - 1, block, target.at[hops - 1], self.place.beside(hops))
+
+    def mp_gather(self, group, source, target):
+        for hops in range(1, self.place.nm):
+            here = target.at[self.place.m]
+            self.copies.start(group, hops - 1, source, here, self.place.along(hops))
+
+    def wait(self, group):
+        for step, slot in list(self.copies.started):
+            if step == group:
+                self.copies.arrived(step, slot)
+
+    def drain(self):
+        self.copies.drain()
+
+
+def gather_steps(place, shard, whole, send_sems, recv_sems, local_sems, load, compute, last):
+    nm, nb, core = place.nm, place.nb, place.core
     copies = Copies(send_sems, recv_sems)
-    z_slots = [hops - 1 for hops in range(1, nm)]
     stage_slot = lambda stage, half: nm - 1 + 2 * stage + half
     twin = nm - 1 + 2 * nb
     locals_ = {}
-    place.greet()
 
     def begin(j):
         here = whole.at[(j,) + place.mine() + (core,)]
@@ -240,6 +281,13 @@
     return exponents / jnp.sum(exponents, axis=-1, keepdims=True)
 
 
+def label_pick(front, count):
+    labels = front[:, :, FREQ : FREQ + 1].reshape(-1, 1)
+    lanes = lax.broadcasted_iota(jnp.int32, (labels.shape[0], count), 1).astype(F32)
+    return (lanes == labels).astype(BF)
+
+
+PER_INDEX = NMB * WMB
 BLOCK = 64
 PER_WINDOW = WTOK // BLOCK
 NBLOCK = ROWS // BLOCK
@@ -273,7 +321,17 @@
 )
 
 
-def forward_kernel(nd, nm, shard, residual, mod, flags, *refs):
+def forward_kernel(nd, nm, shard, flags, front_in, ends_in, latents, positions, time_in, time_out, classes, adaptive, *refs):
+    (residual_out, mod, ends, front, time_pre, condition, token_total) = refs[:7]
+    refs = refs[7:]
+    (residual, parts, parts_in, mods, mods_in, rows_ref, counts, swap_send, swap_recv) = refs[-9:]
+    refs = refs[:-9]
+    place = Place(nd, nm)
+    swap = Exchange(place, swap_send, swap_recv)
+    place.greet(everyone=True)
+    dp_id = place.dp_id
+    windows = nd * PER_INDEX
+    upright = parts.shape[1] == windows
     (whole, n_one_t, qkv_out, mixed_out, branch_one_out, middle_out, n_two_t, hidden_out, slope_out, branch_two_out) = refs[:10]
     (n_one, qkv, mixed, branch_one, middle, n_two, flipped, hidden, slope, branch_two, loaded) = refs[10:21]
     send_sems, recv_sems, local_sems, load_sems, spill_sems = refs[21:]
@@ -293,6 +351,64 @@
 
     def tile(j, m):
         return loaded.at[j % slots, m].reshape(D, TILE)
+
+    def first_swap():
+        front[dp_id] = front_in[...]
+        for which in range(2):
+            ends[which, dp_id] = ends_in[which]
+        swap.dp_gather(0, front_in, front)
+        swap.dp_gather(1, ends_in.at[0], ends.at[0])
+        swap.dp_gather(2, ends_in.at[1], ends.at[1])
+
+    def time_layers():
+        swap.wait(0)
+        features = front[:, :, :FREQ].reshape(windows, FREQ).astype(BF)
+        time_pre[...] = dot_nn(features, time_in[...])
+        time_hidden = silu(time_pre[...]).astype(BF)
+        for index in range(nd):
+            if upright:
+                parts[index] = dot_nn(time_hidden, time_out[index])
+            else:
+                parts[index] = dot_general(time_out[index], time_hidden, 0, 1)
+        swap.dp_scatter(3, parts, parts_in)
+        counts[place.m] = jnp.sum(front[:, :, FREQ + 128 :], axis=0)
+        swap.mp_gather(5, counts.at[place.m], counts)
+
+    def condition_layers():
+        swap.wait(3)
+        total = parts[dp_id] + jnp.sum(parts_in[...], axis=0)
+        total = total if upright else total.T
+        total = total + dot_nn(label_pick(front, classes.shape[0]), classes[...])
+        condition[...] = total
+        row_ids = lax.broadcasted_iota(jnp.int32, (nd * NMB, windows), 0)
+        column_ids = lax.broadcasted_iota(jnp.int32, (nd * NMB, windows), 1)
+        wanted = row_ids // NMB * PER_INDEX + place.m * NMB + row_ids % NMB
+        own = dot_nn((wanted == column_ids).astype(BF), silu(total).astype(BF)).astype(BF)
+        for which in range(6):
+            rows_ref[...] = dot_nn(own, adaptive[which])
+
+            def move(row):
+                mods[row // NMB, row % NMB, which : which + 1, :] = rows_ref[pl.ds(row, 1), :]
+
+            each(nd * NMB, move)
+        swap.dp_scatter(4, mods, mods_in)
+
+    def modulation():
+        swap.wait(4)
+        for window in range(NMB):
+            mod[window] = mods[dp_id, window] + jnp.sum(mods_in[:, window], axis=0)
+        swap.wait(5)
+        token_total[...] = jnp.sum(counts[...], axis=0)
+        swap.wait(1)
+        swap.wait(2)
+        embed_mat = ends[0].reshape(D, PATCH)
+
+        def body(window):
+            here = span(window, WTOK)
+            residual[here, :] = dot_nt(latents[here, :], embed_mat) + positions[...]
+
+        each(NMB, body)
+        spill("residual", residual, residual_out)
 
     def first_norm():
         def body(at):
@@ -379,8 +495,9 @@
     need = {"qkv": lambda j: j, "out": lambda: 3, "up": lambda f: 4 + 2 * f, "down": lambda f: 5 + 2 * f}
 
     def compute(turn):
-        if turn == 1:
-            first_norm()
+        early = (first_swap, time_layers, condition_layers, modulation, first_norm)
+        if turn < len(early):
+            early[turn]()
         for when, (name, *args) in FORWARD_TURNS:
             if when == turn:
                 if name in need:
@@ -388,17 +505,28 @@
                 units[name](*args)
 
     last = max(when for when, _ in FORWARD_TURNS)
-    gather_steps(nd, nm, shard, whole, send_sems, recv_sems, local_sems, load, compute, last)
+    gather_steps(place, shard, whole, send_sems, recv_sems, local_sems, load, compute, last)
     for name, copy in spilled.items():
         if name not in [(kind, f) for kind in ("hidden", "slope") for f in (0, 1)]:
             copy.wait()
-
-
-def forward_blocks(shard, residual, mod, flags):
+    swap.drain()
+
+
+def forward_blocks(shard, *others):
     nd, nm = lax.axis_size("dp"), lax.axis_size("mp")
     nb = nd.bit_length() - 2
     rows = shard.shape[1]
     slots = 2 * (nm - 1 + 2 * nb) + 1
+    windows = nd * PER_INDEX
+    tall = windows <= rows
+    small = [
+        ((NMB, 6, D), F32),
+        ((2, nd, rows, PATCH), BF),
+        ((nd, PER_INDEX, FREQ + 256), F32),
+        ((windows, rows), F32),
+        ((windows, rows), F32),
+        ((PER_INDEX, 128), F32),
+    ]
     shapes = [
         ((NJ, nm) + (2,) * nb + (2, rows, TILE), BF),
         ((D, ROWS), BF),
@@ -413,9 +541,14 @@
     ]
     return pl.pallas_call(
         functools.partial(forward_kernel, nd, nm),
-        out_shape=[jax.ShapeDtypeStruct(shape, dtype) for shape, dtype in shapes],
-        in_specs=[pl.BlockSpec(memory_space=pl.ANY)] + [pl.BlockSpec(memory_space=pltpu.VMEM)] * 3,
-        out_specs=[pl.BlockSpec(memory_space=pl.ANY)] * len(shapes),
+        out_shape=[
+            jax.ShapeDtypeStruct(shape, dtype) for shape, dtype in [((ROWS, D), F32)] + small + shapes
+        ],
+        in_specs=[pl.BlockSpec(memory_space=pl.ANY)]
+        + [pl.BlockSpec(memory_space=pltpu.VMEM)] * len(others),
+        out_specs=[pl.BlockSpec(memory_space=pl.ANY)]
+        + [pl.BlockSpec(memory_space=pltpu.VMEM)] * len(small)
+        + [pl.BlockSpec(memory_space=pl.ANY)] * len(shapes),
         scratch_shapes=[
             pltpu.VMEM((ROWS, D), BF),
             pltpu.VMEM((3, nm, ROWS, TILE), BF),
@@ -433,11 +566,20 @@
             pltpu.SemaphoreType.DMA((NJ,)),
             pltpu.SemaphoreType.DMA((NJ,)),
             pltpu.SemaphoreType.DMA((24,)),
+            pltpu.VMEM((ROWS, D), F32),
+            pltpu.VMEM((nd, windows if tall else rows, rows if tall else windows), F32),
+            pltpu.VMEM((nd - 1, windows if tall else rows, rows if tall else windows), F32),
+            pltpu.VMEM((nd, NMB, 6, D), F32),
+            pltpu.VMEM((nd - 1, NMB, 6, D), F32),
+            pltpu.VMEM((nd * NMB, D), F32),
+            pltpu.VMEM((nm, PER_INDEX, 128), F32),
+            pltpu.SemaphoreType.DMA((6, max(nd, nm) - 1)),
+            pltpu.SemaphoreType.DMA((6, max(nd, nm) - 1)),
         ],
         compiler_params=pltpu.CompilerParams(
             collective_id=0, has_side_effects=True, vmem_limit_bytes=60 << 20
         ),
-    )(shard, residual, mod, flags)
+    )(shard, *others)
 
 
 PIECES = (5, 4, 7, 6, 9, 8, 11, 10, 3, 2, 1, 0)
@@ -466,7 +608,9 @@
 
 
 def backward_kernel(nd, nm, whole, n_one_t, qkv, mixed, branch_one, middle, n_two_t, hidden, slope, branch_two, residual, *refs):
-    (mod, flags, row_mask, token_total, noise, latents, head_t) = refs[:7]
+    (mod, flags, row_mask, token_total_in, noise, latents, both_ends) = refs[:7]
+    token_total = token_total_in[0:1, 0:1]
+    head_mat = both_ends[1].reshape(D, PATCH)
     (total, loss, ends, grad_mod) = refs[7:11]
     (partial, twin_ref, xa, xb, grad_rows, grad_in, grad_low, grad_low_t, normed_t, pool, loaded, z_ref) = refs[11:23]
     rest = refs[23:]
@@ -604,13 +748,13 @@
             branch = xb[here, :]
             normed, inverse = row_norm(xa[here, :] + gate * branch)
             low = normed.astype(BF)
-            error = dot_nt(low, head_t[...]) - noise[here, :]
+            error = dot_nn(low, head_mat) - noise[here, :]
             mask = row_mask[here, :]
             share = jnp.sum(error * error, axis=-1, keepdims=True) * (1.0 / PATCH) * mask
-            loss[...] += jnp.sum(share, axis=0, keepdims=True) / token_total[...]
-            grad_pred = (2.0 / PATCH * error * mask / token_total[...]).astype(BF)
-            ends[1] += dot_tn(grad_pred, low)
-            grad = norm_back(dot_nn(grad_pred, head_t[...]), normed, inverse)
+            loss[...] += jnp.sum(share, axis=0, keepdims=True) / token_total
+            grad_pred = (2.0 / PATCH * error * mask / token_total).astype(BF)
+            ends[:, PATCH:] += dot_tn(low, grad_pred)
+            grad = norm_back(dot_nt(grad_pred, head_mat), normed, inverse)
             add_mod(window, 5, grad * branch)
             grad_rows[here, :] = grad
             grad_low[here, :] = (grad * gate).astype(BF)
@@ -724,7 +868,7 @@
         loads["residual"].wait()
 
         def after(window, here, grad):
-            ends[0] += dot_tn(latents[here, :], grad.astype(BF))
+            ends[:, :PATCH] += dot_tn(grad.astype(BF), latents[here, :])
 
         norm_unit(0, after)
 
@@ -765,7 +909,7 @@
             compute(turn)
 
 
-def backward_blocks(saved, residual, mod, flags, row_mask, token_total, noise, latents, head_t):
+def backward_blocks(saved, residual, mod, flags, row_mask, token_total, noise, latents, ends):
     nd, nm = lax.axis_size("dp"), lax.axis_size("mp")
     nb = nd.bit_length() - 2
     rows = D // nd
@@ -777,13 +921,13 @@
         stage_shapes.append(pltpu.VMEM((NJ, nm // 2) + high_first + (rows, TILE), BF))
         stage_shapes.append(pltpu.VMEM((NJ, nm - nm // 2) + high_first[::-1] + (rows, TILE), BF))
     in_hbm = (*saved, residual)
-    in_vmem = (mod, flags, row_mask, token_total, noise, latents, head_t)
+    in_vmem = (mod, flags, row_mask, token_total, noise, latents, ends)
     return pl.pallas_call(
         functools.partial(backward_kernel, nd, nm),
         out_shape=[
             jax.ShapeDtypeStruct((NJ, rows, TILE), F32),
             jax.ShapeDtypeStruct((1, 1), F32),
-            jax.ShapeDtypeStruct((2, PATCH, D), F32),
+            jax.ShapeDtypeStruct((D, 2 * PATCH), F32),
             jax.ShapeDtypeStruct((NMB, 6, D), F32),
         ],
         in_specs=[pl.BlockSpec(memory_space=pl.ANY)] * len(in_hbm)
@@ -814,6 +958,127 @@
     )(*in_hbm, *in_vmem)
 
 
+def tail_kernel(nd, nm, reduced, loss, ends, grad_mod, front, time_pre, condition, time_in, time_out, classes, adaptive, *refs):
+    (ends_sum, adaptive_grad, time_in_grad, time_out_grad, classes_grad, sums) = refs[:6]
+    (ends_in, ends_rows, mod_rows, mod_in, own_mod, all_mod, act_rows, cond_all, terms, term_rows, send_sems, recv_sems) = refs[6:]
+    place = Place(nd, nm)
+    swap = Exchange(place, send_sems, recv_sems)
+    dp_id, m = place.dp_id, place.m
+    windows, rows = time_pre.shape
+    place.greet(everyone=True)
+    mod_in[m] = grad_mod[...]
+    swap.mp_gather(0, grad_mod, mod_in)
+    swap.dp_scatter(1, ends, ends_in)
+
+    swap.wait(0)
+    for index in range(nm):
+        for step in range(NMB):
+            for which in range(6):
+                row = index * NMB + step
+                mod_rows[which, row : row + 1, :] = mod_in[index, step, which : which + 1, :]
+    for pair in range(3):
+        own_mod[pair] = mod_rows[2 * pair : 2 * pair + 2].reshape(2 * PER_INDEX, D).astype(BF)
+        all_mod[dp_id, pair] = own_mod[pair]
+    swap.dp_gather(2, own_mod, all_mod)
+    swap.wait(1)
+    ends_rows[m] = ends[dp_id] + jnp.sum(ends_in[...], axis=0)
+    swap.mp_gather(3, ends_rows.at[m], ends_rows)
+    cond_act = silu(condition[...]).reshape(nd, PER_INDEX, rows)
+    act_rows[...] = jnp.zeros_like(act_rows)
+    for side in range(2):
+        act_rows[side, :, side * PER_INDEX : (side + 1) * PER_INDEX, :] = cond_act
+    features = front[:, :, :FREQ].reshape(windows, FREQ).astype(BF)
+    time_hidden = silu(time_pre[...]).astype(BF)
+    pick = label_pick(front, classes.shape[0])
+    squares = jnp.zeros((8, 128), F32)
+    whole_squares = jnp.zeros((8, 128), F32)
+
+    def square_sum(values):
+        return jnp.sum(jnp.sum(values * values, axis=0, keepdims=True), axis=1, keepdims=True)
+
+    for j in range(NJ):
+        whole_squares = whole_squares + square_sum(reduced[j])
+    swap.wait(2)
+    grad_cond = jnp.zeros((windows, rows), F32)
+    for which in range(6):
+        pair, side = which // 2, which % 2
+        block = all_mod[:, pair].reshape(nd * 2 * PER_INDEX, D)
+        act = act_rows[side].reshape(nd * 2 * PER_INDEX, rows).astype(BF)
+        gradient = dot_tn(act, block)
+        adaptive_grad[which] = gradient
+        squares = squares + square_sum(gradient)
+        back = dot_nt(block, adaptive[which]).reshape(nd, 2, PER_INDEX, rows)
+        grad_cond = grad_cond + back[:, side].reshape(windows, rows)
+    grad_cond = (grad_cond * silu_slope(condition[...])).astype(BF)
+    cond_all[dp_id] = grad_cond
+    swap.dp_gather(4, cond_all.at[dp_id], cond_all)
+    gradient = dot_tn(pick, grad_cond)
+    classes_grad[...] = gradient
+    squares = squares + square_sum(gradient)
+    swap.wait(3)
+    ends_sum[...] = jnp.sum(ends_rows[...], axis=0)
+    squares = squares + square_sum(ends_sum[...])
+    swap.wait(4)
+    grad_time = jnp.zeros((windows, rows), F32)
+    for index in range(nd):
+        gradient = dot_tn(time_hidden, cond_all[index])
+        time_out_grad[index] = gradient
+        squares = squares + square_sum(gradient)
+        grad_time = grad_time + dot_nt(cond_all[index], time_out[index])
+    grad_time = (grad_time * silu_slope(time_pre[...])).astype(BF)
+    gradient = dot_tn(features, grad_time)
+    time_in_grad[...] = gradient
+    squares = squares + square_sum(gradient)
+
+    terms[dp_id, 0] = squares * (1.0 / nm) + whole_squares
+    terms[dp_id, 1] = jnp.zeros((8, 128), F32) + loss[...]
+    swap.dp_gather(5, terms.at[dp_id], terms)
+    swap.wait(5)
+    term_rows[m] = jnp.sum(terms[...], axis=0)
+    swap.mp_gather(6, term_rows.at[m], term_rows)
+    swap.wait(6)
+    sums[...] = jnp.sum(term_rows[...], axis=0)
+    swap.drain()
+
+
+def tail_blocks(*operands):
+    nd, nm = lax.axis_size("dp"), lax.axis_size("mp")
+    rows = D // nd
+    windows = nd * PER_INDEX
+    classes = operands[-2].shape[0]
+    shapes = [
+        (rows, 2 * PATCH),
+        (6, rows, D),
+        (FREQ, rows),
+        (nd, rows, rows),
+        (classes, rows),
+        (2, 8, 128),
+    ]
+    return pl.pallas_call(
+        functools.partial(tail_kernel, nd, nm),
+        out_shape=[jax.ShapeDtypeStruct(shape, F32) for shape in shapes],
+        in_specs=[pl.BlockSpec(memory_space=pltpu.VMEM)] * len(operands),
+        out_specs=[pl.BlockSpec(memory_space=pltpu.VMEM)] * len(shapes),
+        scratch_shapes=[
+            pltpu.VMEM((nd - 1, rows, 2 * PATCH), F32),
+            pltpu.VMEM((nm, rows, 2 * PATCH), F32),
+            pltpu.VMEM((6, PER_INDEX, D), F32),
+            pltpu.VMEM((nm, NMB, 6, D), F32),
+            pltpu.VMEM((3, 2 * PER_INDEX, D), BF),
+            pltpu.VMEM((nd, 3, 2 * PER_INDEX, D), BF),
+            pltpu.VMEM((2, nd, 2 * PER_INDEX, rows), F32),
+            pltpu.VMEM((nd, windows, rows), BF),
+            pltpu.VMEM((nd, 2, 8, 128), F32),
+            pltpu.VMEM((nm, 2, 8, 128), F32),
+            pltpu.SemaphoreType.DMA((7, max(nd, nm) - 1)),
+            pltpu.SemaphoreType.DMA((7, max(nd, nm) - 1)),
+        ],
+        compiler_params=pltpu.CompilerParams(
+            collective_id=2, has_side_effects=True, vmem_limit_bytes=40 << 20
+        ),
+    )(*operands)
+
+
 def adam_update(state_in, gradient, factor):
     clipped = gradient * factor
     first_moment = beta_one * state_in[1] + (1.0 - beta_one) * clipped
@@ -845,8 +1110,7 @@
     state_expand,
     state_contract,
 ):
-    nd, nm = lax.axis_size("dp"), lax.axis_size("mp")
-    dp_id, mp_id = lax.axis_index("dp"), lax.axis_index("mp")
+    nd = lax.axis_size("dp")
     rows = state_attention_in.shape[1]
     attn_in_tiles = state_attention_in[0].transpose(1, 0, 2)
     expand_tiles = state_expand[0].reshape(rows, 4, TILE).transpose(1, 0, 2)
@@ -857,72 +1121,53 @@
     ).astype(BF)
 
     mask = token_mask.astype(F32).reshape(ROWS)
-    token_total = lax.psum(jnp.sum(mask), ("dp", "mp"))
-    ends = jnp.stack([state_embed[0], state_head[0].T]).astype(BF)
-    ends = lax.all_gather(ends, "dp", axis=2, tiled=True)
-    embed_mat, head_t = ends[0], ends[1]
-
-    both_ids = lax.all_gather(jnp.stack([timesteps, labels])[:, 0], "dp", axis=1, tiled=False)
-    both_ids = both_ids.reshape(2, nd * NMB * WMB)
-    features = timestep_features(both_ids[0]).astype(BF)
-    pick = (both_ids[1][:, None] == jnp.arange(CLASSES)[None, :]).astype(BF)
-    time_pre = dot_nn(features, state_time_in[0].astype(BF))
-    time_hidden = jax.nn.silu(time_pre).astype(BF)
-    time_out_part = state_time_out[0].astype(BF)
-    condition = lax.psum_scatter(
-        dot_nn(time_hidden, time_out_part), "dp", scatter_dimension=1, tiled=True
-    ) + dot_nn(pick, state_classes[0].astype(BF))
-    cond_act = jax.nn.silu(condition).astype(BF)
-    adaptive_part = state_adaptive[0].astype(BF).reshape(rows, 6 * D)
-    mine = lax.dynamic_index_in_dim(
-        cond_act.reshape(nd * NMB, WMB, rows), mp_id, 1, keepdims=False
+    ends_shard = jnp.stack([state_embed[0].T, state_head[0]]).astype(BF)
+    step_ids = timesteps[0].T.reshape(PER_INDEX)
+    label_ids = labels[0].T.reshape(PER_INDEX, 1).astype(F32)
+    features = timestep_features(step_ids).astype(BF).astype(F32)
+    front = jnp.concatenate(
+        [
+            features,
+            jnp.broadcast_to(label_ids, (PER_INDEX, 128)),
+            jnp.broadcast_to(jnp.sum(mask), (PER_INDEX, 128)),
+        ],
+        axis=1,
     )
-    mod = lax.psum_scatter(dot_nn(mine, adaptive_part), "dp", scatter_dimension=0, tiled=True)
-    mod = mod.reshape(NMB, 6, D)
-
+    time_in_part = state_time_in[0].astype(BF)
+    time_out_part = state_time_out[0].astype(BF).reshape(rows, nd, rows).transpose(1, 0, 2)
+    class_pad = -CLASSES % 128
+    classes_part = jnp.pad(state_classes[0].astype(BF), ((0, class_pad), (0, 0)))
+    adaptive_part = state_adaptive[0].astype(BF).transpose(1, 0, 2)
+    weights = (time_in_part, time_out_part, classes_part, adaptive_part)
     latent_rows = latents.reshape(ROWS, PATCH)
     noise_rows = noise_target.reshape(ROWS, PATCH)
     positions = window_positions(jnp.arange(WTOK, dtype=jnp.int32))
-    residual = (tokens3(dot_nn(latent_rows, embed_mat)) + positions[None]).reshape(ROWS, D)
     flags = token_mask.reshape(NMB, 1, WTOK)
-    saved = forward_blocks(shard, residual, mod, flags)
+    residual, mod, ends, front_all, time_pre, condition, token_total, *saved = forward_blocks(
+        shard, flags, front, ends_shard, latent_rows, positions, *weights
+    )
     reduced, loss_local, ends_grad, grad_mod = backward_blocks(
-        saved,
-        residual,
-        mod,
-        flags,
-        mask[:, None],
-        token_total.reshape(1, 1),
-        noise_rows,
-        latent_rows,
-        head_t,
+        saved, residual, mod, flags, mask[:, None], token_total, noise_rows, latent_rows, ends
     )
-    loss_local = loss_local[0, 0]
-    ends_grad = lax.psum(ends_grad, ("dp", "mp"))
-    ends_grad = lax.dynamic_slice_in_dim(ends_grad, dp_id * rows, rows, 2)
-    grad_mod = grad_mod.astype(BF).reshape(NMB, 6 * D)
-    grad_mod = lax.all_gather(grad_mod, ("dp", "mp"), axis=0, tiled=False)
-    grad_mod = grad_mod.reshape(nd, nm, NMB, 6 * D).transpose(0, 2, 1, 3)
-    grad_mod = grad_mod.reshape(nd * NMB * WMB, 6 * D)
-    adaptive_grad = dot_tn(cond_act, grad_mod).reshape(rows, 6, D)
-    grad_cond = (dot_nt(grad_mod, adaptive_part) * silu_slope(condition)).astype(BF)
-    classes_grad = dot_tn(pick, grad_cond)
-    grad_cond_all = lax.all_gather(grad_cond, "dp", axis=1, tiled=True)
-    time_out_grad = dot_tn(time_hidden, grad_cond_all)
-    grad_time = (dot_nt(grad_cond_all, time_out_part) * silu_slope(time_pre)).astype(BF)
-    time_in_grad = dot_tn(features, grad_time)
-
+    ends_sum, adaptive_grad, time_in_grad, time_out_grad, classes_grad, sums = tail_blocks(
+        reduced,
+        loss_local,
+        ends_grad.reshape(nd, rows, 2 * PATCH),
+        grad_mod,
+        front_all,
+        time_pre,
+        condition,
+        *weights,
+    )
     small_grads = (
-        ends_grad[0],
-        ends_grad[1].T,
+        ends_sum[:, :PATCH].T,
+        ends_sum[:, PATCH:],
         time_in_grad,
-        time_out_grad,
-        classes_grad,
-        adaptive_grad,
+        time_out_grad.transpose(1, 0, 2).reshape(rows, D),
+        classes_grad[:CLASSES],
+        adaptive_grad.transpose(1, 0, 2),
     )
-    square_small = sum(jnp.sum(gradient * gradient) for gradient in small_grads)
-    square_local = jnp.sum(reduced * reduced) + square_small / nm
-    loss_value, square_total = lax.psum((loss_local, square_local), ("dp", "mp"))
+    square_total, loss_value = sums[0, 0, 0], sums[1, 0, 0]
     grad_norm = jnp.sqrt(square_total)
     factor = jnp.minimum(1.0, threshold / grad_norm)
     ff_reduced = reduced[4:].reshape(4, 2, rows, TILE)

time: 779 us -> 420 us (0.54)
  blocking collectives: 180 us -> 0 us
  waiting for transfers between devices: 170 us -> 0 us
  Pallas kernels: 286 us -> 332 us
  other arithmetic: 55.8 us -> 35.7 us
  between operations: 21.5 us -> 3.39 us
  matrix products: 15.1 us -> 0 us
    psum x1 -> x0, waiting for transfers between devices: 117 us -> none  [per_device(): ends_grad = lax.psum(ends_grad, ('dp', 'mp'))]
    all_gather x4 -> x0, blocking collectives: 100 us -> none  [the longest x1 71.7 us: per_device(): grad_mod = lax.all_gather(grad_mod, ('dp', 'mp'), axis=0, tiled=False)]
    psum x2 -> x0, blocking collectives: 79.5 us -> none  [the longest x1 39.8 us: per_device(): token_total = lax.psum(jnp.sum(mask), ('dp', 'mp'))]
    unnamed x4 -> x0, waiting for transfers between devices: 52.7 us -> none
    pallas_call x0 -> x1, Pallas kernels: none -> 32.6 us  [tail_blocks(): pl.pallas_call(functools.partial(tail_kernel, nd, nm), out_shape=[jax.Sha...]
    dot_general x10 -> x0, matrix products: 15.1 us -> none  [the longest x4 8.14 us: dot_tn(): lax.dot_general(a, b, (((0,), (0,)), ((), ())), preferred_element_type=F32)]
    pallas_call x1, Pallas kernels: 133 us -> 144 us  [forward_blocks(): pl.pallas_call(functools.partial(forward_kernel, nd, nm), out_shape=[jax....]
    another operation x15 -> x16, other arithmetic: 31.2 us -> 21.6 us  [adam_update(): return (new_weight, jnp.stack([first_moment, root_moment]))]
  transfers between devices with their start and end apart: 3 -> 0, of which waited for: 2 -> 0; matrix products, arithmetic and copies ran while one was open for 5% -> 0% of each run, Pallas kernels for 0% -> 0%
where the time goes in v3:
time: 420 us; the launch traced here: 415 us
  Pallas kernels  332 us (79%)
  local copies, waits for them, and re-layouts  43.4 us (10%)
  other arithmetic  35.7 us (9%)
    pallas_call x1, Pallas kernels, backward_blocks(): pl.pallas_call(functools.partial(backward_kernel, nd, nm), out_shape=[jax...  156 us
    pallas_call x1, Pallas kernels, forward_blocks(): pl.pallas_call(functools.partial(forward_kernel, nd, nm), out_shape=[jax....  144 us
    pallas_call x1, Pallas kernels, tail_blocks(): pl.pallas_call(functools.partial(tail_kernel, nd, nm), out_shape=[jax.Sha...  32.6 us
    another operation x16, other arithmetic, adam_update(): return (new_weight, jnp.stack([first_moment, root_moment]))  21.6 us
    unnamed x106, local copies, waits for them, and re-layouts  18.3 us

profile of v3, /device:TPU:0, one launch (start us, length us, event | category | flops | bytes accessed | tf_op | source)
XLA Modules:
  0.0 414.9 jit_solution(17024639031275021264)
XLA Ops:
  0.7 1.5 fusion.89
  2.3 1.4 fusion.90
  3.8 0.6 pad_maximum_fusion.11.ends_in
  4.4 2.5 fusion.88
  7.1 0.9 copy.146
  8.0 1.1 fusion.87
  9.5 1.1 slice.341
  10.8 1.0 fusion.51
  11.9 0.9 fusion.66
  12.9 0.9 pad_maximum_fusion.5.shard
  13.8 2.4 multiply_sine_fusion
  16.2 1.2 pad_maximum_fusion.1.positions
  18.0 0.6 convert_reduce_fusion
  18.6 0.6 broadcast_in_dim.18
  19.3 0.6 maximum_maximum_fusion.front_in
  19.9 3.3 fusion.5.adaptive
  23.2 1.0 bitcast_convert_fusion.2
  24.2 0.7 pad.4.classes
  24.9 0.8 copy.144
  25.7 1.5 bitcast_convert_fusion.3.time_in
  27.2 0.6 reshape.215.flags.refs_1_
  27.8 143.8 %shard_map.318 = (f32[640,1024]{1,0:T(8,128)}, f32[2,6,1024]{2,1,0:T(8,128)}, bf16[2,8,128,32]{3,2,1,0:T(8,128)(2,1)}, f32[8,8,512]{2,1,0:T(8,128)}, f32[64,128]...) custom-call(bf16[12,128,256]{2,1,0:T(8,128)(2,1)} %pad_maximum_fusio, ...), custom_call_target="tpu_custom_call" | custom-call | tf_op jit(solution)/shard_map/pallas_call | solution.py:542
  171.6 1.0 broadcast_in_dim_reshape.4.refs_2_
  172.6 0.9 copy.147
  173.5 156.0 %shard_map.319 = (f32[12,128,256]{2,1,0:T(8,128)}, f32[1,1]{1,0:T(1,128)}, f32[1024,64]{1,0:T(8,128)}, f32[2,6,1024]{2,1,0:T(8,128)}) custom-call(bf16[12,4,2,2,2,128,256]{6,5,4,3,2,1,0:T(8,128)(2,1)} %get-tuple-element.49.whole, bf16[1024,640]{1,0:T(8,128)(2,1)} %get-tuple-element.50.n_one_t, bf16[3,4,640,256]{3,2,1,0:T(8,128)(2,1)} %get-tuple-element.51.qkv, ...), custom_call_target="tpu_custom_call" | custom-call | tf_op jit(solution)/shard_map/pallas_call | solution.py:925
  329.6 1.4 copy-done.1
  331.0 1.0 copy-done.8
  332.0 0.9 copy-done.11
  332.9 0.8 copy-done.12
  333.8 32.6 %shard_map.320 = (f32[128,64]{1,0:T(8,128)S(1)}, f32[6,128,1024]{2,1,0:T(8,128)S(1)}, f32[256,128]{1,0:T(8,128)S(1)}, f32[8,128,128]{2,1,0:T(8,128)S(1)}, f32[64...) custom-call(f32[12,128,256]{2,1,0:T(8,128)S(1)} %copy-done.1, f32[1,1]{1,0:T(1,128)} %get-tuple-element.64.loss, ...), custom_call_target="tpu_custom_call" | custom-call | tf_op jit(solution)/shard_map/pallas_call | solution.py:1057
  366.4 1.7 copy-done.3
  368.0 0.7 copy-done.9
  368.7 0.5 fusion.91
  369.9 1.3 slice.184
  371.2 0.9 fusion.31
  372.3 0.3 fusion.33
  372.6 1.0 pad_maximum_fusion.4
  373.7 1.2 copy.163
  374.9 0.2 copy.184
  375.3 0.3 fusion.36
  375.6 1.0 pad_maximum_fusion.3
  376.7 2.5 copy.173
  379.2 2.7 bitcast_subtract_fusion.2
  381.9 2.0 copy.172
  383.9 2.6 bitcast_subtract_fusion.1
  386.6 1.6 copy.161
  388.2 2.0 fusion.75
  390.2 0.7 pad_maximum_fusion.10
  390.9 2.3 fusion.72
  393.2 0.9 pad_maximum_fusion.6
  394.2 6.2 %fusion.6 = (f32[1,128,6,1024]{3,1,2,0:T(8,128)S(1)}, f32[1,128,6,1024]{3,1,2,0:T(8,128)S(1)}, f32[128,6,1024]{2,0,1:T(8,128)}) fusion(f32[6,128,1024]{2,1,0:T(8,128)S(1)} %copy-done.4, f32[]{:T(128)S(6)} %min_shard_map.3, f32[3,128,6,1024]{3,1,2,0:T(8,128)} %param.25), kind=kLoop, calls=%fused_computation.33 | loop fusion | flops 13369344 | bytes 22020100 | tf_op jit(solution)/shard_map/stack | solution.py:1093
  400.3 3.3 pad_maximum_fusion
  403.6 1.0 fusion.73
  404.6 0.9 pad_maximum_fusion.7
  405.5 0.2 copy.158
  406.1 0.3 fusion.39
  406.5 1.3 copy.171
  407.9 0.4 bitcast_subtract_fusion.3
  408.3 1.0 copy.170
  409.3 0.7 pad_maximum_fusion.9
  410.5 0.6 pad_maximum_fusion.13
  411.1 0.7 copy.169
  412.2 0.6 pad_maximum_fusion.12
  412.9 0.7 copy.168
  (122 shorter events, 3.6 us)
Async XLA Ops:
  0.7 7.3 %copy-start.25 = (f32[3,128,1024]{2,1,0:T(8,128)S(1)}, f32[3,128,1024]{2,1,0:T(8,128)}, u32[]{:S(2)}) copy-start(f32[3,128,1024]{2,1,0:T(8,128)} %param.28) | copy-start | bytes 4718596
  2.2 1.4 copy-start.29
  3.8 3.1 copy-start.27
  7.1 2.2 copy-start.18
  9.3 6.9 %copy-start.20 = (f32[1,128,1024]{1,2,0:T(8,128)}, f32[1,128,1024]{1,2,0:T(8,128)S(1)}, u32[]{:S(2)}) copy-start(f32[1,128,1024]{1,2,0:T(8,128)S(1)} %copy.174) | copy-start | bytes 1572868
  10.8 6.6 %copy-start.41 = (s32[1,2,4]{2,1,0:T(2,128)S(1)}, s32[1,2,4]{2,1,0:T(2,128)}, u32[]{:S(2)}) copy-start(s32[1,2,4]{2,1,0:T(2,128)} %param.18) | copy-start | bytes 100
  10.8 6.9 %copy-start.42 = (s32[1,2,4]{2,1,0:T(2,128)S(1)}, s32[1,2,4]{2,1,0:T(2,128)}, u32[]{:S(2)}) copy-start(s32[1,2,4]{2,1,0:T(2,128)} %param.19) | copy-start | bytes 100
  10.8 7.2 %copy-start.40 = (s32[1,2,320]{2,1,0:T(2,128)S(1)}, s32[1,2,320]{2,1,0:T(2,128)}, u32[]{:S(2)}) copy-start(s32[1,2,320]{2,1,0:T(2,128)} %param.17) | copy-start | bytes 7684
  16.2 8.7 %copy-start.39 = (bf16[1,2,320,32]{2,3,1,0:T(8,128)(2,1)S(1)}, bf16[1,2,320,32]{2,3,1,0:T(8,128)(2,1)}, u32[]{:S(2)}) copy-start(bf16[1,2,320,32]{2,3,1,0:T(8,128)(2,1)} %param.15) | copy-start | bytes 122884
  23.2 149.4 %copy-start.35 = (f32[1,2,320,32]{2,3,1,0:T(8,128)S(1)}, f32[1,2,320,32]{2,3,1,0:T(8,128)}, u32[]{:S(2)}) copy-start(f32[1,2,320,32]{2,3,1,0:T(8,128)} %param.16) | copy-start | bytes 245764
  173.4 156.1 %copy-start = (bf16[6,128,1024]{2,1,0:T(8,128)(2,1)S(1)}, bf16[6,128,1024]{2,1,0:T(8,128)(2,1)}, u32[]{:S(2)}) copy-start(bf16[6,128,1024]{2,1,0:T(8,128)(2,1)} %fusion.5.adaptive) | copy-start | bytes 4718596
  173.4 156.1 %copy-start.5 = (bf16[128,8,128]{2,0,1:T(8,128)(2,1)S(1)}, bf16[128,8,128]{2,0,1:T(8,128)(2,1)}, u32[]{:S(2)}) copy-start(bf16[128,8,128]{2,0,1:T(8,128)(2,1)} %copy.146) | copy-start | bytes 786436
  173.4 156.1 %copy-start.6 = (bf16[640,128]{1,0:T(8,128)(2,1)S(1)}, bf16[640,128]{1,0:T(8,128)(2,1)}, u32[]{:S(2)}) copy-start(bf16[640,128]{1,0:T(8,128)(2,1)} %pad.4.classes) | copy-start | bytes 491524
  173.4 156.1 %copy-start.7 = (bf16[256,128]{1,0:T(8,128)(2,1)S(1)}, bf16[256,128]{1,0:T(8,128)(2,1)}, u32[]{:S(2)}) copy-start(bf16[256,128]{1,0:T(8,128)(2,1)} %bitcast_convert_fusion.3.time_in) | copy-start | bytes 196612
  173.4 156.1 %copy-start.13 = (f32[64,128]{1,0:T(8,128)S(1)}, f32[64,128]{1,0:T(8,128)}, u32[]{:S(2)}) copy-start(f32[64,128]{1,0:T(8,128)} %get-tuple-element.68.time_pre) | copy-start | bytes 98308
  173.5 156.1 %copy-start.14 = (f32[64,128]{1,0:T(8,128)S(1)}, f32[64,128]{1,0:T(8,128)}, u32[]{:S(2)}) copy-start(f32[64,128]{1,0:T(8,128)} %get-tuple-element.69.condition) | copy-start | bytes 98308
  329.6 1.4 copy-start.1
  331.0 1.0 copy-start.8
  332.0 0.9 copy-start.11
  332.9 0.8 copy-start.12
  366.3 1.7 copy-start.3
  368.0 0.7 copy-start.9
  368.7 3.7 copy-start.15
  372.6 2.3 copy-start.24
  372.6 2.5 copy-start.23
  375.1 1.5 copy-start.16
  375.3 1.3 copy-start.17
  379.2 7.4 %copy-start.2 = (f32[12,128,256]{2,1,0:T(8,128)S(1)}, f32[12,128,256]{2,1,0:T(8,128)}, u32[]{:S(2)}) copy-start(f32[12,128,256]{2,1,0:T(8,128)} %get-tuple-element.63.reduced) | copy-start | bytes 4718596
  383.9 4.3 %copy-start.10 = (f32[256,128]{1,0:T(8,128)S(1)}, f32[256,128]{1,0:T(8,128)}, u32[]{:S(2)}) copy-start(f32[256,128]{1,0:T(8,128)} %copy-done.9) | copy-start | bytes 393220
  383.9 4.3 %copy-start.31 = (f32[3,256,128]{2,1,0:T(8,128)S(1)}, f32[3,256,128]{2,1,0:T(8,128)}, u32[]{:S(2)}) copy-start(f32[3,256,128]{2,1,0:T(8,128)} %param.27) | copy-start | bytes 1179652
  386.6 1.6 copy-start.32
  388.2 6.0 %copy-start.4 = (f32[6,128,1024]{2,1,0:T(8,128)S(1)}, f32[6,128,1024]{2,1,0:T(8,128)}, u32[]{:S(2)}) copy-start(f32[6,128,1024]{2,1,0:T(8,128)} %copy-done.3) | copy-start | bytes 9437188
  400.3 3.3 copy-start.26
  403.6 2.1 copy-start.22
  403.6 2.3 copy-start.21
  406.1 1.7 copy-start.19
  406.5 2.8 copy-start.33
  406.5 2.8 copy-start.34
  406.5 3.7 copy-start.30
  407.8 2.2 copy-start.38
  407.8 2.3 copy-start.37
  407.8 4.0 copy-start.36
  407.8 4.2 %copy-start.28 = (f32[1,32,128]{1,2,0:T(8,128)S(1)}, f32[1,32,128]{1,2,0:T(8,128)}, u32[]{:S(2)}) copy-start(f32[1,32,128]{1,2,0:T(8,128)} %copy-done.27) | copy-start | bytes 49156
